TPU v7x, 32 devices: a whole 2x2x4 slice. The times are simulated.
32 devices in a mesh: layer: 4 (over y, core), row: 2 (over x), col: 4 (over z).
Axes of the slice: x: 2, y: 2, z: 4, core: 2. Of those that a mesh axis runs over, the one named last changes fastest.
Arguments:
- ancestor: float32 [6144, 6144], P('row', 'col'), may hold values from -6 to 6
- leaf_lower: bfloat16 [4, 8, 6144, 512], P('layer', 'col', 'row'), may hold values from -6 to 6
- leaf_upper: bfloat16 [4, 8, 512, 6144], P('layer', None, 'row', 'col'), may hold values from -6 to 6
- leaf_upper_inv: bfloat16 [4, 8, 512, 512], P('layer', 'col'), may hold values from -1 to 1, as said below
- leaf_lower_inv: bfloat16 [4, 8, 512, 512], P('layer'), may hold values from -1 to 2, as said below
- leaf_pivots: int32 [4, 8, 512], P('layer'), may hold values from 0 to 511, each once within a row
- leaf_tiles: int32 [4, 8, 24, 24], P('layer'), may hold values 0 or 1
- anc_upper_inv: bfloat16 [512, 512], replicated, may hold values from -1 to 1, as said below
- anc_lower_inv: bfloat16 [512, 512], replicated, may hold values from -1 to 2, as said below
- anc_pivots: int32 [512], replicated, may hold values from 0 to 511, each once
- anc_tiles: int32 [24, 24], replicated, may hold values 0 or 1
Outputs:
- anc_lower: bfloat16 [6144, 512], P('row')
- anc_upper: bfloat16 [512, 6144], P(None, 'col')
- schur: float32 [6144, 6144], P('row', 'col')
Inputs may be any that keep to these rules, and one draw needn't show every extreme that they name: leaf_upper_inv[l,k] is upper triangular with positive diagonal. leaf_lower_inv[l,k] is lower triangular with positive diagonal. `anc_upper_inv`: upper triangular with positive diagonal. `anc_lower_inv`: lower triangular with positive diagonal.
All inputs are finite; a program needn't handle non-finite values. No bound on the sum of `leaf_tiles` on one device may be relied on, other than what follows from the above.
Results may differ from a plain program's by a relative error of at most 0.0085.
Values may be sent and summed in bfloat16 or wider, within the bound.
No kernel may reach another device: no remote copies, remote signals or barrier semaphores. Data moves between devices by JAX's collectives and lax.ppermute only.
A program may use at most 320 MiB of HBM per device.

v0:
```python
import jax
import jax.numpy as jnp
from jax import lax
from jax.sharding import PartitionSpec as P

W = 512
TB = 256
NT = 24


def from_root(value, axis, source):
    kept = jnp.where(lax.axis_index(axis) == source, value, 0).astype(value.dtype)
    return lax.psum(kept, axis)


def onehot_tiles(first, count):
    positions = first + jnp.arange(count, dtype=jnp.int32)
    tile_index = positions // TB
    return (tile_index[:, None] == jnp.arange(NT, dtype=jnp.int32)[None, :]).astype(jnp.float32)


def shards(
    ancestor,
    leaf_lower,
    leaf_upper,
    leaf_upper_inv,
    leaf_lower_inv,
    leaf_pivots,
    leaf_tiles,
    anc_upper_inv,
    anc_lower_inv,
    anc_pivots,
    anc_tiles,
):
    row_count, col_count = ancestor.shape
    panel_rows = leaf_upper.shape[2]
    row_onehot = onehot_tiles(lax.axis_index("row") * row_count, row_count)
    col_onehot = onehot_tiles(lax.axis_index("col") * col_count, col_count)
    upper_local = leaf_upper[0]
    rows_all = lax.all_gather(upper_local, "row", axis=1, tiled=True)
    permuted = jnp.take_along_axis(rows_all, leaf_pivots[0][:, :, None], axis=1)
    upper_all = jnp.einsum(
        "kij,kjc->kic", leaf_lower_inv[0], permuted, preferred_element_type=jnp.float32
    ).astype(jnp.bfloat16)
    own_lower = jnp.einsum(
        "jrw,jwv->jrv", leaf_lower[0], leaf_upper_inv[0], preferred_element_type=jnp.float32
    ).astype(jnp.bfloat16)
    tiles_float = leaf_tiles[0].astype(jnp.float32)
    masks = jnp.einsum("rt,mts,cs->mrc", row_onehot, tiles_float, col_onehot)
    products = jnp.einsum(
        "mrw,mwc->mrc",
        lax.all_gather(own_lower, "col", axis=0, tiled=True),
        upper_all,
        preferred_element_type=jnp.float32,
    )
    contrib = jnp.sum(masks * products, axis=0)
    total = lax.psum(contrib, "layer")
    a_sum = ancestor + total
    local_pivot = a_sum[:panel_rows].astype(jnp.bfloat16)
    gathered = lax.all_gather(local_pivot, "row", axis=0, tiled=True)
    reordered = jnp.take(gathered, anc_pivots, axis=0)
    anc_upper = jnp.dot(anc_lower_inv, reordered, preferred_element_type=jnp.float32).astype(
        jnp.bfloat16
    )
    columns = a_sum[:, :W].astype(jnp.bfloat16)
    panel = jnp.dot(columns, anc_upper_inv, preferred_element_type=jnp.float32).astype(jnp.bfloat16)
    anc_lower = from_root(panel, "col", 0)
    anc_mask = jnp.einsum("rt,ts,cs->rc", row_onehot, anc_tiles.astype(jnp.float32), col_onehot)
    schur = a_sum - anc_mask * jnp.dot(anc_lower, anc_upper, preferred_element_type=jnp.float32)
    return (anc_lower, anc_upper, schur)


def solution(mesh):
    return jax.shard_map(
        shards,
        mesh=mesh,
        in_specs=(
            P("row", "col"),
            P("layer", "col", "row", None),
            P("layer", None, "row", "col"),
            P("layer", "col", None, None),
            P("layer", None, None, None),
            P("layer", None, None),
            P("layer", None, None, None),
            P(),
            P(),
            P(),
            P(),
        ),
        out_specs=(P("row", None), P(None, "col"), P("row", "col")),
        check_vma=False,
    )
```

profile of v0, /device:TPU:0, one launch (start us, length us, event | category | flops | bytes accessed | tf_op | source)
XLA Modules:
  0.0 1271.7 jit_solution(3268475370140669336)
XLA Ops:
  7.2 0.0 copy-start
  7.2 0.0 all-gather.9.cloned.1.call-start
  7.2 0.7 all-gather.9.cloned.1.call-update
  7.9 0.0 all-gather.5.cloned.1.call-start
  8.0 0.4 copy-done
  8.4 8.1 fusion.9
  16.5 0.0 copy-start.6
  16.5 0.0 all-gather.5.cloned.1.call-update
  16.5 0.0 all-reduce.3.cloned.1.call-start
  16.6 0.6 copy-done.6
  17.3 0.0 copy-start.4
  17.3 0.1 copy-done.3
  17.4 0.5 fusion.82
  17.9 146.6 %all-gather.9.cloned.1.call-done = bf16[1,8,512,1536]{3,2,1,0:T(8,128)(2,1)} async-done(((bf16[1,8,256,1536]{3,2,1,0:T(8,128)(2,1)}), bf16[1,8,512,1536]{3,2,1,0:T(8,128)(2,1)}) %all-gather.9.cloned.1.call-update) | async-done | bytes 12582928 | tf_op jit(solution)/shard_map/all_gather | solution.py:40
  164.5 92.7 %gather_fusion.1 = bf16[4096,1536]{1,0:T(8,128)(2,1)} fusion(bf16[8,512,1536]{2,1,0:T(8,128)(2,1)} %bitcast.64, s32[4096]{0:T(1024)S(1)} %bitcast.65), kind=kCustom, calls=%fused_computation.1 | custom fusion | bytes 25198592 | tf_op jit(solution)/shard_map/jit(take_along_axis)/gather | solution.py:41
  257.3 0.0 copy-done.4
  257.3 14.8 %convolution_convert_fusion.clone.4 = bf16[8,1536,512]{2,1,0:T(8,128)(2,1)} fusion(bf16[8,512,1536]{2,1,0:T(8,128)(2,1)} %bitcast.66, pred[8,512]{1,0:T(8,128)(4,1)S(1)} %compare_and_fusion, bf16[1,8,512,512]{3,2,1,0:T(8,128)(2,1)} %param.15), kind=kOutput, calls=%fused_computation.5.clone.clone.clone.1 | convolution fusion | flops 6455033856 | bytes 29364224 | tf_op jit(solution)/shard_map/kij,kjc->kic/dot_general | solution.py:42
  272.0 319.3 %all-gather.5.cloned.1.call-done = bf16[8,3072,512]{2,1,0:T(8,128)(2,1)} async-done(((bf16[2,3072,512]{2,1,0:T(8,128)(2,1)}), bf16[8,3072,512]{2,1,0:T(8,128)(2,1)}) %all-gather.5.cloned.1.call-update) | async-done | bytes 25165840 | tf_op jit(solution)/shard_map/all_gather | solution.py:52
  591.3 67.4 %fusion.7 = f32[8,3072,1536]{1,2,0:T(8,128)} fusion(bf16[8,3072,512]{2,1,0:T(8,128)(2,1)} %all-gather.5.cloned.1.call-done, bf16[8,1536,512]{2,1,0:T(8,128)(2,1)} %convolution_convert_fusion.clone.4), kind=kOutput, calls=%fused_computation.11 | convolution fusion | flops 38654705664 | bytes 188743680 | tf_op jit(solution)/shard_map/mrw,mwc->mrc/dot_general | solution.py:50
  658.7 55.3 %fusion = f32[3072,1536]{0,1:T(8,128)} fusion(f32[8,3072,1536]{1,2,0:T(8,128)} %fusion.7, s32[3072]{0:T(1024)S(1)} %add_select_fusion, f32[1536,8,24]{0,2,1:T(8,128)S(1)} %fusion.82), kind=kOutput, calls=%fused_computation.3 | convolution fusion | flops 1882791936 | bytes 171061248 | tf_op jit(solution)/shard_map/rt,mts,cs->mrc/dot_general | solution.py:49
  714.0 18.7 %copy.17 = f32[3072,1536]{1,0:T(8,128)} copy(f32[3072,1536]{0,1:T(8,128)} %fusion) | data formatting | bytes 37748736 | tf_op jit(solution)/shard_map/reduce_sum | solution.py:56
  732.8 0.0 all-reduce.3.cloned.1.call-update
  732.8 0.0 copy-start.9
  732.8 0.0 all-gather.7.cloned.1.call-start
  732.9 320.1 %all-reduce.3.cloned.1.call-done = f32[3072,1536]{1,0:T(8,128)} async-done(((f32[3072,1536]{1,0:T(8,128)}), f32[3072,1536]{1,0:T(8,128)}) %all-reduce.3.cloned.1.call-update) | async-done | bytes 18874384 | tf_op jit(solution)/shard_map/psum | solution.py:57
  1052.9 20.2 %fusion.56 = (bf16[3072,1536]{1,0:T(8,128)(2,1)S(1)}, f32[3072,1536]{1,0:T(8,128)}) fusion(f32[3072,1536]{1,0:T(8,128)} %param.11, f32[3072,1536]{1,0:T(8,128)} %all-reduce.3.cloned.1.call-done), kind=kLoop, calls=%fused_computation.66 | loop fusion | flops 9437184 | bytes 66060288 | tf_op jit(solution)/shard_map/convert.1
  1073.1 3.7 copy-done.2
  1076.8 0.9 slice.15
  1077.7 0.0 all-gather.7.cloned.1.call-update
  1077.7 0.0 all-reduce.5.cloned.1.call-start
  1077.8 0.0 copy-done.9
  1077.8 0.0 copy-start.8
  1077.8 5.4 fusion.14
  1083.2 0.0 all-reduce.5.cloned.1.call-update
  1083.2 0.0 copy-done.8
  1083.2 0.0 copy-start.10
  1083.3 22.1 %all-gather.7.cloned.1.call-done = bf16[512,1536]{1,0:T(8,128)(2,1)} async-done(((bf16[256,1536]{1,0:T(8,128)(2,1)}), bf16[512,1536]{1,0:T(8,128)(2,1)}) %all-gather.7.cloned.1.call-update) | async-done | bytes 1572880 | tf_op jit(solution)/shard_map/all_gather | solution.py:60
  1105.3 6.0 gather_fusion
  1111.3 0.0 copy-done.10
  1111.3 2.6 convolution_convert_fusion.2
  1113.9 1.6 copy.18
  1115.5 113.8 %all-reduce.5.cloned.1.call-done = bf16[3072,512]{1,0:T(8,128)(2,1)} async-done(((bf16[3072,512]{1,0:T(8,128)(2,1)}), bf16[3072,512]{1,0:T(8,128)(2,1)}) %all-reduce.5.cloned.1.call-update) | async-done | bytes 3145744 | tf_op jit(solution)/shard_map/psum | solution.py:13
  1229.3 11.3 fusion.57
  1240.6 0.0 copy-done.5
  1240.6 0.0 copy-done.7
  1240.6 20.8 %multiply_subtract_fusion = f32[3072,1536]{1,0:T(8,128)} fusion(f32[3072,1536]{1,0:T(8,128)} %get-tuple-element.10, f32[3072,1536]{1,0:T(8,128)} %fusion.57, s32[1536]{0:T(1024)S(1)} %copy-done.5, s32[3072]{0:T(1024)S(1)} %add_select_fusion, s32[24,24]{1,0:T(8,128)S(1)} %copy-done.7), kind=kOutput, calls=%fused_computation.4 | convolution fusion | flops 237883968 | bytes 56643840 | tf_op jit(solution)/shard_map/rt,ts,cs->rc/dot_general | solution.py:68
  1261.4 3.8 copy.23
  1265.1 0.0 copy-done.1
  (13 shorter events, 0.1 us)
Async XLA Ops:
  7.2 1.2 copy-start
  7.2 157.3 %all-gather.9.cloned.1.call-start = ((), (), s32[]{:S(2)}) async-start(), calls=%async_computation.4 | async-start | bytes 18874368 | tf_op jit(solution)/shard_map/all_gather | solution.py:40
  7.9 583.4 %all-gather.5.cloned.1.call-start = ((), (), s32[]{:S(2)}) async-start(), calls=%async_computation | async-start | bytes 31457280 | tf_op jit(solution)/shard_map/all_gather | solution.py:52
  16.5 0.7 copy-start.6
  16.5 0.9 copy-start.3
  16.5 1036.4 %all-reduce.3.cloned.1.call-start = ((), (), s32[]{:S(2)}) async-start(), calls=%async_computation.1 | async-start | bytes 37748736 | tf_op jit(solution)/shard_map/psum | solution.py:57
  17.3 240.0 %copy-start.4 = (s32[1536]{0:T(1024)}, s32[1536]{0:T(1024)S(1)}, u32[]{:S(2)}) copy-start(s32[1536]{0:T(1024)S(1)} %add_select_fusion.1) | copy-start | bytes 18436
  732.8 345.0 %copy-start.9 = (bf16[512,512]{1,0:T(8,128)(2,1)S(1)}, bf16[512,512]{1,0:T(8,128)(2,1)}, u32[]{:S(2)}) copy-start(bf16[512,512]{1,0:T(8,128)(2,1)} %param.18) | copy-start | bytes 1572868
  732.8 372.5 %all-gather.7.cloned.1.call-start = ((), (), s32[]{:S(2)}) async-start(), calls=%async_computation.3 | async-start | bytes 2359296 | tf_op jit(solution)/shard_map/all_gather | solution.py:60
  1073.1 3.7 copy-start.2
  1077.7 151.6 %all-reduce.5.cloned.1.call-start = ((), (), s32[]{:S(2)}) async-start(), calls=%async_computation.2 | async-start | bytes 6291456 | tf_op jit(solution)/shard_map/psum | solution.py:13
  1077.8 5.4 copy-start.8
  1083.2 28.1 %copy-start.10 = (bf16[512,512]{1,0:T(8,128)(2,1)S(1)}, bf16[512,512]{1,0:T(8,128)(2,1)}, u32[]{:S(2)}) copy-start(bf16[512,512]{1,0:T(8,128)(2,1)} %param.19) | copy-start | bytes 1572868
  1115.5 125.1 %copy-start.5 = (s32[1536]{0:T(1024)S(1)}, s32[1536]{0:T(1024)}, u32[]{:S(2)}) copy-start(s32[1536]{0:T(1024)} %copy-done.4) | copy-start | bytes 18436
  1115.5 125.1 %copy-start.7 = (s32[24,24]{1,0:T(8,128)S(1)}, s32[24,24]{1,0:T(8,128)}, u32[]{:S(2)}) copy-start(s32[24,24]{1,0:T(8,128)} %param.21) | copy-start | bytes 6916
  1240.6 24.5 %copy-start.1 = (bf16[1,2,512,512]{3,2,1,0:T(8,128)(2,1)S(1)}, bf16[1,2,512,512]{3,2,1,0:T(8,128)(2,1)}, u32[]{:S(2)}) copy-start(bf16[1,2,512,512]{3,2,1,0:T(8,128)(2,1)} %param.14) | copy-start | bytes 3145732
Sparse Core Ops, SparseCore 0:
  9.6 154.8 all-gather.8
  166.1 425.1 all-gather.4
  732.9 319.9 all-reduce.2
  1077.9 27.4 all-gather.6
  1108.2 121.0 all-reduce.4
where the time goes:
time: 1270 us
  waiting for transfers between devices  923 us (73%)
  matrix products  186 us (15%)
  local copies, waits for them, and re-layouts  129 us (10%)
  other arithmetic  20.3 us (2%)
  between operations  13.9 us (1%)
    psum x1, waiting for transfers between devices, shards(): total = lax.psum(contrib, 'layer')  320 us
    all_gather x1, waiting for transfers between devices, shards(): lax.all_gather(own_lower, 'col', axis=0, tiled=True)  319 us
    all_gather x1, waiting for transfers between devices, shards(): rows_all = lax.all_gather(upper_local, 'row', axis=1, tiled=True)  147 us
    psum x1, waiting for transfers between devices, from_root(): return lax.psum(kept, axis)  114 us
    gather x1, local copies, waits for them, and re-layouts, shards(): permuted = jnp.take_along_axis(rows_all, leaf_pivots[0][:, :, None], axis=1)  92.7 us
    dot_general x1, matrix products, shards(): jnp.einsum('mrw,mwc->mrc', lax.all_gather(own_lower, 'col', axis=0, tiled...  67.4 us
    dot_general x2, matrix products, shards(): masks = jnp.einsum('rt,mts,cs->mrc', row_onehot, tiles_float, col_onehot)  55.8 us
  transfers between devices with their start and end apart: 5, of which 5 were waited for; matrix products, arithmetic and copies ran while one was open for 10% of the time, Pallas kernels for 0%

commit v1 on v0

v1 whole, which is shorter than its diff:
```python
import functools

import jax
import jax.numpy as jnp
from jax import lax
from jax.experimental import pallas as pl
from jax.experimental.pallas import tpu as pltpu
from jax.sharding import PartitionSpec as P

BF = jnp.bfloat16
F32 = jnp.float32
MIB = 1024 * 1024
SWAP = [(0, 1), (1, 0)]
CORE = [(0, 1), (1, 0), (2, 3), (3, 2)]
YPAIR = [(0, 2), (2, 0), (1, 3), (3, 1)]
BUDDY = [(0, 1), (1, 0), (2, 3), (3, 2)]
PIECE = (0, 2, 1, 3)


def dot(a, b):
    return jnp.dot(a, b, preferred_element_type=F32)


def plain(
    ancestor, leaf_lower, leaf_upper, leaf_upper_inv, leaf_lower_inv, leaf_pivots, leaf_tiles,
    anc_upper_inv, anc_lower_inv, anc_pivots, anc_tiles, *, order,
):
    row_count, col_count = ancestor.shape
    panel_rows = leaf_upper.shape[2]
    width = leaf_lower.shape[-1]
    nt = leaf_tiles.shape[-1]
    tb = order // nt

    def onehot_tiles(first, count):
        tile = (first + jnp.arange(count, dtype=jnp.int32)) // tb
        return (tile[:, None] == jnp.arange(nt, dtype=jnp.int32)[None, :]).astype(F32)

    row_onehot = onehot_tiles(lax.axis_index("row") * row_count, row_count)
    col_onehot = onehot_tiles(lax.axis_index("col") * col_count, col_count)
    rows_all = lax.all_gather(leaf_upper[0], "row", axis=1, tiled=True)
    permuted = jnp.take_along_axis(rows_all, leaf_pivots[0][:, :, None], axis=1)
    upper_all = jnp.einsum("kij,kjc->kic", leaf_lower_inv[0], permuted, preferred_element_type=F32).astype(BF)
    own_lower = jnp.einsum("jrw,jwv->jrv", leaf_lower[0], leaf_upper_inv[0], preferred_element_type=F32).astype(BF)
    masks = jnp.einsum("rt,mts,cs->mrc", row_onehot, leaf_tiles[0].astype(F32), col_onehot)
    products = jnp.einsum(
        "mrw,mwc->mrc", lax.all_gather(own_lower, "col", axis=0, tiled=True), upper_all, preferred_element_type=F32
    )
    a_sum = ancestor + lax.psum(jnp.sum(masks * products, axis=0), "layer")
    gathered = lax.all_gather(a_sum[:panel_rows].astype(BF), "row", axis=0, tiled=True)
    anc_upper = dot(anc_lower_inv, jnp.take(gathered, anc_pivots, axis=0)).astype(BF)
    panel = dot(a_sum[:, :width].astype(BF), anc_upper_inv).astype(BF)
    kept = jnp.where(lax.axis_index("col") == 0, panel, 0).astype(BF)
    anc_lower = lax.psum(kept, "col")
    anc_mask = jnp.einsum("rt,ts,cs->rc", row_onehot, anc_tiles.astype(F32), col_onehot)
    return anc_lower, anc_upper, a_sum - anc_mask * dot(anc_lower, anc_upper)


def upper_kernel(mo_ref, mt_ref, so_ref, st_ref, out_ref):
    total = dot(mo_ref[0], so_ref[0, 0]) + dot(mt_ref[0], st_ref[0, 0])
    out_ref[0, 0] = total.astype(BF)


def make_upper(m_own, m_other, s_own, s_other):
    blocks, pair, half, cw = s_own.shape
    w = m_own.shape[1]
    m_spec = pl.BlockSpec((1, w, half), lambda k, b: (k, 0, 0))
    s_spec = pl.BlockSpec((1, 1, half, cw), lambda k, b: (b, k, 0, 0))
    return pl.pallas_call(
        upper_kernel,
        grid=(pair, blocks),
        in_specs=[m_spec, m_spec, s_spec, s_spec],
        out_specs=pl.BlockSpec((1, 1, w, cw), lambda k, b: (b, k, 0, 0)),
        out_shape=jax.ShapeDtypeStruct((blocks, pair, w, cw), BF),
        cost_estimate=pl.CostEstimate(
            flops=4 * blocks * pair * w * half * cw, transcendentals=0,
            bytes_accessed=2 * (2 * s_own.size + blocks * pair * w * cw),
        ),
        compiler_params=pltpu.CompilerParams(vmem_limit_bytes=16 * MIB),
        name="upper",
    )(m_own, m_other, s_own, s_other)


def product_kernel(place, tiles, low0, low1, up0, up1, keep, send, acc, *, g, c, nt, rt, ct, tb, pair, tj):
    b, j = pl.program_id(0), pl.program_id(1)
    x, z, l = place[0], place[1], place[2]
    odd = lax.rem(z, 2)
    column = jnp.where(b == 0, 3 * odd, 1 + odd) * ct + c * tj + j
    for p, flip in enumerate(PIECE):
        i = jnp.bitwise_xor(l, flip)
        rows = pl.ds(pl.multiple_of(i * tb, tb), tb)
        acc[...] = jnp.zeros_like(acc)
        for low, up, owner in ((low0, up0, z), (low1, up1, jnp.bitwise_xor(z, 1))):
            for k in range(pair):
                leaf = owner * pair + k
                flag = tiles[(leaf * nt + x * rt + g * 4 + i) * nt + column]

                @pl.when(flag != 0)
                def _():
                    acc[...] += dot(low[k, rows, :], up[0, k])

        if p < 2:
            keep[p, 0] = acc[...]
        else:
            send[p - 2, 0] = acc[...].astype(BF)


def products(place, tiles, low0, low1, up0, up1, *, g, c, nt, rt, ct, tb):
    blocks, pair, w, cw = up0.shape
    tj = cw // tb
    rows = 4 * tb
    up_spec = pl.BlockSpec((1, pair, w, tb), lambda b, j, *_: (b, 0, 0, j))
    out_spec = pl.BlockSpec((2, 1, tb, tb), lambda b, j, *_: (0, b, 0, j))
    return pl.pallas_call(
        functools.partial(product_kernel, g=g, c=c, nt=nt, rt=rt, ct=ct, tb=tb, pair=pair, tj=tj),
        grid_spec=pltpu.PrefetchScalarGridSpec(
            num_scalar_prefetch=2,
            grid=(blocks, tj),
            in_specs=[
                pl.BlockSpec((pair, rows, w), lambda b, j, *_: (0, g, 0)),
                pl.BlockSpec((pair, rows, w), lambda b, j, *_: (0, 0, 0)),
                up_spec,
                up_spec,
            ],
            out_specs=[out_spec, out_spec],
            scratch_shapes=[pltpu.VMEM((tb, tb), F32)],
        ),
        out_shape=[
            jax.ShapeDtypeStruct((2, blocks, tb, cw), F32),
            jax.ShapeDtypeStruct((2, blocks, tb, cw), BF),
        ],
        cost_estimate=pl.CostEstimate(
            flops=4 * blocks * pair * rows * w * cw, transcendentals=0, bytes_accessed=24 * MIB,
        ),
        compiler_params=pltpu.CompilerParams(vmem_limit_bytes=24 * MIB),
        name="products",
    )(place, tiles, low0, low1, up0, up1)


def final_kernel(place, tiles, *refs, g, c, nt, rt, ct, tb, tj, first, with_lower):
    anc, tq, ty, tc, au, pq, py, pc = refs[:8]
    outs = refs[8:] if first else refs[8 + (2 if with_lower else 1):]
    p = pl.program_id(0)
    x, z, l = place[0], place[1], place[2]
    flip = jnp.where(p == 0, 0, jnp.where(p == 1, 2, jnp.where(p == 2, 1, 3)))
    i = x * rt + g * 4 + jnp.bitwise_xor(l, flip)

    def work(total, panel):
        if with_lower:
            outs[1][...] = panel
        for j in range(tj):
            cols = slice(j * tb, (j + 1) * tb)
            base = anc[:, cols] + total[:, cols].astype(F32)
            flag = tiles[i * nt + z * ct + c * tj + j] != 0

            @pl.when(flag)
            def _():
                outs[0][:, cols] = base - dot(panel, au[:, cols])

            @pl.when(jnp.logical_not(flag))
            def _():
                outs[0][:, cols] = base

    for q, (t, v) in enumerate(((tq, pq), (ty, py), (tc.at[0], pc.at[0]), (tc.at[1], pc.at[1]))):

        @pl.when(p == q)
        def _():
            work(t[...], v[...])


def final(place, tiles, ancestor, total, au, panel, kept, *, g, c, nt, rt, ct, tb, with_lower):
    rows, cols = ancestor.shape
    tq, ty, tc = total
    pq, py, pc = panel
    cw, w = tq.shape[1], pq.shape[1]
    tj = cw // tb
    first = kept is None

    def whole(shape):
        return pl.BlockSpec(shape, lambda p, *_: (0,) * len(shape))

    def tile_row(p, place):
        flip = jnp.where(p == 0, 0, jnp.where(p == 1, 2, jnp.where(p == 2, 1, 3)))
        return g * 4 + jnp.bitwise_xor(place[2], flip)

    out_specs = [pl.BlockSpec((tb, cw), lambda p, place, *_: (tile_row(p, place), c))]
    out_shape = [jax.ShapeDtypeStruct((rows, cols), F32)]
    if with_lower:
        out_specs.append(pl.BlockSpec((tb, w), lambda p, place, *_: (tile_row(p, place), 0)))
        out_shape.append(jax.ShapeDtypeStruct((rows, w), BF))
    in_specs = [
        pl.BlockSpec((tb, cw), lambda p, place, *_: (tile_row(p, place), c)),
        whole(tq.shape), whole(ty.shape), whole(tc.shape), whole(au.shape),
        whole(pq.shape), whole(py.shape), whole(pc.shape),
    ]
    operands = [ancestor, tq, ty, tc, au, pq, py, pc]
    aliases = {}
    if not first:
        for n in range(len(out_shape)):
            aliases[2 + len(operands)] = n
            operands.append(kept[n])
            in_specs.append(pl.BlockSpec(memory_space=pl.ANY))
    return pl.pallas_call(
        functools.partial(
            final_kernel, g=g, c=c, nt=nt, rt=rt, ct=ct, tb=tb, tj=tj, first=first, with_lower=with_lower
        ),
        grid_spec=pltpu.PrefetchScalarGridSpec(
            num_scalar_prefetch=2, grid=(4,), in_specs=in_specs, out_specs=out_specs
        ),
        out_shape=out_shape,
        input_output_aliases=aliases,
        cost_estimate=pl.CostEstimate(flops=8 * tb * w * cw, transcendentals=0, bytes_accessed=40 * tb * cw),
        compiler_params=pltpu.CompilerParams(vmem_limit_bytes=24 * MIB),
        name="final",
    )(place, tiles, *operands)


def onehot_cols(inverse, pivots, first, count):
    wanted = (first + jnp.arange(count, dtype=jnp.int32))
    picks = (pivots[..., :, None] == wanted).astype(BF)
    return jnp.einsum("...it,...tj->...ij", inverse, picks, preferred_element_type=F32).astype(BF)


def paired(
    ancestor, leaf_lower, leaf_upper, leaf_upper_inv, leaf_lower_inv, leaf_pivots, leaf_tiles,
    anc_upper_inv, anc_lower_inv, anc_pivots, anc_tiles, *, order, split,
):
    rows, cols = ancestor.shape
    pair, w = leaf_lower.shape[1], leaf_lower.shape[-1]
    half = leaf_upper.shape[2]
    nt = leaf_tiles.shape[-1]
    tb = order // nt
    rt, ct = rows // tb, cols // tb
    groups, cw = rows // (4 * tb), cols // split
    x, z, l = lax.axis_index("row"), lax.axis_index("col"), lax.axis_index("layer")
    odd = lax.rem(z, 2)
    is_end = (z == 0) | (z == 3)
    near, far = (z // 2) * 2 * pair, (1 - z // 2) * 2 * pair
    place = jnp.stack([x, z, l]).astype(jnp.int32)
    tiles = leaf_tiles.reshape(-1)
    top_tiles = anc_tiles.reshape(-1)
    shape = dict(nt=nt, rt=rt, ct=ct, tb=tb)

    u = leaf_upper[0]
    ups = {}
    for c in range(split):
        for t in range(2):
            same, other = (odd ^ t) * pair, ((1 - odd) ^ t) * pair

            def part(first):
                return lax.dynamic_slice(u, (first, 0, c * cw), (pair, half, cw))

            p1 = lax.ppermute(part(near + other), "col", [(1, 0), (2, 3)])
            p2 = lax.ppermute(part(far + same), "col", [(0, 2), (3, 1)])
            p3 = lax.ppermute(part(far + other), "col", [(1, 2), (2, 1)])
            own = jnp.stack([jnp.where(is_end, part(near + same), p2), jnp.where(is_end, p1, p3)])
            ups[c, t] = (own, lax.ppermute(own, "row", SWAP))

    lower = jnp.einsum("krw,kwv->krv", leaf_lower[0], leaf_upper_inv[0], preferred_element_type=F32).astype(BF)
    buddy = [lax.ppermute(lower[:, g * 4 * tb:(g + 1) * 4 * tb], "col", BUDDY) for g in range(groups)]

    uppers = {}
    mats = []
    for t in range(2):
        first = near + (odd ^ t) * pair
        inverse = lax.dynamic_slice_in_dim(leaf_lower_inv[0], first, pair, 0)
        pivots = lax.dynamic_slice_in_dim(leaf_pivots[0], first, pair, 0)
        mats.append((onehot_cols(inverse, pivots, x * half, half), onehot_cols(inverse, pivots, (1 - x) * half, half)))
    a_own = onehot_cols(anc_lower_inv, anc_pivots, x * half, half)
    a_other = onehot_cols(anc_lower_inv, anc_pivots, (1 - x) * half, half)
    for (c, t), (own, other) in ups.items():
        uppers[c, t] = make_upper(*mats[t], own, other)

    panels, anc_uppers = {}, {}
    schur, anc_lower = None, None
    for c in range(split):
        for g in range(groups):
            keep, send = products(place, tiles, lower, buddy[g], uppers[c, 0], uppers[c, 1], g=g, c=c, **shape)
            recv = lax.ppermute(send, "layer", CORE)
            crossing = (keep[1] + recv[1].astype(F32)).astype(BF)
            arrived = lax.ppermute(crossing, "layer", YPAIR)
            mine = (keep[0] + recv[0].astype(F32) + arrived.astype(F32)).astype(BF)
            outer, inner = mine[0], mine[1]
            q1 = lax.ppermute(inner, "col", [(0, 1), (3, 2)])
            q2 = lax.ppermute(outer, "col", [(1, 3), (2, 0)])
            q3 = lax.ppermute(inner, "col", [(1, 2), (2, 1)])
            stay = jnp.where(is_end, outer.astype(F32) + q2.astype(F32), q1.astype(F32) + q3.astype(F32))
            tq = stay.astype(BF)
            ty = lax.ppermute(tq, "layer", YPAIR)
            tc = lax.ppermute(jnp.stack([tq, ty]), "layer", CORE)
            if c == 0:
                base = lax.dynamic_slice(ancestor, ((g * 4 + l) * tb, 0), (tb, w))
                pq = dot((base + tq[:, :w].astype(F32)).astype(BF), anc_upper_inv).astype(BF)
                sent = [lax.ppermute(pq, "col", [(0, n)]) for n in (1, 2, 3)]
                pq = jnp.where(z == 0, pq, sent[0] + sent[1] + sent[2])
                py = lax.ppermute(pq, "layer", YPAIR)
                panels[g] = (pq, py, lax.ppermute(jnp.stack([pq, py]), "layer", CORE))
            if g == 0:
                top = jnp.where(l == 0, tq, jnp.where(l == 2, ty, jnp.where(l == 1, tc[0], tc[1])))
                pivot = (ancestor[:tb, c * cw:(c + 1) * cw] + top.astype(F32)).astype(BF)
                swapped = lax.ppermute(pivot, "row", SWAP)
                anc_uppers[c] = (dot(a_own, pivot) + dot(a_other, swapped)).astype(BF)
            kept = None if schur is None else ((schur, anc_lower) if c == 0 else (schur,))
            out = final(
                place, top_tiles, ancestor, (tq, ty, tc), anc_uppers[c], panels[g], kept,
                g=g, c=c, with_lower=c == 0, **shape,
            )
            schur = out[0]
            if c == 0:
                anc_lower = out[1]
    anc_upper = jnp.concatenate([anc_uppers[c] for c in range(split)], axis=1)
    return anc_lower, anc_upper, schur


def solution(mesh):
    sizes = mesh.shape

    def shards(*args):
        ancestor, leaf_lower, leaf_upper, leaf_tiles = args[0], args[1], args[2], args[6]
        rows, cols = ancestor.shape
        order = rows * sizes["row"]
        nt = leaf_tiles.shape[-1]
        tb = order // nt
        w, half = leaf_lower.shape[-1], leaf_upper.shape[2]
        fits = (
            (sizes["layer"], sizes["row"], sizes["col"]) == (4, 2, 4)
            and leaf_lower.shape[0] == 1 and leaf_upper.shape[1] == 4 * leaf_lower.shape[1]
            and order % nt == 0 and rows % (4 * tb) == 0 and cols % (2 * tb) == 0
            and half == tb and tb % 128 == 0 and w <= cols // 2
        )
        if fits:
            return paired(*args, order=order, split=2)
        return plain(*args, order=order)

    return jax.shard_map(
        shards,
        mesh=mesh,
        in_specs=(
            P("row", "col"), P("layer", "col", "row", None), P("layer", None, "row", "col"),
            P("layer", "col", None, None), P("layer", None, None, None), P("layer", None, None),
            P("layer", None, None, None), P(), P(), P(), P(),
        ),
        out_specs=(P("row", None), P(None, "col"), P("row", "col")),
        check_vma=False,
    )
```

time: 1270 us -> 695 us (0.55)
  waiting for transfers between devices: 923 us -> 308 us
  matrix products: 186 us -> 19.8 us
  starting transfers between devices: 0.2 us -> 155 us
  Pallas kernels: 0 us -> 135 us
  local copies, waits for them, and re-layouts: 129 us -> 30.8 us
  other arithmetic: 20.3 us -> 37 us
    all_gather x3 -> x0, waiting for transfers between devices: 488 us -> none  [the longest x1 319 us: shards(): lax.all_gather(own_lower, 'col', axis=0, tiled=True)]
    psum x2 -> x0, waiting for transfers between devices: 434 us -> none  [the longest x1 320 us: shards(): total = lax.psum(contrib, 'layer')]
    ppermute x0 -> x78, waiting for transfers between devices: none -> 308 us  [the longest x6 79.1 us: paired(): arrived = lax.ppermute(crossing, 'layer', YPAIR)]
    dot_general x9 -> x14, matrix products: 186 us -> 19.8 us  [the longest x6 10.8 us: onehot_cols(): jnp.einsum('...it,...tj->...ij', inverse, picks, preferred_element_type=F32)]
    ppermute x0 -> x78, starting transfers between devices: none -> 155 us  [the longest x3 31.6 us: paired(): lax.ppermute(lower[:, g * 4 * tb:(g + 1) * 4 * tb], 'col', BUDDY)]
    pallas_call x0 -> x16, Pallas kernels: none -> 135 us  [the longest x6 90.8 us: products(): pl.pallas_call(functools.partial(product_kernel, g=g, c=c, nt=nt, rt=rt,...]
    gather x2 -> x0, local copies, waits for them, and re-layouts: 98.7 us -> none  [the longest x1 92.7 us: shards(): permuted = jnp.take_along_axis(rows_all, leaf_pivots[0][:, :, None], axis=1)]
    convert_element_type x0 -> x19, other arithmetic: none -> 19.4 us  [the longest x6 9.16 us: paired(): crossing = (keep[1] + recv[1].astype(F32)).astype(BF)]
  transfers between devices with their start and end apart: 5 -> 78, of which waited for: 5 -> 32; matrix products, arithmetic and copies ran while one was open for 10% -> 9% of each run, Pallas kernels for 0% -> 19%
where the time goes in v1:
time: 695 us; the launch traced here: 688 us
  waiting for transfers between devices  308 us (44%)
  starting transfers between devices  155 us (22%)
  Pallas kernels  135 us (19%)
  other arithmetic  37 us (5%)
  local copies, waits for them, and re-layouts  30.8 us (4%)
  matrix products  19.8 us (3%)
    pallas_call x6, Pallas kernels, products(): pl.pallas_call(functools.partial(product_kernel, g=g, c=c, nt=nt, rt=rt,...  90.8 us
    ppermute x6, waiting for transfers between devices, paired(): arrived = lax.ppermute(crossing, 'layer', YPAIR)  79.1 us
    ppermute x4, waiting for transfers between devices, paired(): p1 = lax.ppermute(part(near + other), 'col', [(1, 0), (2, 3)])  69.4 us
    ppermute x6, waiting for transfers between devices, paired(): q2 = lax.ppermute(outer, 'col', [(1, 3), (2, 0)])  34.7 us
    ppermute x3, starting transfers between devices, paired(): lax.ppermute(lower[:, g * 4 * tb:(g + 1) * 4 * tb], 'col', BUDDY)  31.6 us
    ppermute x4, waiting for transfers between devices, paired(): p2 = lax.ppermute(part(far + same), 'col', [(0, 2), (3, 1)])  31.3 us
    ppermute x9, starting transfers between devices, paired(): sent = [lax.ppermute(pq, 'col', [(0, n)]) for n in (1, 2, 3)]  29.3 us
    ppermute x6, starting transfers between devices, paired(): q1 = lax.ppermute(inner, 'col', [(0, 1), (3, 2)])  29.2 us
  transfers between devices with their start and end apart: 78, of which 32 were waited for; matrix products, arithmetic and copies ran while one was open for 9% of the time, Pallas kernels for 19%

profile of v1, /device:TPU:0, one launch (start us, length us, event | category | flops | bytes accessed | tf_op | source)
XLA Modules:
  0.0 688.0 jit_solution(4990116207422585840)
XLA Ops:
  0.7 7.5 %dynamic-slice_bitcast_fusion.2 = (bf16[2,256,768]{2,1,0:T(8,128)(2,1)}, bf16[2,256,768]{2,1,0:T(8,128)(2,1)}, bf16[2,256,768]{2,1,0:T(8,128)(2,1)}, bf16[2,256,...) fusion(bf16[1,8,256,1536]{3,2,1,0:T(8,128)(2,1)} %param.13, ...), kind=kLoop, calls=%fused_computation.77 | loop fusion | bytes 18874392 | tf_op jit(solution)/shard_map/dynamic_slice | solution.py:250
  8.2 6.8 collective-permute-start.52
  22.4 5.4 fusion.2.low0
  32.4 6.2 collective-permute-start.1
  40.5 5.9 fusion.64
  54.9 11.1 %collective-permute-done.5 = bf16[2,256,768]{2,1,0:T(8,128)(2,1)} collective-permute-done((bf16[2,256,768]{2,1,0:T(8,128)(2,1)S(1)}, bf16[2,256,768]{2,1,0:T(8,128)(2,1)}, u32[]{:S(2)}, u32[]{:S(2)}) %collective-permute-start.5) | collective-permute-done | bytes 786464 | tf_op jit(solution)/shard_map/ppermute | solution.py:253
  67.3 14.4 %collective-permute-done.1 = bf16[2,256,768]{2,1,0:T(8,128)(2,1)} collective-permute-done((bf16[2,256,768]{2,1,0:T(8,128)(2,1)S(1)}, bf16[2,256,768]{2,1,0:T(8,128)(2,1)}, u32[]{:S(2)}, u32[]{:S(2)}) %collective-permute-start.1) | collective-permute-done | bytes 786464 | tf_op jit(solution)/shard_map/ppermute | solution.py:253
  89.3 29.5 %collective-permute-start.30 = (bf16[2,1024,512]{2,1,0:T(8,128)(2,1)}, bf16[2,1024,512]{2,1,0:T(8,128)(2,1)}, u32[]{:S(2)}, u32[]{:S(2)}) collective-permute-start(bf16[2,1024,512]{2,1,0:T(8,128)(2,1)} %get-tuple-element.57), channel_id=1, source_target_pairs={{0,1},{1,0},{2,3},{3,2},{4,5},{5,4},{6,7},{7,6},{8,9},{9,8},{10,11... | collective-permute-start | bytes 6291464 | tf_op jit(solution)/shard_map/ppermute | solution.py:259
  127.2 10.7 %collective-permute-done.2 = bf16[2,256,768]{2,1,0:T(8,128)(2,1)} collective-permute-done((bf16[2,256,768]{2,1,0:T(8,128)(2,1)}, bf16[2,256,768]{2,1,0:T(8,128)(2,1)}, u32[]{:S(2)}, u32[]{:S(2)}) %collective-permute-start.2) | collective-permute-done | bytes 786464 | tf_op jit(solution)/shard_map/ppermute | solution.py:252
  142.5 56.4 %collective-permute-done.6 = bf16[2,256,768]{2,1,0:T(8,128)(2,1)S(1)} collective-permute-done((bf16[2,256,768]{2,1,0:T(8,128)(2,1)}, bf16[2,256,768]{2,1,0:T(8,128)(2,1)S(1)}, u32[]{:S(2)}, u32[]{:S(2)}) %collective-permute-start.6) | collective-permute-done | bytes 786464 | tf_op jit(solution)/shard_map/ppermute | solution.py:252
  212.3 4.1 upper.6.up0
  216.4 15.0 %products.11 = (f32[2,2,256,768]{3,2,1,0:T(8,128)S(1)}, bf16[2,2,256,768]{3,2,1,0:T(8,128)(2,1)S(1)}) custom-call(s32[3]{0:T(128)S(1)} %pad_add_fusion.place, s32[4608]{0:T(1024)S(1)} %reshape.88.tiles, bf16[2,3072,512]{2,1,0:T(8,128)(2,1)S(1)} %bitcast.209, bf16[2,1024,512]{2,1,0:T(8,128)(2,1)} %collective-permute-done.30.low1, ...), custom_call_target="tpu_custom_call" | custom-call | flops 6442450944 | bytes 25165824 | tf_op jit(solution)/shard_map/products/pallas_call | solution.py:113
  234.2 4.1 upper.4.up0
  240.6 4.1 upper.5.up1
  244.7 14.1 %products.8 = (f32[2,2,256,768]{3,2,1,0:T(8,128)S(1)}, bf16[2,2,256,768]{3,2,1,0:T(8,128)(2,1)S(1)}) custom-call(s32[3]{0:T(128)S(1)} %pad_add_fusion.place, s32[4608]{0:T(1024)S(1)} %reshape.88.tiles, bf16[2,3072,512]{2,1,0:T(8,128)(2,1)S(1)} %bitcast.209, bf16[2,1024,512]{2,1,0:T(8,128)(2,1)} %collective-permute-done.30.low1, ...), custom_call_target="tpu_custom_call" | custom-call | flops 6442450944 | bytes 25165824 | tf_op jit(solution)/shard_map/products/pallas_call | solution.py:113
  260.5 17.4 %products.10 = (f32[2,2,256,768]{3,2,1,0:T(8,128)S(1)}, bf16[2,2,256,768]{3,2,1,0:T(8,128)(2,1)}) custom-call(s32[3]{0:T(128)S(1)} %pad_add_fusion.place, s32[4608]{0:T(1024)S(1)} %reshape.88.tiles, bf16[2,3072,512]{2,1,0:T(8,128)(2,1)S(1)} %bitcast.209, bf16[2,1024,512]{2,1,0:T(8,128)(2,1)} %collective-permute-done.low1, ...), custom_call_target="tpu_custom_call" | custom-call | flops 6442450944 | bytes 25165824 | tf_op jit(solution)/shard_map/products/pallas_call | solution.py:113
  279.7 15.8 %collective-permute-done.16.low1 = bf16[2,1024,512]{2,1,0:T(8,128)(2,1)S(1)} collective-permute-done((bf16[2,1024,512]{2,1,0:T(8,128)(2,1)}, bf16[2,1024,512]{2,1,0:T(8,128)(2,1)S(1)}, u32[]{:S(2)}, u32[]{:S(2)}) %collective-permute-start.16) | collective-permute-done | bytes 2097184 | tf_op jit(solution)/shard_map/ppermute | solution.py:259
  295.5 15.8 %products.9 = (f32[2,2,256,768]{3,2,1,0:T(8,128)S(1)}, bf16[2,2,256,768]{3,2,1,0:T(8,128)(2,1)}) custom-call(s32[3]{0:T(128)S(1)} %pad_add_fusion.place, s32[4608]{0:T(1024)S(1)} %reshape.88.tiles, bf16[2,3072,512]{2,1,0:T(8,128)(2,1)S(1)} %bitcast.209, bf16[2,1024,512]{2,1,0:T(8,128)(2,1)S(1)} %collective-permute-done.16.low1, ...), custom_call_target="tpu_custom_call" | custom-call | flops 6442450944 | bytes 25165824 | tf_op jit(solution)/shard_map/products/pallas_call | solution.py:113
  312.9 14.7 %products.7 = (f32[2,2,256,768]{3,2,1,0:T(8,128)S(1)}, bf16[2,2,256,768]{3,2,1,0:T(8,128)(2,1)}) custom-call(s32[3]{0:T(128)S(1)} %pad_add_fusion.place, s32[4608]{0:T(1024)S(1)} %reshape.88.tiles, bf16[2,3072,512]{2,1,0:T(8,128)(2,1)S(1)} %bitcast.209, bf16[2,1024,512]{2,1,0:T(8,128)(2,1)S(1)} %collective-permute-done.16.low1, ...), custom_call_target="tpu_custom_call" | custom-call | flops 6442450944 | bytes 25165824 | tf_op jit(solution)/shard_map/products/pallas_call | solution.py:113
  329.9 14.0 %products.6 = (f32[2,2,256,768]{3,2,1,0:T(8,128)S(1)}, bf16[2,2,256,768]{3,2,1,0:T(8,128)(2,1)}) custom-call(s32[3]{0:T(128)S(1)} %pad_add_fusion.place, s32[4608]{0:T(1024)S(1)} %reshape.88.tiles, bf16[2,3072,512]{2,1,0:T(8,128)(2,1)S(1)} %bitcast.209, bf16[2,1024,512]{2,1,0:T(8,128)(2,1)} %collective-permute-done.low1, ...), custom_call_target="tpu_custom_call" | custom-call | flops 6442450944 | bytes 25165824 | tf_op jit(solution)/shard_map/products/pallas_call | solution.py:113
  364.5 8.2 %collective-permute-done.72 = bf16[2,256,768]{2,1,0:T(8,128)(2,1)S(1)} collective-permute-done((bf16[2,256,768]{2,1,0:T(8,128)(2,1)S(1)}, bf16[2,256,768]{2,1,0:T(8,128)(2,1)S(1)}, u32[]{:S(2)}, u32[]{:S(2)}) %collective-permute-start.72) | collective-permute-done | bytes 786464 | tf_op jit(solution)/shard_map/ppermute | solution.py:280
  374.2 15.4 %collective-permute-done.32 = bf16[2,256,768]{2,1,0:T(8,128)(2,1)S(1)} collective-permute-done((bf16[2,256,768]{2,1,0:T(8,128)(2,1)S(1)}, bf16[2,256,768]{2,1,0:T(8,128)(2,1)S(1)}, u32[]{:S(2)}, u32[]{:S(2)}) %collective-permute-start.32) | collective-permute-done | bytes 786464 | tf_op jit(solution)/shard_map/ppermute | solution.py:280
  391.7 14.6 %collective-permute-done.65 = bf16[2,256,768]{2,1,0:T(8,128)(2,1)S(1)} collective-permute-done((bf16[2,256,768]{2,1,0:T(8,128)(2,1)S(1)}, bf16[2,256,768]{2,1,0:T(8,128)(2,1)S(1)}, u32[]{:S(2)}, u32[]{:S(2)}) %collective-permute-start.65) | collective-permute-done | bytes 786464 | tf_op jit(solution)/shard_map/ppermute | solution.py:280
  409.4 13.8 %collective-permute-done.57 = bf16[2,256,768]{2,1,0:T(8,128)(2,1)S(1)} collective-permute-done((bf16[2,256,768]{2,1,0:T(8,128)(2,1)S(1)}, bf16[2,256,768]{2,1,0:T(8,128)(2,1)S(1)}, u32[]{:S(2)}, u32[]{:S(2)}) %collective-permute-start.57) | collective-permute-done | bytes 786464 | tf_op jit(solution)/shard_map/ppermute | solution.py:280
  426.1 13.9 %collective-permute-done.18 = bf16[2,256,768]{2,1,0:T(8,128)(2,1)S(1)} collective-permute-done((bf16[2,256,768]{2,1,0:T(8,128)(2,1)S(1)}, bf16[2,256,768]{2,1,0:T(8,128)(2,1)S(1)}, u32[]{:S(2)}, u32[]{:S(2)}) %collective-permute-start.18) | collective-permute-done | bytes 786464 | tf_op jit(solution)/shard_map/ppermute | solution.py:280
  442.7 13.2 %collective-permute-done.10 = bf16[2,256,768]{2,1,0:T(8,128)(2,1)S(1)} collective-permute-done((bf16[2,256,768]{2,1,0:T(8,128)(2,1)S(1)}, bf16[2,256,768]{2,1,0:T(8,128)(2,1)S(1)}, u32[]{:S(2)}, u32[]{:S(2)}) %collective-permute-start.10) | collective-permute-done | bytes 786464 | tf_op jit(solution)/shard_map/ppermute | solution.py:280
  458.8 4.1 collective-permute-start.34
  465.1 7.3 %collective-permute-start.67 = (bf16[256,768]{1,0:T(8,128)(2,1)S(1)}, bf16[256,768]{1,0:T(8,128)(2,1)S(1)}, u32[]{:S(2)}, u32[]{:S(2)}) collective-permute-start(bf16[256,768]{1,0:T(8,128)(2,1)S(1)} %get-tuple-element.63), channel_id=1, source_target_pairs={{0,1},{3,2},{4,5},{7,6},{8,9},{11,10},{12,13},{15,14},{16,17},{19,... | collective-permute-start | bytes 1179656 | tf_op jit(solution)/shard_map/ppermute | solution.py:283
  482.0 9.7 %collective-permute-start.59 = (bf16[256,768]{1,0:T(8,128)(2,1)S(1)}, bf16[256,768]{1,0:T(8,128)(2,1)S(1)}, u32[]{:S(2)}, u32[]{:S(2)}) collective-permute-start(bf16[256,768]{1,0:T(8,128)(2,1)S(1)} %get-tuple-element.65), channel_id=1, source_target_pairs={{0,1},{3,2},{4,5},{7,6},{8,9},{11,10},{12,13},{15,14},{16,17},{19,... | collective-permute-start | bytes 1179656 | tf_op jit(solution)/shard_map/ppermute | solution.py:283
  491.8 11.2 %collective-permute-done.19 = bf16[256,768]{1,0:T(8,128)(2,1)S(1)} collective-permute-done((bf16[256,768]{1,0:T(8,128)(2,1)S(1)}, bf16[256,768]{1,0:T(8,128)(2,1)S(1)}, u32[]{:S(2)}, u32[]{:S(2)}) %collective-permute-start.19) | collective-permute-done | bytes 393248 | tf_op jit(solution)/shard_map/ppermute | solution.py:284
  508.9 18.0 %collective-permute-done.58 = bf16[256,768]{1,0:T(8,128)(2,1)S(1)} collective-permute-done((bf16[256,768]{1,0:T(8,128)(2,1)S(1)}, bf16[256,768]{1,0:T(8,128)(2,1)S(1)}, u32[]{:S(2)}, u32[]{:S(2)}) %collective-permute-start.58) | collective-permute-done | bytes 393248 | tf_op jit(solution)/shard_map/ppermute | solution.py:284
  528.6 4.2 collective-permute-start.40
  535.0 4.5 collective-permute-done.11
  539.5 13.1 %collective-permute-start.38 = (bf16[256,512]{1,0:T(8,128)(2,1)S(1)}, bf16[256,512]{1,0:T(8,128)(2,1)S(1)}, u32[]{:S(2)}, u32[]{:S(2)}) collective-permute-start(bf16[256,512]{1,0:T(8,128)(2,1)S(1)} %convolution_convert_fusion.7), channel_id=1, source_target_pairs={{0,1},{4,5},{8,9},{12,13},{16,17},{20,21},{24,25},{28,29}} | collective-permute-start | bytes 786440 | tf_op jit(solution)/shard_map/ppermute | solution.py:293
  565.7 4.3 collective-permute-done.44
  570.0 5.6 collective-permute-done.43
  575.7 5.6 collective-permute-done.27
  581.2 5.6 collective-permute-done.26
  592.8 22.5 %collective-permute-done.76.refs_2_ = bf16[256,768]{1,0:T(8,128)(2,1)S(1)} collective-permute-done((bf16[256,768]{1,0:T(8,128)(2,1)S(1)}, bf16[256,768]{1,0:T(8,128)(2,1)S(1)}, u32[]{:S(2)}, u32[]{:S(2)}) %collective-permute-start.76) | collective-permute-done | bytes 393248 | tf_op jit(solution)/shard_map/ppermute | solution.py:288
  616.4 4.0 collective-permute-done.69.refs_2_
  626.1 5.6 collective-permute-done.46.refs_6_
  631.7 5.1 collective-permute-done.28.refs_6_
  642.5 6.9 collective-permute-done.24
  651.5 4.9 final.6
  656.4 4.6 final.7
  661.0 4.6 final.8
  674.8 5.2 final.10.refs_8_
  682.7 4.9 final.11
  (308 shorter events, 172.3 us)
Async XLA Ops:
  15.0 34.3 %collective-permute-start.48 = (bf16[2,256,768]{2,1,0:T(8,128)(2,1)}, bf16[2,256,768]{2,1,0:T(8,128)(2,1)}, u32[]{:S(2)}, u32[]{:S(2)}) collective-permute-start(bf16[2,256,768]{2,1,0:T(8,128)(2,1)} %get-tuple-element.48), channel_id=1, source_target_pairs={{0,2},{3,1},{4,6},{7,5},{8,10},{11,9},{12,14},{15,13},{16,18},{19,... | collective-permute-start | bytes 2359304 | tf_op jit(solution)/shard_map/ppermute | solution.py:253
  17.2 48.8 %collective-permute-start.5 = (bf16[2,256,768]{2,1,0:T(8,128)(2,1)S(1)}, bf16[2,256,768]{2,1,0:T(8,128)(2,1)}, u32[]{:S(2)}, u32[]{:S(2)}) collective-permute-start(bf16[2,256,768]{2,1,0:T(8,128)(2,1)S(1)} %get-tuple-element.51), channel_id=1, source_target_pairs={{0,2},{3,1},{4,6},{7,5},{8,10},{11,9},{12,14},{15,13},{16,18},{19,... | collective-permute-start | bytes 2359304 | tf_op jit(solution)/shard_map/ppermute | solution.py:253
  19.4 31.4 %collective-permute-start.54 = (bf16[2,256,768]{2,1,0:T(8,128)(2,1)}, bf16[2,256,768]{2,1,0:T(8,128)(2,1)}, u32[]{:S(2)}, u32[]{:S(2)}) collective-permute-start(bf16[2,256,768]{2,1,0:T(8,128)(2,1)} %get-tuple-element.55), channel_id=1, source_target_pairs={{1,2},{2,1},{5,6},{6,5},{9,10},{10,9},{13,14},{14,13},{17,18},{18,... | collective-permute-start | bytes 2359304 | tf_op jit(solution)/shard_map/ppermute | solution.py:254
  20.9 31.2 %collective-permute-start.53 = (bf16[2,256,768]{2,1,0:T(8,128)(2,1)}, bf16[2,256,768]{2,1,0:T(8,128)(2,1)}, u32[]{:S(2)}, u32[]{:S(2)}) collective-permute-start(bf16[2,256,768]{2,1,0:T(8,128)(2,1)} %get-tuple-element.56), channel_id=1, source_target_pairs={{1,0},{2,3},{5,4},{6,7},{9,8},{10,11},{13,12},{14,15},{17,16},{18,... | collective-permute-start | bytes 2359304 | tf_op jit(solution)/shard_map/ppermute | solution.py:252
  32.4 49.3 %collective-permute-start.1 = (bf16[2,256,768]{2,1,0:T(8,128)(2,1)S(1)}, bf16[2,256,768]{2,1,0:T(8,128)(2,1)}, u32[]{:S(2)}, u32[]{:S(2)}) collective-permute-start(bf16[2,256,768]{2,1,0:T(8,128)(2,1)S(1)} %get-tuple-element.54), channel_id=1, source_target_pairs={{0,2},{3,1},{4,6},{7,5},{8,10},{11,9},{12,14},{15,13},{16,18},{19,... | collective-permute-start | bytes 2359304 | tf_op jit(solution)/shard_map/ppermute | solution.py:253
  49.3 40.1 %collective-permute-start.50 = (bf16[2,256,768]{2,1,0:T(8,128)(2,1)}, bf16[2,256,768]{2,1,0:T(8,128)(2,1)}, u32[]{:S(2)}, u32[]{:S(2)}) collective-permute-start(bf16[2,256,768]{2,1,0:T(8,128)(2,1)} %get-tuple-element.46), channel_id=1, source_target_pairs={{1,2},{2,1},{5,6},{6,5},{9,10},{10,9},{13,14},{14,13},{17,18},{18,... | collective-permute-start | bytes 2359304 | tf_op jit(solution)/shard_map/ppermute | solution.py:254
  50.8 70.2 %collective-permute-start.49 = (bf16[2,256,768]{2,1,0:T(8,128)(2,1)}, bf16[2,256,768]{2,1,0:T(8,128)(2,1)}, u32[]{:S(2)}, u32[]{:S(2)}) collective-permute-start(bf16[2,256,768]{2,1,0:T(8,128)(2,1)} %get-tuple-element.47), channel_id=1, source_target_pairs={{1,0},{2,3},{5,4},{6,7},{9,8},{10,11},{13,12},{14,15},{17,16},{18,... | collective-permute-start | bytes 2359304 | tf_op jit(solution)/shard_map/ppermute | solution.py:252
  52.1 69.6 %collective-permute-start.3 = (bf16[2,256,768]{2,1,0:T(8,128)(2,1)}, bf16[2,256,768]{2,1,0:T(8,128)(2,1)}, u32[]{:S(2)}, u32[]{:S(2)}) collective-permute-start(bf16[2,256,768]{2,1,0:T(8,128)(2,1)} %get-tuple-element.52), channel_id=1, source_target_pairs={{1,2},{2,1},{5,6},{6,5},{9,10},{10,9},{13,14},{14,13},{17,18},{18,... | collective-permute-start | bytes 2359304 | tf_op jit(solution)/shard_map/ppermute | solution.py:254
  66.0 71.9 %collective-permute-start.2 = (bf16[2,256,768]{2,1,0:T(8,128)(2,1)}, bf16[2,256,768]{2,1,0:T(8,128)(2,1)}, u32[]{:S(2)}, u32[]{:S(2)}) collective-permute-start(bf16[2,256,768]{2,1,0:T(8,128)(2,1)} %get-tuple-element.53), channel_id=1, source_target_pairs={{1,0},{2,3},{5,4},{6,7},{9,8},{10,11},{13,12},{14,15},{17,16},{18,... | collective-permute-start | bytes 2359304 | tf_op jit(solution)/shard_map/ppermute | solution.py:252
  85.2 118.3 %collective-permute-start.55 = (bf16[2,2,256,768]{3,2,1,0:T(8,128)(2,1)S(1)}, bf16[2,2,256,768]{3,2,1,0:T(8,128)(2,1)}, u32[]{:S(2)}, u32[]{:S(2)}) collective-permute-start(bf16[2,2,256,768]{3,2,1,0:T(8,128)(2,1)S(1)} %pad_maximum_fusion.3.so_ref), channel_id=1, source_target_pairs={{0,4},{4,0},{1,5},{5,1},{2,6},{6,2},{3,7},{7,3},{8,12},{12,8},{9,1... | collective-permute-start | bytes 4718600 | tf_op jit(solution)/shard_map/ppermute | solution.py:256
  89.3 127.0 %collective-permute-start.30 = (bf16[2,1024,512]{2,1,0:T(8,128)(2,1)}, bf16[2,1024,512]{2,1,0:T(8,128)(2,1)}, u32[]{:S(2)}, u32[]{:S(2)}) collective-permute-start(bf16[2,1024,512]{2,1,0:T(8,128)(2,1)} %get-tuple-element.57), channel_id=1, source_target_pairs={{0,1},{1,0},{2,3},{3,2},{4,5},{5,4},{6,7},{7,6},{8,9},{9,8},{10,11... | collective-permute-start | bytes 6291464 | tf_op jit(solution)/shard_map/ppermute | solution.py:259
  121.8 77.1 %collective-permute-start.6 = (bf16[2,256,768]{2,1,0:T(8,128)(2,1)}, bf16[2,256,768]{2,1,0:T(8,128)(2,1)S(1)}, u32[]{:S(2)}, u32[]{:S(2)}) collective-permute-start(bf16[2,256,768]{2,1,0:T(8,128)(2,1)} %get-tuple-element.50), channel_id=1, source_target_pairs={{1,0},{2,3},{5,4},{6,7},{9,8},{10,11},{13,12},{14,15},{17,16},{18,... | collective-permute-start | bytes 2359304 | tf_op jit(solution)/shard_map/ppermute | solution.py:252
  137.9 72.3 %collective-permute-start.51 = (bf16[2,2,256,768]{3,2,1,0:T(8,128)(2,1)}, bf16[2,2,256,768]{3,2,1,0:T(8,128)(2,1)}, u32[]{:S(2)}, u32[]{:S(2)}) collective-permute-start(bf16[2,2,256,768]{3,2,1,0:T(8,128)(2,1)} %pad_maximum_fusion.2.so_ref), channel_id=1, source_target_pairs={{0,4},{4,0},{1,5},{5,1},{2,6},{6,2},{3,7},{7,3},{8,12},{12,8},{9,1... | collective-permute-start | bytes 4718600 | tf_op jit(solution)/shard_map/ppermute | solution.py:256
  141.9 92.2 %collective-permute-start.4 = (bf16[2,2,256,768]{3,2,1,0:T(8,128)(2,1)}, bf16[2,2,256,768]{3,2,1,0:T(8,128)(2,1)}, u32[]{:S(2)}, u32[]{:S(2)}) collective-permute-start(bf16[2,2,256,768]{3,2,1,0:T(8,128)(2,1)} %pad_maximum_fusion.so_ref), channel_id=1, source_target_pairs={{0,4},{4,0},{1,5},{5,1},{2,6},{6,2},{3,7},{7,3},{8,12},{12,8},{9,1... | collective-permute-start | bytes 4718600 | tf_op jit(solution)/shard_map/ppermute | solution.py:256
  200.3 40.3 %collective-permute-start.8 = (bf16[2,2,256,768]{3,2,1,0:T(8,128)(2,1)}, bf16[2,2,256,768]{3,2,1,0:T(8,128)(2,1)}, u32[]{:S(2)}, u32[]{:S(2)}) collective-permute-start(bf16[2,2,256,768]{3,2,1,0:T(8,128)(2,1)} %pad_maximum_fusion.1.so_ref), channel_id=1, source_target_pairs={{0,4},{4,0},{1,5},{5,1},{2,6},{6,2},{3,7},{7,3},{8,12},{12,8},{9,1... | collective-permute-start | bytes 4718600 | tf_op jit(solution)/shard_map/ppermute | solution.py:256
  203.6 56.9 %collective-permute-start = (bf16[2,1024,512]{2,1,0:T(8,128)(2,1)}, bf16[2,1024,512]{2,1,0:T(8,128)(2,1)}, u32[]{:S(2)}, u32[]{:S(2)}) collective-permute-start(bf16[2,1024,512]{2,1,0:T(8,128)(2,1)} %get-tuple-element.59), channel_id=1, source_target_pairs={{0,1},{1,0},{2,3},{3,2},{4,5},{5,4},{6,7},{7,6},{8,9},{9,8},{10,11... | collective-permute-start | bytes 6291464 | tf_op jit(solution)/shard_map/ppermute | solution.py:259
  210.2 85.3 %collective-permute-start.16 = (bf16[2,1024,512]{2,1,0:T(8,128)(2,1)}, bf16[2,1024,512]{2,1,0:T(8,128)(2,1)S(1)}, u32[]{:S(2)}, u32[]{:S(2)}) collective-permute-start(bf16[2,1024,512]{2,1,0:T(8,128)(2,1)} %get-tuple-element.58), channel_id=1, source_target_pairs={{0,1},{1,0},{2,3},{3,2},{4,5},{5,4},{6,7},{7,6},{8,9},{9,8},{10,11... | collective-permute-start | bytes 6291464 | tf_op jit(solution)/shard_map/ppermute | solution.py:259
  233.1 112.4 %collective-permute-start.71 = (bf16[2,2,256,768]{3,2,1,0:T(8,128)(2,1)S(1)}, bf16[2,2,256,768]{3,2,1,0:T(8,128)(2,1)S(1)}, u32[]{:S(2)}, u32[]{:S(2)}) collective-permute-start(bf16[2,2,256,768]{3,2,1,0:T(8,128)(2,1)S(1)} %get-tuple-element.37), channel_id=1, source_target_pairs={{0,8},{8,0},{16,24},{24,16},{1,9},{9,1},{17,25},{25,17},{2,10},{10... | collective-permute-start | bytes 4718600 | tf_op jit(solution)/shard_map/ppermute | solution.py:278
  260.4 91.7 %collective-permute-start.31 = (bf16[2,2,256,768]{3,2,1,0:T(8,128)(2,1)S(1)}, bf16[2,2,256,768]{3,2,1,0:T(8,128)(2,1)}, u32[]{:S(2)}, u32[]{:S(2)}) collective-permute-start(bf16[2,2,256,768]{3,2,1,0:T(8,128)(2,1)S(1)} %get-tuple-element.26), channel_id=1, source_target_pairs={{0,8},{8,0},{16,24},{24,16},{1,9},{9,1},{17,25},{25,17},{2,10},{10... | collective-permute-start | bytes 4718600 | tf_op jit(solution)/shard_map/ppermute | solution.py:278
  279.5 74.8 %collective-permute-start.64 = (bf16[2,2,256,768]{3,2,1,0:T(8,128)(2,1)}, bf16[2,2,256,768]{3,2,1,0:T(8,128)(2,1)}, u32[]{:S(2)}, u32[]{:S(2)}) collective-permute-start(bf16[2,2,256,768]{3,2,1,0:T(8,128)(2,1)} %get-tuple-element.35), channel_id=1, source_target_pairs={{0,8},{8,0},{16,24},{24,16},{1,9},{9,1},{17,25},{25,17},{2,10},{10... | collective-permute-start | bytes 4718600 | tf_op jit(solution)/shard_map/ppermute | solution.py:278
  312.9 44.3 %collective-permute-start.56 = (bf16[2,2,256,768]{3,2,1,0:T(8,128)(2,1)}, bf16[2,2,256,768]{3,2,1,0:T(8,128)(2,1)}, u32[]{:S(2)}, u32[]{:S(2)}) collective-permute-start(bf16[2,2,256,768]{3,2,1,0:T(8,128)(2,1)} %get-tuple-element.33), channel_id=1, source_target_pairs={{0,8},{8,0},{16,24},{24,16},{1,9},{9,1},{17,25},{25,17},{2,10},{10... | collective-permute-start | bytes 4718600 | tf_op jit(solution)/shard_map/ppermute | solution.py:278
  329.3 30.1 %collective-permute-start.17 = (bf16[2,2,256,768]{3,2,1,0:T(8,128)(2,1)}, bf16[2,2,256,768]{3,2,1,0:T(8,128)(2,1)}, u32[]{:S(2)}, u32[]{:S(2)}) collective-permute-start(bf16[2,2,256,768]{3,2,1,0:T(8,128)(2,1)} %get-tuple-element.24), channel_id=1, source_target_pairs={{0,8},{8,0},{16,24},{24,16},{1,9},{9,1},{17,25},{25,17},{2,10},{10... | collective-permute-start | bytes 4718600 | tf_op jit(solution)/shard_map/ppermute | solution.py:278
  354.3 35.2 %collective-permute-start.32 = (bf16[2,256,768]{2,1,0:T(8,128)(2,1)S(1)}, bf16[2,256,768]{2,1,0:T(8,128)(2,1)S(1)}, u32[]{:S(2)}, u32[]{:S(2)}) collective-permute-start(bf16[2,256,768]{2,1,0:T(8,128)(2,1)S(1)} %fusion.26), channel_id=1, source_target_pairs={{0,16},{16,0},{8,24},{24,8},{1,17},{17,1},{9,25},{25,9},{2,18},{18... | collective-permute-start | bytes 2359304 | tf_op jit(solution)/shard_map/ppermute | solution.py:280
  357.3 49.1 %collective-permute-start.65 = (bf16[2,256,768]{2,1,0:T(8,128)(2,1)S(1)}, bf16[2,256,768]{2,1,0:T(8,128)(2,1)S(1)}, u32[]{:S(2)}, u32[]{:S(2)}) collective-permute-start(bf16[2,256,768]{2,1,0:T(8,128)(2,1)S(1)} %fusion.28), channel_id=1, source_target_pairs={{0,16},{16,0},{8,24},{24,8},{1,17},{17,1},{9,25},{25,9},{2,18},{18... | collective-permute-start | bytes 2359304 | tf_op jit(solution)/shard_map/ppermute | solution.py:280
  359.4 63.8 %collective-permute-start.57 = (bf16[2,256,768]{2,1,0:T(8,128)(2,1)S(1)}, bf16[2,256,768]{2,1,0:T(8,128)(2,1)S(1)}, u32[]{:S(2)}, u32[]{:S(2)}) collective-permute-start(bf16[2,256,768]{2,1,0:T(8,128)(2,1)S(1)} %fusion.27), channel_id=1, source_target_pairs={{0,16},{16,0},{8,24},{24,8},{1,17},{17,1},{9,25},{25,9},{2,18},{18... | collective-permute-start | bytes 2359304 | tf_op jit(solution)/shard_map/ppermute | solution.py:280
  362.3 77.7 %collective-permute-start.18 = (bf16[2,256,768]{2,1,0:T(8,128)(2,1)S(1)}, bf16[2,256,768]{2,1,0:T(8,128)(2,1)S(1)}, u32[]{:S(2)}, u32[]{:S(2)}) collective-permute-start(bf16[2,256,768]{2,1,0:T(8,128)(2,1)S(1)} %fusion.25), channel_id=1, source_target_pairs={{0,16},{16,0},{8,24},{24,8},{1,17},{17,1},{9,25},{25,9},{2,18},{18... | collective-permute-start | bytes 2359304 | tf_op jit(solution)/shard_map/ppermute | solution.py:280
  372.7 83.3 %collective-permute-start.10 = (bf16[2,256,768]{2,1,0:T(8,128)(2,1)S(1)}, bf16[2,256,768]{2,1,0:T(8,128)(2,1)S(1)}, u32[]{:S(2)}, u32[]{:S(2)}) collective-permute-start(bf16[2,256,768]{2,1,0:T(8,128)(2,1)S(1)} %fusion.24), channel_id=1, source_target_pairs={{0,16},{16,0},{8,24},{24,8},{1,17},{17,1},{9,25},{25,9},{2,18},{18... | collective-permute-start | bytes 2359304 | tf_op jit(solution)/shard_map/ppermute | solution.py:280
  389.5 73.4 %collective-permute-start.75 = (bf16[256,768]{1,0:T(8,128)(2,1)S(1)}, bf16[256,768]{1,0:T(8,128)(2,1)S(1)}, u32[]{:S(2)}, u32[]{:S(2)}) collective-permute-start(bf16[256,768]{1,0:T(8,128)(2,1)S(1)} %get-tuple-element.61), channel_id=1, source_target_pairs={{1,2},{2,1},{5,6},{6,5},{9,10},{10,9},{13,14},{14,13},{17,18},{18,... | collective-permute-start | bytes 1179656 | tf_op jit(solution)/shard_map/ppermute | solution.py:285
  406.4 57.9 %collective-permute-start.74 = (bf16[256,768]{1,0:T(8,128)(2,1)S(1)}, bf16[256,768]{1,0:T(8,128)(2,1)S(1)}, u32[]{:S(2)}, u32[]{:S(2)}) collective-permute-start(bf16[256,768]{1,0:T(8,128)(2,1)S(1)} %get-tuple-element.61), channel_id=1, source_target_pairs={{0,1},{3,2},{4,5},{7,6},{8,9},{11,10},{12,13},{15,14},{16,17},{19,... | collective-permute-start | bytes 1179656 | tf_op jit(solution)/shard_map/ppermute | solution.py:283
  423.2 35.6 %collective-permute-start.73 = (bf16[256,768]{1,0:T(8,128)(2,1)S(1)}, bf16[256,768]{1,0:T(8,128)(2,1)S(1)}, u32[]{:S(2)}, u32[]{:S(2)}) collective-permute-start(bf16[256,768]{1,0:T(8,128)(2,1)S(1)} %get-tuple-element.60), channel_id=1, source_target_pairs={{1,3},{2,0},{5,7},{6,4},{9,11},{10,8},{13,15},{14,12},{17,19},{18,... | collective-permute-start | bytes 1179656 | tf_op jit(solution)/shard_map/ppermute | solution.py:284
  472.7 31.1 %collective-permute-start.21 = (bf16[256,768]{1,0:T(8,128)(2,1)S(1)}, bf16[256,768]{1,0:T(8,128)(2,1)S(1)}, u32[]{:S(2)}, u32[]{:S(2)}) collective-permute-start(bf16[256,768]{1,0:T(8,128)(2,1)S(1)} %get-tuple-element.69), channel_id=1, source_target_pairs={{1,2},{2,1},{5,6},{6,5},{9,10},{10,9},{13,14},{14,13},{17,18},{18,... | collective-permute-start | bytes 1179656 | tf_op jit(solution)/shard_map/ppermute | solution.py:285
  473.4 33.6 %collective-permute-start.20 = (bf16[256,768]{1,0:T(8,128)(2,1)S(1)}, bf16[256,768]{1,0:T(8,128)(2,1)S(1)}, u32[]{:S(2)}, u32[]{:S(2)}) collective-permute-start(bf16[256,768]{1,0:T(8,128)(2,1)S(1)} %get-tuple-element.69), channel_id=1, source_target_pairs={{0,1},{3,2},{4,5},{7,6},{8,9},{11,10},{12,13},{15,14},{16,17},{19,... | collective-permute-start | bytes 1179656 | tf_op jit(solution)/shard_map/ppermute | solution.py:283
  479.3 49.3 %collective-permute-start.60 = (bf16[256,768]{1,0:T(8,128)(2,1)S(1)}, bf16[256,768]{1,0:T(8,128)(2,1)S(1)}, u32[]{:S(2)}, u32[]{:S(2)}) collective-permute-start(bf16[256,768]{1,0:T(8,128)(2,1)S(1)} %get-tuple-element.65), channel_id=1, source_target_pairs={{1,2},{2,1},{5,6},{6,5},{9,10},{10,9},{13,14},{14,13},{17,18},{18,... | collective-permute-start | bytes 1179656 | tf_op jit(solution)/shard_map/ppermute | solution.py:285
  482.0 50.8 %collective-permute-start.59 = (bf16[256,768]{1,0:T(8,128)(2,1)S(1)}, bf16[256,768]{1,0:T(8,128)(2,1)S(1)}, u32[]{:S(2)}, u32[]{:S(2)}) collective-permute-start(bf16[256,768]{1,0:T(8,128)(2,1)S(1)} %get-tuple-element.65), channel_id=1, source_target_pairs={{0,1},{3,2},{4,5},{7,6},{8,9},{11,10},{12,13},{15,14},{16,17},{19,... | collective-permute-start | bytes 1179656 | tf_op jit(solution)/shard_map/ppermute | solution.py:283
  503.0 49.6 %collective-permute-start.13 = (bf16[256,768]{1,0:T(8,128)(2,1)S(1)}, bf16[256,768]{1,0:T(8,128)(2,1)S(1)}, u32[]{:S(2)}, u32[]{:S(2)}) collective-permute-start(bf16[256,768]{1,0:T(8,128)(2,1)S(1)} %get-tuple-element.71), channel_id=1, source_target_pairs={{1,2},{2,1},{5,6},{6,5},{9,10},{10,9},{13,14},{14,13},{17,18},{18,... | collective-permute-start | bytes 1179656 | tf_op jit(solution)/shard_map/ppermute | solution.py:285
  503.7 52.4 %collective-permute-start.12 = (bf16[256,768]{1,0:T(8,128)(2,1)S(1)}, bf16[256,768]{1,0:T(8,128)(2,1)S(1)}, u32[]{:S(2)}, u32[]{:S(2)}) collective-permute-start(bf16[256,768]{1,0:T(8,128)(2,1)S(1)} %get-tuple-element.71), channel_id=1, source_target_pairs={{0,1},{3,2},{4,5},{7,6},{8,9},{11,10},{12,13},{15,14},{16,17},{19,... | collective-permute-start | bytes 1179656 | tf_op jit(solution)/shard_map/ppermute | solution.py:283
  528.6 29.1 %collective-permute-start.40 = (bf16[256,512]{1,0:T(8,128)(2,1)S(1)}, bf16[256,512]{1,0:T(8,128)(2,1)S(1)}, u32[]{:S(2)}, u32[]{:S(2)}) collective-permute-start(bf16[256,512]{1,0:T(8,128)(2,1)S(1)} %convolution_convert_fusion.7), channel_id=1, source_target_pairs={{0,3},{4,7},{8,11},{12,15},{16,19},{20,23},{24,27},{28,31}} | collective-permute-start | bytes 786440 | tf_op jit(solution)/shard_map/ppermute | solution.py:293
  532.8 26.5 %collective-permute-start.39 = (bf16[256,512]{1,0:T(8,128)(2,1)S(1)}, bf16[256,512]{1,0:T(8,128)(2,1)S(1)}, u32[]{:S(2)}, u32[]{:S(2)}) collective-permute-start(bf16[256,512]{1,0:T(8,128)(2,1)S(1)} %convolution_convert_fusion.7), channel_id=1, source_target_pairs={{0,2},{4,6},{8,10},{12,14},{16,18},{20,22},{24,26},{28,30}} | collective-permute-start | bytes 786440 | tf_op jit(solution)/shard_map/ppermute | solution.py:293
  560.6 26.2 %collective-permute-start.26 = (bf16[256,512]{1,0:T(8,128)(2,1)S(1)}, bf16[256,512]{1,0:T(8,128)(2,1)S(1)}, u32[]{:S(2)}, u32[]{:S(2)}) collective-permute-start(bf16[256,512]{1,0:T(8,128)(2,1)S(1)} %convolution_convert_fusion.8), channel_id=1, source_target_pairs={{0,2},{4,6},{8,10},{12,14},{16,18},{20,22},{24,26},{28,30}} | collective-permute-start | bytes 786440 | tf_op jit(solution)/shard_map/ppermute | solution.py:293
  564.4 26.0 %collective-permute-start.25 = (bf16[256,512]{1,0:T(8,128)(2,1)S(1)}, bf16[256,512]{1,0:T(8,128)(2,1)S(1)}, u32[]{:S(2)}, u32[]{:S(2)}) collective-permute-start(bf16[256,512]{1,0:T(8,128)(2,1)S(1)} %convolution_convert_fusion.8), channel_id=1, source_target_pairs={{0,1},{4,5},{8,9},{12,13},{16,17},{20,21},{24,25},{28,29}} | collective-permute-start | bytes 786440 | tf_op jit(solution)/shard_map/ppermute | solution.py:293
  581.2 35.1 %collective-permute-start.36 = (bf16[256,768]{1,0:T(8,128)(2,1)S(1)}, bf16[256,768]{1,0:T(8,128)(2,1)S(1)}, u32[]{:S(2)}, u32[]{:S(2)}) collective-permute-start(bf16[256,768]{1,0:T(8,128)(2,1)S(1)} %select_convert_fusion.3.refs_1_), channel_id=1, source_target_pairs={{0,16},{16,0},{8,24},{24,8},{1,17},{17,1},{9,25},{25,9},{2,18},{18... | collective-permute-start | bytes 1179656 | tf_op jit(solution)/shard_map/ppermute | solution.py:288
  586.9 34.6 %collective-permute-start.14 = (bf16[256,768]{1,0:T(8,128)(2,1)S(1)}, bf16[256,768]{1,0:T(8,128)(2,1)S(1)}, u32[]{:S(2)}, u32[]{:S(2)}) collective-permute-start(bf16[256,768]{1,0:T(8,128)(2,1)S(1)} %select_convert_fusion.5.refs_1_), channel_id=1, source_target_pairs={{0,16},{16,0},{8,24},{24,8},{1,17},{17,1},{9,25},{25,9},{2,18},{18... | collective-permute-start | bytes 1179656 | tf_op jit(solution)/shard_map/ppermute | solution.py:288
  590.4 30.0 %collective-permute-start.69 = (bf16[256,768]{1,0:T(8,128)(2,1)S(1)}, bf16[256,768]{1,0:T(8,128)(2,1)S(1)}, u32[]{:S(2)}, u32[]{:S(2)}) collective-permute-start(bf16[256,768]{1,0:T(8,128)(2,1)S(1)} %select_convert_fusion.1.refs_1_), channel_id=1, source_target_pairs={{0,16},{16,0},{8,24},{24,8},{1,17},{17,1},{9,25},{25,9},{2,18},{18... | collective-permute-start | bytes 1179656 | tf_op jit(solution)/shard_map/ppermute | solution.py:288
  592.6 44.2 %collective-permute-start.62 = (bf16[2,256,768]{2,1,0:T(8,128)(2,1)S(1)}, bf16[2,256,768]{2,1,0:T(8,128)(2,1)S(1)}, u32[]{:S(2)}, u32[]{:S(2)}) collective-permute-start(bf16[2,256,768]{2,1,0:T(8,128)(2,1)S(1)} %pad_maximum_fusion.8), channel_id=1, source_target_pairs={{0,8},{8,0},{16,24},{24,16},{1,9},{9,1},{17,25},{25,17},{2,10},{10... | collective-permute-start | bytes 2359304 | tf_op jit(solution)/shard_map/ppermute | solution.py:289
  626.0 30.4 %collective-permute-start.37 = (bf16[2,256,768]{2,1,0:T(8,128)(2,1)S(1)}, bf16[2,256,768]{2,1,0:T(8,128)(2,1)S(1)}, u32[]{:S(2)}, u32[]{:S(2)}) collective-permute-start(bf16[2,256,768]{2,1,0:T(8,128)(2,1)S(1)} %pad_maximum_fusion.7), channel_id=1, source_target_pairs={{0,8},{8,0},{16,24},{24,16},{1,9},{9,1},{17,25},{25,17},{2,10},{10... | collective-permute-start | bytes 2359304 | tf_op jit(solution)/shard_map/ppermute | solution.py:289
  631.6 29.4 %collective-permute-start.15 = (bf16[2,256,768]{2,1,0:T(8,128)(2,1)S(1)}, bf16[2,256,768]{2,1,0:T(8,128)(2,1)S(1)}, u32[]{:S(2)}, u32[]{:S(2)}) collective-permute-start(bf16[2,256,768]{2,1,0:T(8,128)(2,1)S(1)} %pad_maximum_fusion.5), channel_id=1, source_target_pairs={{0,8},{8,0},{16,24},{24,16},{1,9},{9,1},{17,25},{25,17},{2,10},{10... | collective-permute-start | bytes 2359304 | tf_op jit(solution)/shard_map/ppermute | solution.py:289
  642.1 28.0 %collective-permute-start.77 = (bf16[2,256,768]{2,1,0:T(8,128)(2,1)}, bf16[2,256,768]{2,1,0:T(8,128)(2,1)}, u32[]{:S(2)}, u32[]{:S(2)}) collective-permute-start(bf16[2,256,768]{2,1,0:T(8,128)(2,1)} %pad_maximum_fusion.10), channel_id=1, source_target_pairs={{0,8},{8,0},{16,24},{24,16},{1,9},{9,1},{17,25},{25,17},{2,10},{10... | collective-permute-start | bytes 2359304 | tf_op jit(solution)/shard_map/ppermute | solution.py:289
  656.4 26.2 %collective-permute-start.70 = (bf16[2,256,768]{2,1,0:T(8,128)(2,1)}, bf16[2,256,768]{2,1,0:T(8,128)(2,1)}, u32[]{:S(2)}, u32[]{:S(2)}) collective-permute-start(bf16[2,256,768]{2,1,0:T(8,128)(2,1)} %pad_maximum_fusion.9), channel_id=1, source_target_pairs={{0,8},{8,0},{16,24},{24,16},{1,9},{9,1},{17,25},{25,17},{2,10},{10... | collective-permute-start | bytes 2359304 | tf_op jit(solution)/shard_map/ppermute | solution.py:289
  (86 other events, 2063.6 us)

commit v2 on v1

--- a/solution.py
+++ b/solution.py
@@ -10,6 +10,8 @@
 BF = jnp.bfloat16
 F32 = jnp.float32
 MIB = 1024 * 1024
+GAP = 2
+COST = pl.CostEstimate(flops=1, transcendentals=0, bytes_accessed=1)
 SWAP = [(0, 1), (1, 0)]
 CORE = [(0, 1), (1, 0), (2, 3), (3, 2)]
 YPAIR = [(0, 2), (2, 0), (1, 3), (3, 1)]
@@ -55,6 +57,103 @@
     return anc_lower, anc_upper, a_sum - anc_mask * dot(anc_lower, anc_upper)
 
 
+def spec(shape, index=None):
+    if index is None:
+        return pl.BlockSpec(shape, lambda *_: (0,) * len(shape))
+    return pl.BlockSpec(shape, index)
+
+
+def step(body, name, place, operands, outs, *, in_specs=None, out_specs=None, grid=(1,)):
+    in_specs = in_specs or [None] * len(operands)
+    in_specs = [spec(o.shape) if i is None else i for o, i in zip(operands, in_specs)]
+    out_specs = out_specs or [spec(o) for o in outs]
+    made = pl.pallas_call(
+        body,
+        grid_spec=pltpu.PrefetchScalarGridSpec(
+            num_scalar_prefetch=1, grid=grid, in_specs=in_specs, out_specs=out_specs
+        ),
+        out_shape=[jax.ShapeDtypeStruct(o, BF) for o in outs],
+        cost_estimate=COST,
+        compiler_params=pltpu.CompilerParams(vmem_limit_bytes=16 * MIB),
+        name=name,
+    )(place, *operands)
+    return made if len(made) > 1 else made[0]
+
+
+def ends(place):
+    return (place[1] == 0) | (place[1] == 3)
+
+
+def lower_kernel(place, low, inv, out):
+    out[0] = dot(low[0, 0], inv[0, 0]).astype(BF)
+
+
+def stack_kernel(place, first, kept, came, out):
+    out[0] = first[...]
+
+    @pl.when(ends(place))
+    def _():
+        out[1] = kept[...]
+
+    @pl.when(jnp.logical_not(ends(place)))
+    def _():
+        out[1] = came[...]
+
+
+def pair_kernel(place, one, two, out):
+    out[0] = one[...]
+    out[1] = two[...]
+
+
+def cross_kernel(place, keep, recv, out):
+    out[0] = (keep[0, 0] + recv[0, 0].astype(F32)).astype(BF)
+
+
+def spread_kernel(place, keep, recv, came, to_a, to_b):
+    def mine(b):
+        return (keep[0, b] + recv[0, b].astype(F32) + came[b].astype(F32)).astype(BF)
+
+    to_a[...] = mine(0)
+    to_b[...] = mine(1)
+
+
+def total_kernel(place, arrived, kept, came, out):
+    @pl.when(ends(place))
+    def _():
+        out[...] = (arrived[...].astype(F32) + kept[...].astype(F32)).astype(BF)
+
+    @pl.when(jnp.logical_not(ends(place)))
+    def _():
+        out[...] = (arrived[...].astype(F32) + came[...].astype(F32)).astype(BF)
+
+
+def panel_kernel(place, anc, tq, inv, out):
+    w = inv.shape[0]
+    out[...] = dot((anc[...] + tq[:, :w].astype(F32)).astype(BF), inv[...]).astype(BF)
+
+
+def choose_kernel(place, own, came, out, *, source):
+    @pl.when(lax.rem(place[1], source) == 0)
+    def _():
+        out[...] = own[...]
+
+    @pl.when(lax.rem(place[1], source) != 0)
+    def _():
+        out[...] = came[...]
+
+
+def pivot_kernel(place, anc, tq, ty, tc, out):
+    for layer, top in ((0, tq), (2, ty), (1, tc.at[0]), (3, tc.at[1])):
+
+        @pl.when(place[2] == layer)
+        def _():
+            out[...] = (anc[...] + top[...].astype(F32)).astype(BF)
+
+
+def panel_upper_kernel(place, m_own, m_other, own, other, out):
+    out[...] = (dot(m_own[...], own[...]) + dot(m_other[...], other[...])).astype(BF)
+
+
 def upper_kernel(mo_ref, mt_ref, so_ref, st_ref, out_ref):
     total = dot(mo_ref[0], so_ref[0, 0]) + dot(mt_ref[0], st_ref[0, 0])
     out_ref[0, 0] = total.astype(BF)
@@ -71,69 +170,63 @@
         in_specs=[m_spec, m_spec, s_spec, s_spec],
         out_specs=pl.BlockSpec((1, 1, w, cw), lambda k, b: (b, k, 0, 0)),
         out_shape=jax.ShapeDtypeStruct((blocks, pair, w, cw), BF),
-        cost_estimate=pl.CostEstimate(
-            flops=4 * blocks * pair * w * half * cw, transcendentals=0,
-            bytes_accessed=2 * (2 * s_own.size + blocks * pair * w * cw),
-        ),
+        cost_estimate=COST,
         compiler_params=pltpu.CompilerParams(vmem_limit_bytes=16 * MIB),
         name="upper",
     )(m_own, m_other, s_own, s_other)
 
 
-def product_kernel(place, tiles, low0, low1, up0, up1, keep, send, acc, *, g, c, nt, rt, ct, tb, pair, tj):
+def product_kernel(place, tiles, low0, low1, up0, up1, keep, send, *, g, c, nt, rt, ct, tb, pair, tj):
     b, j = pl.program_id(0), pl.program_id(1)
     x, z, l = place[0], place[1], place[2]
     odd = lax.rem(z, 2)
-    column = jnp.where(b == 0, 3 * odd, 1 + odd) * ct + c * tj + j
+    column = jnp.where(b == 0, jnp.where(odd == 0, jnp.where(z == 0, 1, 0), jnp.where(z == 1, 3, 2)),
+                       jnp.where(z == 0, 0, jnp.where(z == 3, 3, 3 - z)))
+    column = column * ct + c * tj + j
     for p, flip in enumerate(PIECE):
         i = jnp.bitwise_xor(l, flip)
         rows = pl.ds(pl.multiple_of(i * tb, tb), tb)
-        acc[...] = jnp.zeros_like(acc)
-        for low, up, owner in ((low0, up0, z), (low1, up1, jnp.bitwise_xor(z, 1))):
+        total = None
+        for t, (low, up) in enumerate(((low0, up0), (low1, up1))):
             for k in range(pair):
-                leaf = owner * pair + k
+                leaf = (z - odd + t) * pair + k
                 flag = tiles[(leaf * nt + x * rt + g * 4 + i) * nt + column]
-
-                @pl.when(flag != 0)
-                def _():
-                    acc[...] += dot(low[k, rows, :], up[0, k])
-
+                term = dot(low[0, k, rows, :] * flag.astype(F32).astype(BF), up[0, k])
+                total = term if total is None else total + term
         if p < 2:
-            keep[p, 0] = acc[...]
+            keep[p, 0] = total
         else:
-            send[p - 2, 0] = acc[...].astype(BF)
-
-
-def products(place, tiles, low0, low1, up0, up1, *, g, c, nt, rt, ct, tb):
+            send[p - 2, 0] = total.astype(BF)
+
+
+def products(place, tiles, lows, up0, up1, *, g, c, nt, rt, ct, tb):
     blocks, pair, w, cw = up0.shape
     tj = cw // tb
     rows = 4 * tb
     up_spec = pl.BlockSpec((1, pair, w, tb), lambda b, j, *_: (b, 0, 0, j))
     out_spec = pl.BlockSpec((2, 1, tb, tb), lambda b, j, *_: (0, b, 0, j))
+    shared, at = lows
+    low_specs = [pl.BlockSpec((1, pair, rows, w), lambda b, j, *_, t=t: (t, 0, at, 0)) for t in range(2)]
     return pl.pallas_call(
         functools.partial(product_kernel, g=g, c=c, nt=nt, rt=rt, ct=ct, tb=tb, pair=pair, tj=tj),
         grid_spec=pltpu.PrefetchScalarGridSpec(
             num_scalar_prefetch=2,
             grid=(blocks, tj),
             in_specs=[
-                pl.BlockSpec((pair, rows, w), lambda b, j, *_: (0, g, 0)),
-                pl.BlockSpec((pair, rows, w), lambda b, j, *_: (0, 0, 0)),
+                *low_specs,
                 up_spec,
                 up_spec,
             ],
             out_specs=[out_spec, out_spec],
-            scratch_shapes=[pltpu.VMEM((tb, tb), F32)],
         ),
         out_shape=[
             jax.ShapeDtypeStruct((2, blocks, tb, cw), F32),
             jax.ShapeDtypeStruct((2, blocks, tb, cw), BF),
         ],
-        cost_estimate=pl.CostEstimate(
-            flops=4 * blocks * pair * rows * w * cw, transcendentals=0, bytes_accessed=24 * MIB,
-        ),
+        cost_estimate=COST,
         compiler_params=pltpu.CompilerParams(vmem_limit_bytes=24 * MIB),
         name="products",
-    )(place, tiles, low0, low1, up0, up1)
+    )(place, tiles, shared, shared, up0, up1)
 
 
 def final_kernel(place, tiles, *refs, g, c, nt, rt, ct, tb, tj, first, with_lower):
@@ -208,7 +301,7 @@
         ),
         out_shape=out_shape,
         input_output_aliases=aliases,
-        cost_estimate=pl.CostEstimate(flops=8 * tb * w * cw, transcendentals=0, bytes_accessed=40 * tb * cw),
+        cost_estimate=COST,
         compiler_params=pltpu.CompilerParams(vmem_limit_bytes=24 * MIB),
         name="final",
     )(place, tiles, *operands)
@@ -218,6 +311,10 @@
     wanted = (first + jnp.arange(count, dtype=jnp.int32))
     picks = (pivots[..., :, None] == wanted).astype(BF)
     return jnp.einsum("...it,...tj->...ij", inverse, picks, preferred_element_type=F32).astype(BF)
+
+
+def after(value, *earlier):
+    return lax.optimization_barrier((value, *earlier))[0]
 
 
 def paired(
@@ -239,76 +336,210 @@
     tiles = leaf_tiles.reshape(-1)
     top_tiles = anc_tiles.reshape(-1)
     shape = dict(nt=nt, rt=rt, ct=ct, tb=tb)
-
     u = leaf_upper[0]
-    ups = {}
-    for c in range(split):
+    chunks = sorted(((g, c) for c in range(split) for g in range(groups)), key=lambda gc: (gc[0] + 1.5 * gc[1]))
+    parts = [(c, t) for c in range(split) for t in range(2)]
+    v = {}
+    last = [place]
+
+    def ordered(value):
+        return after(value, last[0])
+
+    def done(name, value, token=None):
+        v[name] = value
+        last[0] = value if token is None else token
+
+    def slices(m):
+        c, t = parts[m]
+        src = ordered(u)
+
+        def part(first):
+            return lax.dynamic_slice(src, (first, 0, c * cw), (pair, half, cw))
+
+        to_a = part(jnp.where(is_end, far, near) + t * pair)
+        to_b = part(jnp.where(is_end, near, far) + t * pair)
+        to_a, to_b = lax.optimization_barrier((to_a, to_b))
+        v["a", m] = lax.ppermute(to_a, "col", [(1, 0), (2, 3), (0, 2), (3, 1)])
+        v["b", m] = (to_b, lax.ppermute(to_b, "col", [(1, 2), (2, 1)]))
+        last[0] = to_b
+
+    def lower(first, count):
+        n = count * 4
+        own = step(
+            lower_kernel, "lower", place, [ordered(leaf_lower), leaf_upper_inv], [(pair, n * tb, w)],
+            in_specs=[
+                spec((1, 1, tb, w), lambda k, i, *_: (0, k, first * 4 + i, 0)),
+                spec((1, 1, w, w), lambda k, i, *_: (0, k, 0, 0)),
+            ],
+            out_specs=[spec((1, tb, w), lambda k, i, *_: (k, i, 0))], grid=(pair, n),
+        )
+        done(("lower", first), own)
+
+    def share(first, count):
+        own = v["lower", first]
+        got = lax.all_gather(own, "col", axis_index_groups=[[0, 1], [2, 3]], axis=0, tiled=False)
+        for g in range(first, first + count):
+            v["low", g] = got, g - first
+
+    def stack(m):
+        kept, came = v["b", m]
+        own = step(stack_kernel, "stack", place, [ordered(v["a", m]), kept, came], [(2, pair, half, cw)])
+        done(("own", m), own)
+        v["other", m] = lax.ppermute(own, "row", SWAP)
+
+    def matrices():
         for t in range(2):
-            same, other = (odd ^ t) * pair, ((1 - odd) ^ t) * pair
-
-            def part(first):
-                return lax.dynamic_slice(u, (first, 0, c * cw), (pair, half, cw))
-
-            p1 = lax.ppermute(part(near + other), "col", [(1, 0), (2, 3)])
-            p2 = lax.ppermute(part(far + same), "col", [(0, 2), (3, 1)])
-            p3 = lax.ppermute(part(far + other), "col", [(1, 2), (2, 1)])
-            own = jnp.stack([jnp.where(is_end, part(near + same), p2), jnp.where(is_end, p1, p3)])
-            ups[c, t] = (own, lax.ppermute(own, "row", SWAP))
-
-    lower = jnp.einsum("krw,kwv->krv", leaf_lower[0], leaf_upper_inv[0], preferred_element_type=F32).astype(BF)
-    buddy = [lax.ppermute(lower[:, g * 4 * tb:(g + 1) * 4 * tb], "col", BUDDY) for g in range(groups)]
-
-    uppers = {}
-    mats = []
-    for t in range(2):
-        first = near + (odd ^ t) * pair
-        inverse = lax.dynamic_slice_in_dim(leaf_lower_inv[0], first, pair, 0)
-        pivots = lax.dynamic_slice_in_dim(leaf_pivots[0], first, pair, 0)
-        mats.append((onehot_cols(inverse, pivots, x * half, half), onehot_cols(inverse, pivots, (1 - x) * half, half)))
-    a_own = onehot_cols(anc_lower_inv, anc_pivots, x * half, half)
-    a_other = onehot_cols(anc_lower_inv, anc_pivots, (1 - x) * half, half)
-    for (c, t), (own, other) in ups.items():
-        uppers[c, t] = make_upper(*mats[t], own, other)
-
-    panels, anc_uppers = {}, {}
-    schur, anc_lower = None, None
-    for c in range(split):
-        for g in range(groups):
-            keep, send = products(place, tiles, lower, buddy[g], uppers[c, 0], uppers[c, 1], g=g, c=c, **shape)
-            recv = lax.ppermute(send, "layer", CORE)
-            crossing = (keep[1] + recv[1].astype(F32)).astype(BF)
-            arrived = lax.ppermute(crossing, "layer", YPAIR)
-            mine = (keep[0] + recv[0].astype(F32) + arrived.astype(F32)).astype(BF)
-            outer, inner = mine[0], mine[1]
-            q1 = lax.ppermute(inner, "col", [(0, 1), (3, 2)])
-            q2 = lax.ppermute(outer, "col", [(1, 3), (2, 0)])
-            q3 = lax.ppermute(inner, "col", [(1, 2), (2, 1)])
-            stay = jnp.where(is_end, outer.astype(F32) + q2.astype(F32), q1.astype(F32) + q3.astype(F32))
-            tq = stay.astype(BF)
-            ty = lax.ppermute(tq, "layer", YPAIR)
-            tc = lax.ppermute(jnp.stack([tq, ty]), "layer", CORE)
-            if c == 0:
-                base = lax.dynamic_slice(ancestor, ((g * 4 + l) * tb, 0), (tb, w))
-                pq = dot((base + tq[:, :w].astype(F32)).astype(BF), anc_upper_inv).astype(BF)
-                sent = [lax.ppermute(pq, "col", [(0, n)]) for n in (1, 2, 3)]
-                pq = jnp.where(z == 0, pq, sent[0] + sent[1] + sent[2])
-                py = lax.ppermute(pq, "layer", YPAIR)
-                panels[g] = (pq, py, lax.ppermute(jnp.stack([pq, py]), "layer", CORE))
-            if g == 0:
-                top = jnp.where(l == 0, tq, jnp.where(l == 2, ty, jnp.where(l == 1, tc[0], tc[1])))
-                pivot = (ancestor[:tb, c * cw:(c + 1) * cw] + top.astype(F32)).astype(BF)
-                swapped = lax.ppermute(pivot, "row", SWAP)
-                anc_uppers[c] = (dot(a_own, pivot) + dot(a_other, swapped)).astype(BF)
-            kept = None if schur is None else ((schur, anc_lower) if c == 0 else (schur,))
-            out = final(
-                place, top_tiles, ancestor, (tq, ty, tc), anc_uppers[c], panels[g], kept,
-                g=g, c=c, with_lower=c == 0, **shape,
-            )
-            schur = out[0]
-            if c == 0:
-                anc_lower = out[1]
-    anc_upper = jnp.concatenate([anc_uppers[c] for c in range(split)], axis=1)
-    return anc_lower, anc_upper, schur
+            first = near + t * pair
+            inverse = ordered(lax.dynamic_slice_in_dim(leaf_lower_inv[0], first, pair, 0))
+            pivots = lax.dynamic_slice_in_dim(leaf_pivots[0], first, pair, 0)
+            one = onehot_cols(inverse, pivots, x * half, half)
+            two = onehot_cols(inverse, pivots, (1 - x) * half, half)
+            done(("m", t), (one, two), two)
+        inverse = ordered(anc_lower_inv)
+        one = onehot_cols(inverse, anc_pivots, x * half, half)
+        two = onehot_cols(inverse, anc_pivots, (1 - x) * half, half)
+        done("anc_m", (one, two), two)
+
+    def upper(m):
+        own = ordered(v["own", m])
+        done(("upper",) + parts[m], make_upper(*v["m", parts[m][1]], own, v["other", m]))
+
+    def multiply(n):
+        g, c = chunks[n]
+        keep, send = products(
+            place, tiles, v["low", g], ordered(v["upper", c, 0]), v["upper", c, 1], g=g, c=c, **shape
+        )
+        done(("keep", n), keep, send)
+        v["core", n] = lax.ppermute(send, "layer", CORE)
+
+    def cross(n):
+        crossing = step(
+            cross_kernel, "cross", place, [ordered(v["keep", n]), v["core", n]], [(2, tb, cw)],
+            in_specs=[spec((1, 1, tb, cw), lambda b, *_: (1, b, 0, 0))] * 2,
+            out_specs=[spec((1, tb, cw), lambda b, *_: (b, 0, 0))], grid=(2,),
+        )
+        v["y", n] = lax.ppermute(crossing, "layer", YPAIR)
+        last[0] = crossing
+
+    def spread(n):
+        to_a, to_b = step(
+            spread_kernel, "spread", place, [ordered(v["keep", n]), v["core", n], v["y", n]], [(tb, cw)] * 2,
+            in_specs=[spec((1, 2, tb, cw))] * 2 + [None],
+        )
+        v["qa", n] = lax.ppermute(to_a, "col", [(0, 1), (3, 2), (1, 3), (2, 0)])
+        v["qb", n] = (to_b, lax.ppermute(to_b, "col", [(1, 2), (2, 1)]))
+        last[0] = to_b
+
+    def total(n):
+        kept, came = v["qb", n]
+        tq = step(total_kernel, "total", place, [ordered(v["qa", n]), kept, came], [(tb, cw)])
+        v["ty", n] = lax.ppermute(tq, "layer", YPAIR)
+        done(("tq", n), tq)
+
+    def both(one, two):
+        return step(pair_kernel, "pair", place, [ordered(one), two], [(2,) + one.shape])
+
+    def gather(n):
+        two = both(v["tq", n], v["ty", n])
+        v["tc", n] = lax.ppermute(two, "layer", CORE)
+        last[0] = two
+
+    def panel(n):
+        g, c = chunks[n]
+        pq = step(
+            panel_kernel, "panel", place, [ancestor, ordered(v["tq", n]), anc_upper_inv], [(tb, w)],
+            in_specs=[spec((tb, w), lambda i, p: (g * 4 + p[2], 0)), None, None],
+        )
+        v["p1", g] = (pq, lax.ppermute(pq, "col", [(0, 2)]))
+        last[0] = pq
+
+    def choose(source, own, came):
+        return step(
+            functools.partial(choose_kernel, source=source), "choose", place, [ordered(own), came], [own.shape]
+        )
+
+    def panel_two(n):
+        g, c = chunks[n]
+        pq = choose(4, *v["p1", g])
+        v["p2", g] = (pq, lax.ppermute(pq, "col", [(0, 1), (2, 3)]))
+        last[0] = pq
+
+    def panel_y(n):
+        g, c = chunks[n]
+        pq = choose(2, *v["p2", g])
+        v["py", g] = lax.ppermute(pq, "layer", YPAIR)
+        done(("pq", g), pq)
+
+    def panel_core(n):
+        g, c = chunks[n]
+        two = both(v["pq", g], v["py", g])
+        v["pc", g] = lax.ppermute(two, "layer", CORE)
+        last[0] = two
+
+    def pivot(n):
+        g, c = chunks[n]
+        rows_own = step(
+            pivot_kernel, "pivot", place, [ancestor, ordered(v["tq", n]), v["ty", n], v["tc", n]], [(tb, cw)],
+            in_specs=[spec((tb, cw), lambda *_: (0, c)), None, None, None],
+        )
+        v["pivot", c] = (rows_own, lax.ppermute(rows_own, "row", SWAP))
+        last[0] = rows_own
+
+    def pivot_two(n):
+        g, c = chunks[n]
+        one, two = v["anc_m"]
+        rows_own, rows_other = v["pivot", c]
+        done(("anc_upper", c), step(
+            panel_upper_kernel, "anc_upper", place, [one, two, ordered(rows_own), rows_other], [(w, cw)]
+        ))
+
+    out = {}
+
+    def finish(n):
+        g, c = chunks[n]
+        with_lower = c == 0
+        kept = None if not out else ((out["schur"], out["lower"]) if with_lower else (out["schur"],))
+        made = final(
+            place, top_tiles, ancestor, (ordered(v["tq", n]), v["ty", n], v["tc", n]), v["anc_upper", c],
+            (v["pq", g], v["py", g], v["pc", g]), kept, g=g, c=c, with_lower=with_lower, **shape,
+        )
+        out["schur"] = made[0]
+        if with_lower:
+            out["lower"] = made[1]
+        last[0] = made[0]
+
+    slices(0)
+    lower(0, 1)
+    slices(1)
+    share(0, 1)
+    slices(2)
+    lower(1, groups - 1)
+    slices(3)
+    stack(0)
+    matrices()
+    stack(1)
+    last[0] = after(last[0], v["low", 0][0])
+    v["lower", 1] = after(v["lower", 1], last[0])
+    share(1, groups - 1)
+    upper(0)
+    stack(2)
+    upper(1)
+    work = [(0, 3.5, stack, 3), (1, 1.5, upper, 2), (3, 1.5, upper, 3)]
+    for n, (g, c) in enumerate(chunks):
+        slot = n + GAP * (n > 0)
+        steps = [
+            (0, 0, multiply), (1, 1, spread), (2, 2, total), (0, 3, cross), (3, 4, gather),
+        ]
+        if g == 0:
+            steps += [(3, 6, pivot), (4, 5, pivot_two)]
+        if c == 0:
+            steps += [(2, 2.1, panel), (3, 4.1, panel_two), (4, 4.2, panel_y), (5, 4.3, panel_core)]
+        steps.append((5 if c == 0 else 4, 7, finish))
+        work += [(slot + lag, position, stage, n) for lag, position, stage in steps]
+    for _, _, stage, n in sorted(work, key=lambda e: e[:2]):
+        stage(n)
+    anc_upper = jnp.concatenate([v["anc_upper", c] for c in range(split)], axis=1)
+    return out["lower"], anc_upper, out["schur"]
 
 
 def solution(mesh):

time: 695 us -> 590 us (0.85)
  starting transfers between devices: 155 us -> 66.8 us
  waiting for transfers between devices: 308 us -> 268 us
  other arithmetic: 37 us -> 1.35 us
  local copies, waits for them, and re-layouts: 30.8 us -> 64.2 us
  Pallas kernels: 135 us -> 156 us
  between operations: 2.51 us -> 16.4 us
  matrix products: 19.8 us -> 7.27 us
    ppermute x78 -> x62, starting transfers between devices: 155 us -> 66.7 us  [the longest x3 15.6 us: panel(): v['p1', g] = (pq, lax.ppermute(pq, 'col', [(0, 2)]))]
    pallas_call x0 -> x46, Pallas kernels: none -> 53.8 us  [step(): pl.pallas_call(body, grid_spec=pltpu.PrefetchScalarGridSpec(num_scalar_pr...]
    ppermute x78 -> x62, waiting for transfers between devices: 308 us -> 254 us  [the longest x6 69.5 us: cross(): v['y', n] = lax.ppermute(crossing, 'layer', YPAIR)]
    unnamed x112 -> x256, local copies, waits for them, and re-layouts: 16.8 us -> 51.4 us
    pallas_call x6, Pallas kernels: 90.8 us -> 57.1 us  [products(): pl.pallas_call(functools.partial(product_kernel, g=g, c=c, nt=nt, rt=rt,...]
    convert_element_type x19 -> x0, other arithmetic: 19.4 us -> none  [the longest x6 9.16 us: paired(): crossing = (keep[1] + recv[1].astype(F32)).astype(BF)]
    another operation x18 -> x0, other arithmetic: 14.8 us -> none  [the longest x9 12.2 us: paired(): jnp.stack([jnp.where(is_end, part(near + same), p2), jnp.where(is_end, p1...]
    all_gather x0 -> x2, waiting for transfers between devices: none -> 13.3 us  [share(): lax.all_gather(own, 'col', axis_index_groups=[[0, 1], [2, 3]], axis=0, ti...]
  transfers between devices with their start and end apart: 78 -> 64, of which waited for: 32 -> 25; matrix products, arithmetic and copies ran while one was open for 9% -> 3% of each run, Pallas kernels for 19% -> 16%
where the time goes in v2:
time: 590 us; the launch traced here: 580 us
  waiting for transfers between devices  268 us (45%)
  Pallas kernels  156 us (26%)
  starting transfers between devices  66.8 us (11%)
  local copies, waits for them, and re-layouts  64.2 us (11%)
  between operations  16.4 us (3%)
  matrix products  7.27 us (1%)
    ppermute x6, waiting for transfers between devices, cross(): v['y', n] = lax.ppermute(crossing, 'layer', YPAIR)  69.5 us
    ppermute x4, waiting for transfers between devices, slices(): v['a', m] = lax.ppermute(to_a, 'col', [(1, 0), (2, 3), (0, 2), (3, 1)])  69.1 us
    ppermute x4, waiting for transfers between devices, stack(): v['other', m] = lax.ppermute(own, 'row', SWAP)  57.8 us
    pallas_call x6, Pallas kernels, products(): pl.pallas_call(functools.partial(product_kernel, g=g, c=c, nt=nt, rt=rt,...  57.1 us
    pallas_call x46, Pallas kernels, step(): pl.pallas_call(body, grid_spec=pltpu.PrefetchScalarGridSpec(num_scalar_pr...  53.8 us
    unnamed x256, local copies, waits for them, and re-layouts  51.4 us
    pallas_call x6, Pallas kernels, final(): pl.pallas_call(functools.partial(final_kernel, g=g, c=c, nt=nt, rt=rt, ct...  31.3 us
    ppermute x3, starting transfers between devices, panel(): v['p1', g] = (pq, lax.ppermute(pq, 'col', [(0, 2)]))  15.6 us
  transfers between devices with their start and end apart: 64, of which 25 were waited for; matrix products, arithmetic and copies ran while one was open for 3% of the time, Pallas kernels for 16%

profile of v2, /device:TPU:0, one launch (start us, length us, event | category | flops | bytes accessed | tf_op | source)
XLA Modules:
  0.0 579.5 jit_solution(5211017194640071238)
XLA Ops:
  10.1 2.8 copy-done.21
  12.9 4.9 lower.2
  19.5 4.8 collective-permute-start.1
  24.3 2.8 constant_dynamic-slice_fusion.4
  29.5 2.8 constant_dynamic-slice_fusion.2
  32.3 5.5 lower.3
  44.2 10.8 %collective-permute-done.1.first = bf16[2,256,768]{2,1,0:T(8,128)(2,1)} collective-permute-done((bf16[2,256,768]{2,1,0:T(8,128)(2,1)}, bf16[2,256,768]{2,1,0:T(8,128)(2,1)}, u32[]{:S(2)}, u32[]{:S(2)}) %collective-permute-start.1) | collective-permute-done | bytes 786464 | tf_op jit(solution)/shard_map/ppermute | solution.py:362
  60.4 26.9 %collective-permute-done.first = bf16[2,256,768]{2,1,0:T(8,128)(2,1)} collective-permute-done((bf16[2,256,768]{2,1,0:T(8,128)(2,1)}, bf16[2,256,768]{2,1,0:T(8,128)(2,1)}, u32[]{:S(2)}, u32[]{:S(2)}) %collective-permute-start) | collective-permute-done | bytes 786464 | tf_op jit(solution)/shard_map/ppermute | solution.py:362
  90.7 13.3 %all-gather.5.cloned.1.call-done = bf16[4,1024,512]{2,1,0:T(8,128)(2,1)} async-done(((bf16[2,1024,512]{2,1,0:T(8,128)(2,1)}), bf16[4,1024,512]{2,1,0:T(8,128)(2,1)}) %all-gather.5.cloned.1.call-update) | async-done | bytes 4194320 | tf_op jit(solution)/shard_map/all_gather | solution.py:380
  114.3 27.1 %collective-permute-done.4.st_ref = bf16[2,2,256,768]{3,2,1,0:T(8,128)(2,1)} collective-permute-done((bf16[2,2,256,768]{3,2,1,0:T(8,128)(2,1)S(1)}, bf16[2,2,256,768]{3,2,1,0:T(8,128)(2,1)}, u32[]{:S(2)}, u32[]{:S(2)}) %collective-permute-start.4) | collective-permute-done | bytes 1572896 | tf_op jit(solution)/shard_map/ppermute | solution.py:388
  141.4 3.8 upper.4.up0
  145.3 3.0 stack.22.so_ref
  148.3 25.9 %collective-permute-done.7.st_ref = bf16[2,2,256,768]{3,2,1,0:T(8,128)(2,1)} collective-permute-done((bf16[2,2,256,768]{3,2,1,0:T(8,128)(2,1)}, bf16[2,2,256,768]{3,2,1,0:T(8,128)(2,1)}, u32[]{:S(2)}, u32[]{:S(2)}) %collective-permute-start.7) | collective-permute-done | bytes 1572896 | tf_op jit(solution)/shard_map/ppermute | solution.py:388
  174.2 3.8 upper.5.up1
  178.1 9.2 %products.6 = (f32[2,2,256,768]{3,2,1,0:T(8,128)S(1)}, bf16[2,2,256,768]{3,2,1,0:T(8,128)(2,1)S(1)}) custom-call(s32[3]{0:T(128)S(1)} %pad_add_fusion.place, s32[4608]{0:T(1024)S(1)} %reshape.38.tiles, bf16[2,2,1024,512]{3,2,1,0:T(8,128)(2,1)S(1)} %bitcast.38, bf16[2,2,1024,512]{3,2,1,0:T(8,128)(2,1)S(1)} %bitcast.39, ...), custom_call_target="tpu_custom_call" | custom-call | flops 1 | bytes 1 | tf_op jit(solution)/shard_map/products/pallas_call | solution.py:210
  194.7 31.4 %collective-permute-done.8.first = bf16[2,256,768]{2,1,0:T(8,128)(2,1)S(1)} collective-permute-done((bf16[2,256,768]{2,1,0:T(8,128)(2,1)S(1)}, bf16[2,256,768]{2,1,0:T(8,128)(2,1)S(1)}, u32[]{:S(2)}, u32[]{:S(2)}) %collective-permute-start.8) | collective-permute-done | bytes 786464 | tf_op jit(solution)/shard_map/ppermute | solution.py:362
  235.6 5.6 collective-permute-done.12.arrived
  243.5 3.4 copy-done.3
  250.7 9.5 %products.7 = (f32[2,2,256,768]{3,2,1,0:T(8,128)S(1)}, bf16[2,2,256,768]{3,2,1,0:T(8,128)(2,1)S(1)}) custom-call(s32[3]{0:T(128)S(1)} %pad_add_fusion.place, s32[4608]{0:T(1024)S(1)} %reshape.38.tiles, bf16[2,2,2048,512]{3,2,1,0:T(8,128)(2,1)S(1)} %bitcast.30, bf16[2,2,2048,512]{3,2,1,0:T(8,128)(2,1)S(1)} %bitcast.31, ...), custom_call_target="tpu_custom_call" | custom-call | flops 1 | bytes 1 | tf_op jit(solution)/shard_map/products/pallas_call | solution.py:210
  261.8 4.9 collective-permute-done.15.st_ref
  266.6 3.8 upper.7.up1
  272.8 9.3 %collective-permute-start.18 = (bf16[256,512]{1,0:T(8,128)(2,1)S(1)}, bf16[256,512]{1,0:T(8,128)(2,1)S(1)}, u32[]{:S(2)}, u32[]{:S(2)}) collective-permute-start(bf16[256,512]{1,0:T(8,128)(2,1)S(1)} %copy-done.79), channel_id=1, source_target_pairs={{0,2},{4,6},{8,10},{12,14},{16,18},{20,22},{24,26},{28,30}} | collective-permute-start | bytes 786440 | tf_op jit(solution)/shard_map/ppermute | solution.py:453
  282.1 6.2 %collective-permute-done.18.came = bf16[256,512]{1,0:T(8,128)(2,1)S(1)} collective-permute-done((bf16[256,512]{1,0:T(8,128)(2,1)S(1)}, bf16[256,512]{1,0:T(8,128)(2,1)S(1)}, u32[]{:S(2)}, u32[]{:S(2)}) %collective-permute-start.18) | collective-permute-done | bytes 262176 | tf_op jit(solution)/shard_map/ppermute | solution.py:453
  292.4 9.8 %products.8 = (f32[2,2,256,768]{3,2,1,0:T(8,128)S(1)}, bf16[2,2,256,768]{3,2,1,0:T(8,128)(2,1)}) custom-call(s32[3]{0:T(128)S(1)} %pad_add_fusion.place, s32[4608]{0:T(1024)S(1)} %reshape.38.tiles, bf16[2,2,1024,512]{3,2,1,0:T(8,128)(2,1)S(1)} %bitcast.40, bf16[2,2,1024,512]{3,2,1,0:T(8,128)(2,1)S(1)} %bitcast.41, bf16[2,2,512,768]{3,2,1,0:T(8,128)(2,1)S(1)} %copy-done.9, ...), custom_call_target="tpu_custom_call" | custom-call | flops 1 | bytes 1 | tf_op jit(solution)/shard_map/products/pallas_call | solution.py:210
  306.1 16.3 %collective-permute-done.20.came = bf16[2,256,768]{2,1,0:T(8,128)(2,1)S(1)} collective-permute-done((bf16[2,256,768]{2,1,0:T(8,128)(2,1)}, bf16[2,256,768]{2,1,0:T(8,128)(2,1)S(1)}, u32[]{:S(2)}, u32[]{:S(2)}) %collective-permute-start.20) | collective-permute-done | bytes 786464 | tf_op jit(solution)/shard_map/ppermute | solution.py:421
  327.5 3.4 copy-done.4
  330.9 9.5 %products.9 = (f32[2,2,256,768]{3,2,1,0:T(8,128)S(1)}, bf16[2,2,256,768]{3,2,1,0:T(8,128)(2,1)S(1)}) custom-call(s32[3]{0:T(128)S(1)} %pad_add_fusion.place, s32[4608]{0:T(1024)S(1)} %reshape.38.tiles, bf16[2,2,2048,512]{3,2,1,0:T(8,128)(2,1)S(1)} %bitcast.32, bf16[2,2,2048,512]{3,2,1,0:T(8,128)(2,1)S(1)} %bitcast.33, ...), custom_call_target="tpu_custom_call" | custom-call | flops 1 | bytes 1 | tf_op jit(solution)/shard_map/products/pallas_call | solution.py:210
  344.4 17.8 %collective-permute-done.25.came = bf16[2,256,768]{2,1,0:T(8,128)(2,1)S(1)} collective-permute-done((bf16[2,256,768]{2,1,0:T(8,128)(2,1)}, bf16[2,256,768]{2,1,0:T(8,128)(2,1)S(1)}, u32[]{:S(2)}, u32[]{:S(2)}) %collective-permute-start.25) | collective-permute-done | bytes 786464 | tf_op jit(solution)/shard_map/ppermute | solution.py:421
  375.0 6.4 %copy-done.2 = f32[3072,1536]{1,0:T(8,128)S(1)} copy-done((f32[3072,1536]{1,0:T(8,128)S(1)}, f32[3072,1536]{1,0:T(8,128)}, u32[]{:S(2)}) %copy-start.2) | copy-done | bytes 18874392
  382.3 5.9 %final.6 = (f32[3072,1536]{1,0:T(8,128)}, bf16[3072,512]{1,0:T(8,128)(2,1)}) custom-call(s32[3]{0:T(128)S(1)} %pad_add_fusion.place, s32[576]{0:T(1024)S(1)} %reshape.37.tiles, f32[3072,1536]{1,0:T(8,128)S(1)} %copy-done.2, bf16[256,768]{1,0:T(8,128)(2,1)S(1)} %total.6.tq.one.refs_1_, bf16[256,768]{1,0:T(8,128)(2,1)S(1)} %copy-done.46, ...), custom_call_target="tpu_custom_call" | custom-call | flops 1 | bytes 1 | tf_op jit(solution)/shard_map/final/pallas_call | solution.py:295
  388.3 3.4 copy-done.5
  391.7 9.5 %products.10 = (f32[2,2,256,768]{3,2,1,0:T(8,128)S(1)}, bf16[2,2,256,768]{3,2,1,0:T(8,128)(2,1)S(1)}) custom-call(s32[3]{0:T(128)S(1)} %pad_add_fusion.place, s32[4608]{0:T(1024)S(1)} %reshape.38.tiles, bf16[2,2,2048,512]{3,2,1,0:T(8,128)(2,1)S(1)} %bitcast.34, bf16[2,2,2048,512]{3,2,1,0:T(8,128)(2,1)S(1)} %bitcast.35, ...), custom_call_target="tpu_custom_call" | custom-call | flops 1 | bytes 1 | tf_op jit(solution)/shard_map/products/pallas_call | solution.py:210
  404.5 17.6 %collective-permute-done.30.came = bf16[2,256,768]{2,1,0:T(8,128)(2,1)S(1)} collective-permute-done((bf16[2,256,768]{2,1,0:T(8,128)(2,1)S(1)}, bf16[2,256,768]{2,1,0:T(8,128)(2,1)S(1)}, u32[]{:S(2)}, u32[]{:S(2)}) %collective-permute-start.30) | collective-permute-done | bytes 786464 | tf_op jit(solution)/shard_map/ppermute | solution.py:421
  422.1 4.5 collective-permute-start.36
  432.8 9.5 %products.11 = (f32[2,2,256,768]{3,2,1,0:T(8,128)S(1)}, bf16[2,2,256,768]{3,2,1,0:T(8,128)(2,1)S(1)}) custom-call(s32[3]{0:T(128)S(1)} %pad_add_fusion.place, s32[4608]{0:T(1024)S(1)} %reshape.38.tiles, bf16[2,2,2048,512]{3,2,1,0:T(8,128)(2,1)S(1)} %bitcast.36, bf16[2,2,2048,512]{3,2,1,0:T(8,128)(2,1)S(1)} %bitcast.37, ...), custom_call_target="tpu_custom_call" | custom-call | flops 1 | bytes 1 | tf_op jit(solution)/shard_map/products/pallas_call | solution.py:210
  446.3 17.8 %collective-permute-done.37.came = bf16[2,256,768]{2,1,0:T(8,128)(2,1)S(1)} collective-permute-done((bf16[2,256,768]{2,1,0:T(8,128)(2,1)}, bf16[2,256,768]{2,1,0:T(8,128)(2,1)S(1)}, u32[]{:S(2)}, u32[]{:S(2)}) %collective-permute-start.37) | collective-permute-done | bytes 786464 | tf_op jit(solution)/shard_map/ppermute | solution.py:421
  476.5 5.8 %collective-permute-done.42.came = bf16[256,512]{1,0:T(8,128)(2,1)S(1)} collective-permute-done((bf16[256,512]{1,0:T(8,128)(2,1)S(1)}, bf16[256,512]{1,0:T(8,128)(2,1)S(1)}, u32[]{:S(2)}, u32[]{:S(2)}) %collective-permute-start.42) | collective-permute-done | bytes 262176 | tf_op jit(solution)/shard_map/ppermute | solution.py:464
  482.7 7.6 %collective-permute-done.39.arrived = bf16[256,768]{1,0:T(8,128)(2,1)S(1)} collective-permute-done((bf16[256,768]{1,0:T(8,128)(2,1)S(1)}, bf16[256,768]{1,0:T(8,128)(2,1)S(1)}, u32[]{:S(2)}, u32[]{:S(2)}) %collective-permute-start.39) | collective-permute-done | bytes 393248 | tf_op jit(solution)/shard_map/ppermute | solution.py:429
  495.3 6.3 %collective-permute-done.46.two.refs_2_ = bf16[256,768]{1,0:T(8,128)(2,1)S(1)} collective-permute-done((bf16[256,768]{1,0:T(8,128)(2,1)S(1)}, bf16[256,768]{1,0:T(8,128)(2,1)S(1)}, u32[]{:S(2)}, u32[]{:S(2)}) %collective-permute-start.46) | collective-permute-done | bytes 393248 | tf_op jit(solution)/shard_map/ppermute | solution.py:436
  502.8 4.0 collective-permute-done.49.two.refs_6_
  509.0 9.9 %collective-permute-done.50.other = bf16[256,768]{1,0:T(8,128)(2,1)S(1)} collective-permute-done((bf16[256,768]{1,0:T(8,128)(2,1)S(1)}, bf16[256,768]{1,0:T(8,128)(2,1)S(1)}, u32[]{:S(2)}, u32[]{:S(2)}) %collective-permute-start.50) | collective-permute-done | bytes 393248 | tf_op jit(solution)/shard_map/ppermute | solution.py:485
  521.8 4.6 final.7
  526.4 5.1 final.8.refs_8_
  535.3 3.7 collective-permute-done.55.came
  544.8 3.0 collective-permute-done.57.two.refs_6_
  550.4 4.0 final.9
  556.3 6.2 %final.10.refs_8_ = f32[3072,1536]{1,0:T(8,128)} custom-call(s32[3]{0:T(128)S(1)} %pad_add_fusion.place, s32[576]{0:T(1024)S(1)} %reshape.37.tiles, f32[3072,1536]{1,0:T(8,128)S(1)} %bitcast.27, bf16[256,768]{1,0:T(8,128)(2,1)S(1)} %total.10.one.refs_1_, bf16[256,768]{1,0:T(8,128)(2,1)S(1)} %copy-done.71, ...), custom_call_target="tpu_custom_call", output_to_operand_aliasing={{}: (10, {})} | custom-call | flops 1 | bytes 1 | tf_op jit(solution)/shard_map/final/pallas_call | solution.py:295
  566.7 5.5 final.11
  (422 shorter events, 144.8 us)
Async XLA Ops:
  7.2 96.8 %all-gather.5.cloned.1.call-start = ((), (), s32[]{:S(2)}) async-start(), calls=%async_computation | async-start | bytes 6291456 | tf_op jit(solution)/shard_map/all_gather | solution.py:380
  17.8 225.6 %all-gather.7.cloned.1.call-start = ((), (), s32[]{:S(2)}) async-start(), calls=%async_computation.1 | async-start | bytes 12582912 | tf_op jit(solution)/shard_map/all_gather | solution.py:380
  17.9 37.1 %collective-permute-start.2 = (bf16[2,256,768]{2,1,0:T(8,128)(2,1)}, bf16[2,256,768]{2,1,0:T(8,128)(2,1)}, u32[]{:S(2)}, u32[]{:S(2)}) collective-permute-start(bf16[2,256,768]{2,1,0:T(8,128)(2,1)} %get-tuple-element.113.kept), channel_id=1, source_target_pairs={{1,2},{2,1},{5,6},{6,5},{9,10},{10,9},{13,14},{14,13},{17,18},{18,... | collective-permute-start | bytes 2359304 | tf_op jit(solution)/shard_map/ppermute | solution.py:363
  19.5 35.4 %collective-permute-start.1 = (bf16[2,256,768]{2,1,0:T(8,128)(2,1)}, bf16[2,256,768]{2,1,0:T(8,128)(2,1)}, u32[]{:S(2)}, u32[]{:S(2)}) collective-permute-start(bf16[2,256,768]{2,1,0:T(8,128)(2,1)} %get-tuple-element.121), channel_id=1, source_target_pairs={{1,0},{2,3},{0,2},{3,1},{5,4},{6,7},{4,6},{7,5},{9,8},{10,11},{8,1... | collective-permute-start | bytes 2359304 | tf_op jit(solution)/shard_map/ppermute | solution.py:362
  27.1 60.1 %collective-permute-start = (bf16[2,256,768]{2,1,0:T(8,128)(2,1)}, bf16[2,256,768]{2,1,0:T(8,128)(2,1)}, u32[]{:S(2)}, u32[]{:S(2)}) collective-permute-start(bf16[2,256,768]{2,1,0:T(8,128)(2,1)} %get-tuple-element.120), channel_id=1, source_target_pairs={{1,0},{2,3},{0,2},{3,1},{5,4},{6,7},{4,6},{7,5},{9,8},{10,11},{8,1... | collective-permute-start | bytes 2359304 | tf_op jit(solution)/shard_map/ppermute | solution.py:362
  27.9 59.3 %collective-permute-start.3 = (bf16[2,256,768]{2,1,0:T(8,128)(2,1)}, bf16[2,256,768]{2,1,0:T(8,128)(2,1)}, u32[]{:S(2)}, u32[]{:S(2)}) collective-permute-start(bf16[2,256,768]{2,1,0:T(8,128)(2,1)} %get-tuple-element.116.kept), channel_id=1, source_target_pairs={{1,2},{2,1},{5,6},{6,5},{9,10},{10,9},{13,14},{14,13},{17,18},{18,... | collective-permute-start | bytes 2359304 | tf_op jit(solution)/shard_map/ppermute | solution.py:363
  104.0 37.4 %collective-permute-start.4 = (bf16[2,2,256,768]{3,2,1,0:T(8,128)(2,1)S(1)}, bf16[2,2,256,768]{3,2,1,0:T(8,128)(2,1)}, u32[]{:S(2)}, u32[]{:S(2)}) collective-permute-start(bf16[2,2,256,768]{3,2,1,0:T(8,128)(2,1)S(1)} %stack.20.so_ref), channel_id=1, source_target_pairs={{0,4},{4,0},{1,5},{5,1},{2,6},{6,2},{3,7},{7,3},{8,12},{12,8},{9,1... | collective-permute-start | bytes 4718600 | tf_op jit(solution)/shard_map/ppermute | solution.py:388
  105.5 68.7 %collective-permute-start.7 = (bf16[2,2,256,768]{3,2,1,0:T(8,128)(2,1)}, bf16[2,2,256,768]{3,2,1,0:T(8,128)(2,1)}, u32[]{:S(2)}, u32[]{:S(2)}) collective-permute-start(bf16[2,2,256,768]{3,2,1,0:T(8,128)(2,1)} %copy-done.35), channel_id=1, source_target_pairs={{0,4},{4,0},{1,5},{5,1},{2,6},{6,2},{3,7},{7,3},{8,12},{12,8},{9,1... | collective-permute-start | bytes 4718600 | tf_op jit(solution)/shard_map/ppermute | solution.py:388
  106.1 39.2 %collective-permute-start.5 = (bf16[2,256,768]{2,1,0:T(8,128)(2,1)}, bf16[2,256,768]{2,1,0:T(8,128)(2,1)}, u32[]{:S(2)}, u32[]{:S(2)}) collective-permute-start(bf16[2,256,768]{2,1,0:T(8,128)(2,1)} %get-tuple-element.132), channel_id=1, source_target_pairs={{1,0},{2,3},{0,2},{3,1},{5,4},{6,7},{4,6},{7,5},{9,8},{10,11},{8,1... | collective-permute-start | bytes 2359304 | tf_op jit(solution)/shard_map/ppermute | solution.py:362
  108.8 36.5 %collective-permute-start.6 = (bf16[2,256,768]{2,1,0:T(8,128)(2,1)}, bf16[2,256,768]{2,1,0:T(8,128)(2,1)}, u32[]{:S(2)}, u32[]{:S(2)}) collective-permute-start(bf16[2,256,768]{2,1,0:T(8,128)(2,1)} %get-tuple-element.118.kept), channel_id=1, source_target_pairs={{1,2},{2,1},{5,6},{6,5},{9,10},{10,9},{13,14},{14,13},{17,18},{18,... | collective-permute-start | bytes 2359304 | tf_op jit(solution)/shard_map/ppermute | solution.py:363
  187.4 44.2 %collective-permute-start.13 = (bf16[2,2,256,768]{3,2,1,0:T(8,128)(2,1)S(1)}, bf16[2,2,256,768]{3,2,1,0:T(8,128)(2,1)S(1)}, u32[]{:S(2)}, u32[]{:S(2)}) collective-permute-start(bf16[2,2,256,768]{3,2,1,0:T(8,128)(2,1)S(1)} %stack.22.so_ref), channel_id=1, source_target_pairs={{0,4},{4,0},{1,5},{5,1},{2,6},{6,2},{3,7},{7,3},{8,12},{12,8},{9,1... | collective-permute-start | bytes 4718600 | tf_op jit(solution)/shard_map/ppermute | solution.py:388
  189.0 37.2 %collective-permute-start.8 = (bf16[2,256,768]{2,1,0:T(8,128)(2,1)S(1)}, bf16[2,256,768]{2,1,0:T(8,128)(2,1)S(1)}, u32[]{:S(2)}, u32[]{:S(2)}) collective-permute-start(bf16[2,256,768]{2,1,0:T(8,128)(2,1)S(1)} %copy-done.103), channel_id=1, source_target_pairs={{1,0},{2,3},{0,2},{3,1},{5,4},{6,7},{4,6},{7,5},{9,8},{10,11},{8,1... | collective-permute-start | bytes 2359304 | tf_op jit(solution)/shard_map/ppermute | solution.py:362
  191.7 34.5 %collective-permute-start.10 = (bf16[2,256,768]{2,1,0:T(8,128)(2,1)S(1)}, bf16[2,256,768]{2,1,0:T(8,128)(2,1)S(1)}, u32[]{:S(2)}, u32[]{:S(2)}) collective-permute-start(bf16[2,256,768]{2,1,0:T(8,128)(2,1)S(1)} %get-tuple-element.123.kept), channel_id=1, source_target_pairs={{1,2},{2,1},{5,6},{6,5},{9,10},{10,9},{13,14},{14,13},{17,18},{18,... | collective-permute-start | bytes 2359304 | tf_op jit(solution)/shard_map/ppermute | solution.py:363
  193.2 33.7 %collective-permute-start.11 = (bf16[2,256,768]{2,1,0:T(8,128)(2,1)S(1)}, bf16[2,256,768]{2,1,0:T(8,128)(2,1)S(1)}, u32[]{:S(2)}, u32[]{:S(2)}) collective-permute-start(bf16[2,256,768]{2,1,0:T(8,128)(2,1)S(1)} %cross.6), channel_id=1, source_target_pairs={{0,16},{16,0},{8,24},{24,8},{1,17},{17,1},{9,25},{25,9},{2,18},{18... | collective-permute-start | bytes 2359304 | tf_op jit(solution)/shard_map/ppermute | solution.py:421
  231.0 35.7 %collective-permute-start.15 = (bf16[2,2,256,768]{3,2,1,0:T(8,128)(2,1)S(1)}, bf16[2,2,256,768]{3,2,1,0:T(8,128)(2,1)}, u32[]{:S(2)}, u32[]{:S(2)}) collective-permute-start(bf16[2,2,256,768]{3,2,1,0:T(8,128)(2,1)S(1)} %stack.23.so_ref), channel_id=1, source_target_pairs={{0,4},{4,0},{1,5},{5,1},{2,6},{6,2},{3,7},{7,3},{8,12},{12,8},{9,1... | collective-permute-start | bytes 4718600 | tf_op jit(solution)/shard_map/ppermute | solution.py:388
  272.7 16.2 %collective-permute-start.19 = (bf16[2,256,768]{2,1,0:T(8,128)(2,1)S(1)}, bf16[2,256,768]{2,1,0:T(8,128)(2,1)S(1)}, u32[]{:S(2)}, u32[]{:S(2)}) collective-permute-start(bf16[2,256,768]{2,1,0:T(8,128)(2,1)S(1)} %pair.9), channel_id=1, source_target_pairs={{0,8},{8,0},{16,24},{24,16},{1,9},{9,1},{17,25},{25,17},{2,10},{10... | collective-permute-start | bytes 2359304 | tf_op jit(solution)/shard_map/ppermute | solution.py:444
  272.8 15.5 %collective-permute-start.18 = (bf16[256,512]{1,0:T(8,128)(2,1)S(1)}, bf16[256,512]{1,0:T(8,128)(2,1)S(1)}, u32[]{:S(2)}, u32[]{:S(2)}) collective-permute-start(bf16[256,512]{1,0:T(8,128)(2,1)S(1)} %copy-done.79), channel_id=1, source_target_pairs={{0,2},{4,6},{8,10},{12,14},{16,18},{20,22},{24,26},{28,30}} | collective-permute-start | bytes 786440 | tf_op jit(solution)/shard_map/ppermute | solution.py:453
  302.2 21.8 %collective-permute-start.21 = (bf16[2,2,256,768]{3,2,1,0:T(8,128)(2,1)}, bf16[2,2,256,768]{3,2,1,0:T(8,128)(2,1)S(1)}, u32[]{:S(2)}, u32[]{:S(2)}) collective-permute-start(bf16[2,2,256,768]{3,2,1,0:T(8,128)(2,1)} %get-tuple-element.156), channel_id=1, source_target_pairs={{0,8},{8,0},{16,24},{24,16},{1,9},{9,1},{17,25},{25,17},{2,10},{10... | collective-permute-start | bytes 4718600 | tf_op jit(solution)/shard_map/ppermute | solution.py:413
  302.2 20.2 %collective-permute-start.20 = (bf16[2,256,768]{2,1,0:T(8,128)(2,1)}, bf16[2,256,768]{2,1,0:T(8,128)(2,1)S(1)}, u32[]{:S(2)}, u32[]{:S(2)}) collective-permute-start(bf16[2,256,768]{2,1,0:T(8,128)(2,1)} %copy-done.88), channel_id=1, source_target_pairs={{0,16},{16,0},{8,24},{24,8},{1,17},{17,1},{9,25},{25,9},{2,18},{18... | collective-permute-start | bytes 2359304 | tf_op jit(solution)/shard_map/ppermute | solution.py:421
  303.8 22.5 %collective-permute-start.23 = (bf16[256,768]{1,0:T(8,128)(2,1)}, bf16[256,768]{1,0:T(8,128)(2,1)S(1)}, u32[]{:S(2)}, u32[]{:S(2)}) collective-permute-start(bf16[256,768]{1,0:T(8,128)(2,1)} %copy-done.74), channel_id=1, source_target_pairs={{0,4},{4,0},{1,5},{5,1},{2,6},{6,2},{3,7},{7,3},{8,12},{12,8},{9,1... | collective-permute-start | bytes 1179656 | tf_op jit(solution)/shard_map/ppermute | solution.py:485
  304.3 20.5 %collective-permute-start.22 = (bf16[256,512]{1,0:T(8,128)(2,1)}, bf16[256,512]{1,0:T(8,128)(2,1)S(1)}, u32[]{:S(2)}, u32[]{:S(2)}) collective-permute-start(bf16[256,512]{1,0:T(8,128)(2,1)} %copy-done.84), channel_id=1, source_target_pairs={{0,1},{2,3},{4,5},{6,7},{8,9},{10,11},{12,13},{14,15},{16,17},{18,... | collective-permute-start | bytes 786440 | tf_op jit(solution)/shard_map/ppermute | solution.py:464
  341.6 26.6 %collective-permute-start.27 = (bf16[2,2,256,768]{3,2,1,0:T(8,128)(2,1)}, bf16[2,2,256,768]{3,2,1,0:T(8,128)(2,1)S(1)}, u32[]{:S(2)}, u32[]{:S(2)}) collective-permute-start(bf16[2,2,256,768]{3,2,1,0:T(8,128)(2,1)} %copy-done.98), channel_id=1, source_target_pairs={{0,8},{8,0},{16,24},{24,16},{1,9},{9,1},{17,25},{25,17},{2,10},{10... | collective-permute-start | bytes 4718600 | tf_op jit(solution)/shard_map/ppermute | solution.py:413
  341.6 20.5 %collective-permute-start.25 = (bf16[2,256,768]{2,1,0:T(8,128)(2,1)}, bf16[2,256,768]{2,1,0:T(8,128)(2,1)S(1)}, u32[]{:S(2)}, u32[]{:S(2)}) collective-permute-start(bf16[2,256,768]{2,1,0:T(8,128)(2,1)} %copy-done.91), channel_id=1, source_target_pairs={{0,16},{16,0},{8,24},{24,8},{1,17},{17,1},{9,25},{25,9},{2,18},{18... | collective-permute-start | bytes 2359304 | tf_op jit(solution)/shard_map/ppermute | solution.py:421
  343.0 22.6 %collective-permute-start.24 = (bf16[256,768]{1,0:T(8,128)(2,1)}, bf16[256,768]{1,0:T(8,128)(2,1)S(1)}, u32[]{:S(2)}, u32[]{:S(2)}) collective-permute-start(bf16[256,768]{1,0:T(8,128)(2,1)} %get-tuple-element.164), channel_id=1, source_target_pairs={{0,1},{3,2},{1,3},{2,0},{4,5},{7,6},{5,7},{6,4},{8,9},{11,10},{9,1... | collective-permute-start | bytes 1179656 | tf_op jit(solution)/shard_map/ppermute | solution.py:429
  343.0 22.6 %collective-permute-start.26 = (bf16[256,768]{1,0:T(8,128)(2,1)}, bf16[256,768]{1,0:T(8,128)(2,1)S(1)}, u32[]{:S(2)}, u32[]{:S(2)}) collective-permute-start(bf16[256,768]{1,0:T(8,128)(2,1)} %get-tuple-element.158.kept), channel_id=1, source_target_pairs={{1,2},{2,1},{5,6},{6,5},{9,10},{10,9},{13,14},{14,13},{17,18},{18,... | collective-permute-start | bytes 1179656 | tf_op jit(solution)/shard_map/ppermute | solution.py:430
  343.7 26.1 %collective-permute-start.28 = (bf16[256,512]{1,0:T(8,128)(2,1)}, bf16[256,512]{1,0:T(8,128)(2,1)S(1)}, u32[]{:S(2)}, u32[]{:S(2)}) collective-permute-start(bf16[256,512]{1,0:T(8,128)(2,1)} %choose.7.one.refs_5_), channel_id=1, source_target_pairs={{0,16},{16,0},{8,24},{24,8},{1,17},{17,1},{9,25},{25,9},{2,18},{18... | collective-permute-start | bytes 786440 | tf_op jit(solution)/shard_map/ppermute | solution.py:470
  401.2 27.6 %collective-permute-start.34 = (bf16[2,2,256,768]{3,2,1,0:T(8,128)(2,1)S(1)}, bf16[2,2,256,768]{3,2,1,0:T(8,128)(2,1)S(1)}, u32[]{:S(2)}, u32[]{:S(2)}) collective-permute-start(bf16[2,2,256,768]{3,2,1,0:T(8,128)(2,1)S(1)} %get-tuple-element.175), channel_id=1, source_target_pairs={{0,8},{8,0},{16,24},{24,16},{1,9},{9,1},{17,25},{25,17},{2,10},{10... | collective-permute-start | bytes 4718600 | tf_op jit(solution)/shard_map/ppermute | solution.py:413
  401.7 20.4 %collective-permute-start.30 = (bf16[2,256,768]{2,1,0:T(8,128)(2,1)S(1)}, bf16[2,256,768]{2,1,0:T(8,128)(2,1)S(1)}, u32[]{:S(2)}, u32[]{:S(2)}) collective-permute-start(bf16[2,256,768]{2,1,0:T(8,128)(2,1)S(1)} %copy-done.90), channel_id=1, source_target_pairs={{0,16},{16,0},{8,24},{24,8},{1,17},{17,1},{9,25},{25,9},{2,18},{18... | collective-permute-start | bytes 2359304 | tf_op jit(solution)/shard_map/ppermute | solution.py:421
  403.1 25.0 %collective-permute-start.32 = (bf16[256,768]{1,0:T(8,128)(2,1)S(1)}, bf16[256,768]{1,0:T(8,128)(2,1)S(1)}, u32[]{:S(2)}, u32[]{:S(2)}) collective-permute-start(bf16[256,768]{1,0:T(8,128)(2,1)S(1)} %copy-done.100), channel_id=1, source_target_pairs={{0,1},{3,2},{1,3},{2,0},{4,5},{7,6},{5,7},{6,4},{8,9},{11,10},{9,1... | collective-permute-start | bytes 1179656 | tf_op jit(solution)/shard_map/ppermute | solution.py:429
  403.1 25.0 %collective-permute-start.33 = (bf16[256,768]{1,0:T(8,128)(2,1)S(1)}, bf16[256,768]{1,0:T(8,128)(2,1)S(1)}, u32[]{:S(2)}, u32[]{:S(2)}) collective-permute-start(bf16[256,768]{1,0:T(8,128)(2,1)S(1)} %copy-done.94), channel_id=1, source_target_pairs={{1,2},{2,1},{5,6},{6,5},{9,10},{10,9},{13,14},{14,13},{17,18},{18,... | collective-permute-start | bytes 1179656 | tf_op jit(solution)/shard_map/ppermute | solution.py:430
  403.8 26.3 %collective-permute-start.35 = (bf16[256,768]{1,0:T(8,128)(2,1)S(1)}, bf16[256,768]{1,0:T(8,128)(2,1)S(1)}, u32[]{:S(2)}, u32[]{:S(2)}) collective-permute-start(bf16[256,768]{1,0:T(8,128)(2,1)S(1)} %total.7.tq.one.refs_1_), channel_id=1, source_target_pairs={{0,16},{16,0},{8,24},{24,8},{1,17},{17,1},{9,25},{25,9},{2,18},{18... | collective-permute-start | bytes 1179656 | tf_op jit(solution)/shard_map/ppermute | solution.py:436
  443.5 26.4 %collective-permute-start.40 = (bf16[2,2,256,768]{3,2,1,0:T(8,128)(2,1)}, bf16[2,2,256,768]{3,2,1,0:T(8,128)(2,1)S(1)}, u32[]{:S(2)}, u32[]{:S(2)}) collective-permute-start(bf16[2,2,256,768]{3,2,1,0:T(8,128)(2,1)} %copy-done.97), channel_id=1, source_target_pairs={{0,8},{8,0},{16,24},{24,16},{1,9},{9,1},{17,25},{25,17},{2,10},{10... | collective-permute-start | bytes 4718600 | tf_op jit(solution)/shard_map/ppermute | solution.py:413
  443.5 20.5 %collective-permute-start.37 = (bf16[2,256,768]{2,1,0:T(8,128)(2,1)}, bf16[2,256,768]{2,1,0:T(8,128)(2,1)S(1)}, u32[]{:S(2)}, u32[]{:S(2)}) collective-permute-start(bf16[2,256,768]{2,1,0:T(8,128)(2,1)} %copy-done.92), channel_id=1, source_target_pairs={{0,16},{16,0},{8,24},{24,8},{1,17},{17,1},{9,25},{25,9},{2,18},{18... | collective-permute-start | bytes 2359304 | tf_op jit(solution)/shard_map/ppermute | solution.py:421
  445.1 23.0 %collective-permute-start.31 = (bf16[256,768]{1,0:T(8,128)(2,1)}, bf16[256,768]{1,0:T(8,128)(2,1)S(1)}, u32[]{:S(2)}, u32[]{:S(2)}) collective-permute-start(bf16[256,768]{1,0:T(8,128)(2,1)} %get-tuple-element.177), channel_id=1, source_target_pairs={{0,1},{3,2},{1,3},{2,0},{4,5},{7,6},{5,7},{6,4},{8,9},{11,10},{9,1... | collective-permute-start | bytes 1179656 | tf_op jit(solution)/shard_map/ppermute | solution.py:429
  445.1 23.0 %collective-permute-start.38 = (bf16[256,768]{1,0:T(8,128)(2,1)S(1)}, bf16[256,768]{1,0:T(8,128)(2,1)S(1)}, u32[]{:S(2)}, u32[]{:S(2)}) collective-permute-start(bf16[256,768]{1,0:T(8,128)(2,1)S(1)} %get-tuple-element.180.kept), channel_id=1, source_target_pairs={{1,2},{2,1},{5,6},{6,5},{9,10},{10,9},{13,14},{14,13},{17,18},{18,... | collective-permute-start | bytes 1179656 | tf_op jit(solution)/shard_map/ppermute | solution.py:430
  445.8 26.3 %collective-permute-start.41 = (bf16[256,768]{1,0:T(8,128)(2,1)S(1)}, bf16[256,768]{1,0:T(8,128)(2,1)S(1)}, u32[]{:S(2)}, u32[]{:S(2)}) collective-permute-start(bf16[256,768]{1,0:T(8,128)(2,1)S(1)} %total.8.one.tq.refs_1_), channel_id=1, source_target_pairs={{0,16},{16,0},{8,24},{24,8},{1,17},{17,1},{9,25},{25,9},{2,18},{18... | collective-permute-start | bytes 1179656 | tf_op jit(solution)/shard_map/ppermute | solution.py:436
  472.7 20.0 %collective-permute-start.43 = (bf16[2,256,768]{2,1,0:T(8,128)(2,1)S(1)}, bf16[2,256,768]{2,1,0:T(8,128)(2,1)S(1)}, u32[]{:S(2)}, u32[]{:S(2)}) collective-permute-start(bf16[2,256,768]{2,1,0:T(8,128)(2,1)S(1)} %pair.12), channel_id=1, source_target_pairs={{0,8},{8,0},{16,24},{24,16},{1,9},{9,1},{17,25},{25,17},{2,10},{10... | collective-permute-start | bytes 2359304 | tf_op jit(solution)/shard_map/ppermute | solution.py:444
  472.7 20.4 %collective-permute-start.44 = (bf16[2,256,768]{2,1,0:T(8,128)(2,1)S(1)}, bf16[2,256,768]{2,1,0:T(8,128)(2,1)S(1)}, u32[]{:S(2)}, u32[]{:S(2)}) collective-permute-start(bf16[2,256,768]{2,1,0:T(8,128)(2,1)S(1)} %cross.11), channel_id=1, source_target_pairs={{0,16},{16,0},{8,24},{24,8},{1,17},{17,1},{9,25},{25,9},{2,18},{18... | collective-permute-start | bytes 2359304 | tf_op jit(solution)/shard_map/ppermute | solution.py:421
  475.7 14.6 %collective-permute-start.39 = (bf16[256,768]{1,0:T(8,128)(2,1)S(1)}, bf16[256,768]{1,0:T(8,128)(2,1)S(1)}, u32[]{:S(2)}, u32[]{:S(2)}) collective-permute-start(bf16[256,768]{1,0:T(8,128)(2,1)S(1)} %get-tuple-element.191), channel_id=1, source_target_pairs={{0,1},{3,2},{1,3},{2,0},{4,5},{7,6},{5,7},{6,4},{8,9},{11,10},{9,1... | collective-permute-start | bytes 1179656 | tf_op jit(solution)/shard_map/ppermute | solution.py:429
  475.8 18.9 %collective-permute-start.45 = (bf16[256,768]{1,0:T(8,128)(2,1)S(1)}, bf16[256,768]{1,0:T(8,128)(2,1)S(1)}, u32[]{:S(2)}, u32[]{:S(2)}) collective-permute-start(bf16[256,768]{1,0:T(8,128)(2,1)S(1)} %get-tuple-element.188.kept), channel_id=1, source_target_pairs={{1,2},{2,1},{5,6},{6,5},{9,10},{10,9},{13,14},{14,13},{17,18},{18,... | collective-permute-start | bytes 1179656 | tf_op jit(solution)/shard_map/ppermute | solution.py:430
  482.3 19.3 %collective-permute-start.46 = (bf16[256,768]{1,0:T(8,128)(2,1)S(1)}, bf16[256,768]{1,0:T(8,128)(2,1)S(1)}, u32[]{:S(2)}, u32[]{:S(2)}) collective-permute-start(bf16[256,768]{1,0:T(8,128)(2,1)S(1)} %total.9.tq.one.refs_1_), channel_id=1, source_target_pairs={{0,16},{16,0},{8,24},{24,8},{1,17},{17,1},{9,25},{25,9},{2,18},{18... | collective-permute-start | bytes 1179656 | tf_op jit(solution)/shard_map/ppermute | solution.py:436
  492.7 14.0 %collective-permute-start.49 = (bf16[256,512]{1,0:T(8,128)(2,1)S(1)}, bf16[256,512]{1,0:T(8,128)(2,1)S(1)}, u32[]{:S(2)}, u32[]{:S(2)}) collective-permute-start(bf16[256,512]{1,0:T(8,128)(2,1)S(1)} %choose.9.one.refs_5_), channel_id=1, source_target_pairs={{0,16},{16,0},{8,24},{24,8},{1,17},{17,1},{9,25},{25,9},{2,18},{18... | collective-permute-start | bytes 786440 | tf_op jit(solution)/shard_map/ppermute | solution.py:470
  493.2 28.5 %collective-permute-start.51 = (bf16[2,256,768]{2,1,0:T(8,128)(2,1)S(1)}, bf16[2,256,768]{2,1,0:T(8,128)(2,1)S(1)}, u32[]{:S(2)}, u32[]{:S(2)}) collective-permute-start(bf16[2,256,768]{2,1,0:T(8,128)(2,1)S(1)} %copy-done.87), channel_id=1, source_target_pairs={{0,8},{8,0},{16,24},{24,16},{1,9},{9,1},{17,25},{25,17},{2,10},{10... | collective-permute-start | bytes 2359304 | tf_op jit(solution)/shard_map/ppermute | solution.py:444
  507.3 14.4 %collective-permute-start.52 = (bf16[2,256,512]{2,1,0:T(8,128)(2,1)S(1)}, bf16[2,256,512]{2,1,0:T(8,128)(2,1)S(1)}, u32[]{:S(2)}, u32[]{:S(2)}) collective-permute-start(bf16[2,256,512]{2,1,0:T(8,128)(2,1)S(1)} %pair.14), channel_id=1, source_target_pairs={{0,8},{8,0},{16,24},{24,16},{1,9},{9,1},{17,25},{25,17},{2,10},{10... | collective-permute-start | bytes 1572872 | tf_op jit(solution)/shard_map/ppermute | solution.py:476
  508.3 23.1 %collective-permute-start.48 = (bf16[256,768]{1,0:T(8,128)(2,1)S(1)}, bf16[256,768]{1,0:T(8,128)(2,1)S(1)}, u32[]{:S(2)}, u32[]{:S(2)}) collective-permute-start(bf16[256,768]{1,0:T(8,128)(2,1)S(1)} %get-tuple-element.202), channel_id=1, source_target_pairs={{0,1},{3,2},{1,3},{2,0},{4,5},{7,6},{5,7},{6,4},{8,9},{11,10},{9,1... | collective-permute-start | bytes 1179656 | tf_op jit(solution)/shard_map/ppermute | solution.py:429
  508.3 23.1 %collective-permute-start.53 = (bf16[256,768]{1,0:T(8,128)(2,1)S(1)}, bf16[256,768]{1,0:T(8,128)(2,1)S(1)}, u32[]{:S(2)}, u32[]{:S(2)}) collective-permute-start(bf16[256,768]{1,0:T(8,128)(2,1)S(1)} %get-tuple-element.198.kept), channel_id=1, source_target_pairs={{1,2},{2,1},{5,6},{6,5},{9,10},{10,9},{13,14},{14,13},{17,18},{18,... | collective-permute-start | bytes 1179656 | tf_op jit(solution)/shard_map/ppermute | solution.py:430
  518.9 14.8 %collective-permute-start.54 = (bf16[256,768]{1,0:T(8,128)(2,1)S(1)}, bf16[256,768]{1,0:T(8,128)(2,1)S(1)}, u32[]{:S(2)}, u32[]{:S(2)}) collective-permute-start(bf16[256,768]{1,0:T(8,128)(2,1)S(1)} %total.10.one.refs_1_), channel_id=1, source_target_pairs={{0,16},{16,0},{8,24},{24,8},{1,17},{17,1},{9,25},{25,9},{2,18},{18... | collective-permute-start | bytes 1179656 | tf_op jit(solution)/shard_map/ppermute | solution.py:436
  544.8 17.7 %collective-permute-start.61 = (bf16[2,256,768]{2,1,0:T(8,128)(2,1)}, bf16[2,256,768]{2,1,0:T(8,128)(2,1)}, u32[]{:S(2)}, u32[]{:S(2)}) collective-permute-start(bf16[2,256,768]{2,1,0:T(8,128)(2,1)} %pair.16), channel_id=1, source_target_pairs={{0,8},{8,0},{16,24},{24,16},{1,9},{9,1},{17,25},{25,17},{2,10},{10... | collective-permute-start | bytes 2359304 | tf_op jit(solution)/shard_map/ppermute | solution.py:444
  (144 other events, 2209.0 us)
Sparse Core Ops, SparseCore 0:
  17.9 85.9 all-gather.4
  106.1 133.7 all-gather.6

commit v3 on v2

--- a/solution.py
+++ b/solution.py
@@ -11,7 +11,9 @@
 F32 = jnp.float32
 MIB = 1024 * 1024
 GAP = 2
+SMALL, MAIN, WIDE = 16 * MIB, 20 * MIB, 48 * MIB
 COST = pl.CostEstimate(flops=1, transcendentals=0, bytes_accessed=1)
+LONG = pl.CostEstimate(flops=5 * 10**13, transcendentals=0, bytes_accessed=1)
 SWAP = [(0, 1), (1, 0)]
 CORE = [(0, 1), (1, 0), (2, 3), (3, 2)]
 YPAIR = [(0, 2), (2, 0), (1, 3), (3, 1)]
@@ -63,7 +65,7 @@
     return pl.BlockSpec(shape, index)
 
 
-def step(body, name, place, operands, outs, *, in_specs=None, out_specs=None, grid=(1,)):
+def step(body, name, place, operands, outs, *, in_specs=None, out_specs=None, grid=(1,), cost=COST, vmem=SMALL):
     in_specs = in_specs or [None] * len(operands)
     in_specs = [spec(o.shape) if i is None else i for o, i in zip(operands, in_specs)]
     out_specs = out_specs or [spec(o) for o in outs]
@@ -73,8 +75,8 @@
             num_scalar_prefetch=1, grid=grid, in_specs=in_specs, out_specs=out_specs
         ),
         out_shape=[jax.ShapeDtypeStruct(o, BF) for o in outs],
-        cost_estimate=COST,
-        compiler_params=pltpu.CompilerParams(vmem_limit_bytes=16 * MIB),
+        cost_estimate=cost,
+        compiler_params=pltpu.CompilerParams(vmem_limit_bytes=vmem),
         name=name,
     )(place, *operands)
     return made if len(made) > 1 else made[0]
@@ -82,6 +84,23 @@
 
 def ends(place):
     return (place[1] == 0) | (place[1] == 3)
+
+
+def copy_kernel(place, one, two, to_a, to_b):
+    to_a[...] = one[0]
+    to_b[...] = two[0]
+
+
+def matrix_kernel(place, inv, pivots, out):
+    half = out.shape[-1]
+    for side in range(2):
+        first = jnp.bitwise_xor(place[0], side) * half
+        wanted = first + lax.broadcasted_iota(jnp.int32, (half, inv.shape[-1]), 0)
+        picks = (wanted == pivots[...].reshape(1, -1)).astype(F32).astype(BF)
+        product = lax.dot_general(
+            inv[...].reshape(inv.shape[-2:]), picks, (((1,), (1,)), ((), ())), preferred_element_type=F32
+        )
+        out[side, ...] = product.astype(BF).reshape(out.shape[1:])
 
 
 def lower_kernel(place, low, inv, out):
@@ -150,33 +169,33 @@
             out[...] = (anc[...] + top[...].astype(F32)).astype(BF)
 
 
-def panel_upper_kernel(place, m_own, m_other, own, other, out):
-    out[...] = (dot(m_own[...], own[...]) + dot(m_other[...], other[...])).astype(BF)
+def panel_upper_kernel(place, m, own, other, out):
+    out[...] = (dot(m[0], own[...]) + dot(m[1], other[...])).astype(BF)
 
 
 def upper_kernel(mo_ref, mt_ref, so_ref, st_ref, out_ref):
-    total = dot(mo_ref[0], so_ref[0, 0]) + dot(mt_ref[0], st_ref[0, 0])
+    total = dot(mo_ref[0, 0], so_ref[0, 0]) + dot(mt_ref[0, 0], st_ref[0, 0])
     out_ref[0, 0] = total.astype(BF)
 
 
 def make_upper(m_own, m_other, s_own, s_other):
     blocks, pair, half, cw = s_own.shape
-    w = m_own.shape[1]
-    m_spec = pl.BlockSpec((1, w, half), lambda k, b: (k, 0, 0))
+    w = m_own.shape[2]
+    m_specs = [pl.BlockSpec((1, 1, w, half), lambda k, b, side=side: (side, k, 0, 0)) for side in range(2)]
     s_spec = pl.BlockSpec((1, 1, half, cw), lambda k, b: (b, k, 0, 0))
     return pl.pallas_call(
         upper_kernel,
         grid=(pair, blocks),
-        in_specs=[m_spec, m_spec, s_spec, s_spec],
+        in_specs=[*m_specs, s_spec, s_spec],
         out_specs=pl.BlockSpec((1, 1, w, cw), lambda k, b: (b, k, 0, 0)),
         out_shape=jax.ShapeDtypeStruct((blocks, pair, w, cw), BF),
         cost_estimate=COST,
-        compiler_params=pltpu.CompilerParams(vmem_limit_bytes=16 * MIB),
+        compiler_params=pltpu.CompilerParams(vmem_limit_bytes=SMALL),
         name="upper",
     )(m_own, m_other, s_own, s_other)
 
 
-def product_kernel(place, tiles, low0, low1, up0, up1, keep, send, *, g, c, nt, rt, ct, tb, pair, tj):
+def product_kernel(place, tiles, low0, low1, up0, up1, keep, send, *, swapped, g, c, nt, rt, ct, tb, pair, tj):
     b, j = pl.program_id(0), pl.program_id(1)
     x, z, l = place[0], place[1], place[2]
     odd = lax.rem(z, 2)
@@ -187,11 +206,16 @@
         i = jnp.bitwise_xor(l, flip)
         rows = pl.ds(pl.multiple_of(i * tb, tb), tb)
         total = None
-        for t, (low, up) in enumerate(((low0, up0), (low1, up1))):
+        for t, low in enumerate((low0, low1)):
+            owner = jnp.bitwise_xor(z, t) if swapped else z - odd + t
             for k in range(pair):
-                leaf = (z - odd + t) * pair + k
-                flag = tiles[(leaf * nt + x * rt + g * 4 + i) * nt + column]
-                term = dot(low[0, k, rows, :] * flag.astype(F32).astype(BF), up[0, k])
+                flag = tiles[((owner * pair + k) * nt + x * rt + g * 4 + i) * nt + column]
+                left = low[0, k, rows, :] * flag.astype(F32).astype(BF)
+                if swapped:
+                    right = jnp.where(odd == t, up0[0, k], up1[0, k])
+                else:
+                    right = (up0, up1)[t][0, k]
+                term = dot(left, right)
                 total = term if total is None else total + term
         if p < 2:
             keep[p, 0] = total
@@ -205,10 +229,10 @@
     rows = 4 * tb
     up_spec = pl.BlockSpec((1, pair, w, tb), lambda b, j, *_: (b, 0, 0, j))
     out_spec = pl.BlockSpec((2, 1, tb, tb), lambda b, j, *_: (0, b, 0, j))
-    shared, at = lows
-    low_specs = [pl.BlockSpec((1, pair, rows, w), lambda b, j, *_, t=t: (t, 0, at, 0)) for t in range(2)]
+    one, two, at, swapped = lows
+    low_specs = [pl.BlockSpec((1, pair, rows, w), lambda b, j, *_, t=t: (t, 0, at, 0)) for t in (one[1], two[1])]
     return pl.pallas_call(
-        functools.partial(product_kernel, g=g, c=c, nt=nt, rt=rt, ct=ct, tb=tb, pair=pair, tj=tj),
+        functools.partial(product_kernel, swapped=swapped, g=g, c=c, nt=nt, rt=rt, ct=ct, tb=tb, pair=pair, tj=tj),
         grid_spec=pltpu.PrefetchScalarGridSpec(
             num_scalar_prefetch=2,
             grid=(blocks, tj),
@@ -224,9 +248,9 @@
             jax.ShapeDtypeStruct((2, blocks, tb, cw), BF),
         ],
         cost_estimate=COST,
-        compiler_params=pltpu.CompilerParams(vmem_limit_bytes=24 * MIB),
+        compiler_params=pltpu.CompilerParams(vmem_limit_bytes=MAIN),
         name="products",
-    )(place, tiles, shared, shared, up0, up1)
+    )(place, tiles, one[0], two[0], up0, up1)
 
 
 def final_kernel(place, tiles, *refs, g, c, nt, rt, ct, tb, tj, first, with_lower):
@@ -302,15 +326,9 @@
         out_shape=out_shape,
         input_output_aliases=aliases,
         cost_estimate=COST,
-        compiler_params=pltpu.CompilerParams(vmem_limit_bytes=24 * MIB),
+        compiler_params=pltpu.CompilerParams(vmem_limit_bytes=WIDE),
         name="final",
     )(place, tiles, *operands)
-
-
-def onehot_cols(inverse, pivots, first, count):
-    wanted = (first + jnp.arange(count, dtype=jnp.int32))
-    picks = (pivots[..., :, None] == wanted).astype(BF)
-    return jnp.einsum("...it,...tj->...ij", inverse, picks, preferred_element_type=F32).astype(BF)
 
 
 def after(value, *earlier):
@@ -337,7 +355,7 @@
     top_tiles = anc_tiles.reshape(-1)
     shape = dict(nt=nt, rt=rt, ct=ct, tb=tb)
     u = leaf_upper[0]
-    chunks = sorted(((g, c) for c in range(split) for g in range(groups)), key=lambda gc: (gc[0] + 1.5 * gc[1]))
+    chunks = sorted(((g, c) for c in range(split) for g in range(groups)), key=lambda gc: (gc[0] > 0, gc[1] * 1.5 + gc[0], gc[0]))
     parts = [(c, t) for c in range(split) for t in range(2)]
     v = {}
     last = [place]
@@ -351,14 +369,27 @@
 
     def slices(m):
         c, t = parts[m]
-        src = ordered(u)
-
-        def part(first):
-            return lax.dynamic_slice(src, (first, 0, c * cw), (pair, half, cw))
-
-        to_a = part(jnp.where(is_end, far, near) + t * pair)
-        to_b = part(jnp.where(is_end, near, far) + t * pair)
-        to_a, to_b = lax.optimization_barrier((to_a, to_b))
+
+        def near_pair(p):
+            return p[1] // 2 * 2
+
+        def far_pair(p):
+            return 2 - p[1] // 2 * 2
+
+        def one(k, p):
+            return (0, jnp.where(ends(p), far_pair(p), near_pair(p)) + t, k, 0, c)
+
+        def two(k, p):
+            return (0, jnp.where(ends(p), near_pair(p), far_pair(p)) + t, k, 0, c)
+
+        src = ordered(leaf_upper)
+        src = src.reshape((1, src.shape[1] // pair, pair) + src.shape[2:])
+        block = (1, 1, 1, half, cw)
+        to_a, to_b = step(
+            lambda place, i, j, o, q: copy_kernel(place, i.at[0, 0], j.at[0, 0], o.at[0], q.at[0]), "slices", place,
+            [src, src], [(pair, half, cw)] * 2, in_specs=[spec(block, one), spec(block, two)],
+            out_specs=[spec((1, half, cw), lambda k, p: (k, 0, 0))] * 2, grid=(pair,), vmem=WIDE,
+        )
         v["a", m] = lax.ppermute(to_a, "col", [(1, 0), (2, 3), (0, 2), (3, 1)])
         v["b", m] = (to_b, lax.ppermute(to_b, "col", [(1, 2), (2, 1)]))
         last[0] = to_b
@@ -379,7 +410,11 @@
         own = v["lower", first]
         got = lax.all_gather(own, "col", axis_index_groups=[[0, 1], [2, 3]], axis=0, tiled=False)
         for g in range(first, first + count):
-            v["low", g] = got, g - first
+            v["low", g] = (got, 0), (got, 1), g - first, False
+
+    def exchange(g):
+        own = v["lower", g][None]
+        v["low", g] = (own, 0), (lax.ppermute(own, "col", BUDDY), 0), 0, True
 
     def stack(m):
         kept, came = v["b", m]
@@ -388,17 +423,21 @@
         v["other", m] = lax.ppermute(own, "row", SWAP)
 
     def matrices():
+        pivots = leaf_pivots.reshape(leaf_pivots.shape[1], 1, w)
         for t in range(2):
-            first = near + t * pair
-            inverse = ordered(lax.dynamic_slice_in_dim(leaf_lower_inv[0], first, pair, 0))
-            pivots = lax.dynamic_slice_in_dim(leaf_pivots[0], first, pair, 0)
-            one = onehot_cols(inverse, pivots, x * half, half)
-            two = onehot_cols(inverse, pivots, (1 - x) * half, half)
-            done(("m", t), (one, two), two)
-        inverse = ordered(anc_lower_inv)
-        one = onehot_cols(inverse, anc_pivots, x * half, half)
-        two = onehot_cols(inverse, anc_pivots, (1 - x) * half, half)
-        done("anc_m", (one, two), two)
+            both = step(
+                matrix_kernel, "matrix", place, [ordered(leaf_lower_inv), pivots], [(2, pair, w, half)],
+                in_specs=[
+                    spec((1, 1, w, w), lambda k, p: (0, p[1] // 2 * 2 * pair + t * pair + k, 0, 0)),
+                    spec((1, 1, w), lambda k, p: (p[1] // 2 * 2 * pair + t * pair + k, 0, 0)),
+                ],
+                out_specs=[spec((2, 1, w, half), lambda k, p: (0, k, 0, 0))], grid=(pair,), vmem=WIDE,
+            )
+            done(("m", t), (both, both), both)
+        both = step(
+            matrix_kernel, "matrix", place, [ordered(anc_lower_inv), anc_pivots.reshape(1, w)], [(2, w, half)],
+        )
+        done("anc_m", both, both)
 
     def upper(m):
         own = ordered(v["own", m])
@@ -424,7 +463,7 @@
     def spread(n):
         to_a, to_b = step(
             spread_kernel, "spread", place, [ordered(v["keep", n]), v["core", n], v["y", n]], [(tb, cw)] * 2,
-            in_specs=[spec((1, 2, tb, cw))] * 2 + [None],
+            in_specs=[spec((1, 2, tb, cw))] * 2 + [None], cost=LONG if n else COST,
         )
         v["qa", n] = lax.ppermute(to_a, "col", [(0, 1), (3, 2), (1, 3), (2, 0)])
         v["qb", n] = (to_b, lax.ppermute(to_b, "col", [(1, 2), (2, 1)]))
@@ -448,7 +487,7 @@
         g, c = chunks[n]
         pq = step(
             panel_kernel, "panel", place, [ancestor, ordered(v["tq", n]), anc_upper_inv], [(tb, w)],
-            in_specs=[spec((tb, w), lambda i, p: (g * 4 + p[2], 0)), None, None],
+            in_specs=[spec((tb, w), lambda i, p: (g * 4 + p[2], 0)), None, None], vmem=WIDE,
         )
         v["p1", g] = (pq, lax.ppermute(pq, "col", [(0, 2)]))
         last[0] = pq
@@ -480,17 +519,16 @@
         g, c = chunks[n]
         rows_own = step(
             pivot_kernel, "pivot", place, [ancestor, ordered(v["tq", n]), v["ty", n], v["tc", n]], [(tb, cw)],
-            in_specs=[spec((tb, cw), lambda *_: (0, c)), None, None, None],
+            in_specs=[spec((tb, cw), lambda *_: (0, c)), None, None, None], vmem=WIDE,
         )
         v["pivot", c] = (rows_own, lax.ppermute(rows_own, "row", SWAP))
         last[0] = rows_own
 
     def pivot_two(n):
         g, c = chunks[n]
-        one, two = v["anc_m"]
         rows_own, rows_other = v["pivot", c]
         done(("anc_upper", c), step(
-            panel_upper_kernel, "anc_upper", place, [one, two, ordered(rows_own), rows_other], [(w, cw)]
+            panel_upper_kernel, "anc_upper", place, [v["anc_m"], ordered(rows_own), rows_other], [(w, cw)]
         ))
 
     out = {}
@@ -509,27 +547,25 @@
         last[0] = made[0]
 
     slices(0)
+    slices(1)
     lower(0, 1)
-    slices(1)
     share(0, 1)
     slices(2)
+    slices(3)
     lower(1, groups - 1)
-    slices(3)
+    matrices()
     stack(0)
-    matrices()
     stack(1)
-    last[0] = after(last[0], v["low", 0][0])
+    upper(0)
+    last[0] = after(last[0], v["low", 0][0][0])
     v["lower", 1] = after(v["lower", 1], last[0])
     share(1, groups - 1)
-    upper(0)
     stack(2)
     upper(1)
-    work = [(0, 3.5, stack, 3), (1, 1.5, upper, 2), (3, 1.5, upper, 3)]
+    work = [(0, 3.5, stack, 3), (1, 1.5, upper, 2), (2, 6.5, upper, 3)]
     for n, (g, c) in enumerate(chunks):
         slot = n + GAP * (n > 0)
-        steps = [
-            (0, 0, multiply), (1, 1, spread), (2, 2, total), (0, 3, cross), (3, 4, gather),
-        ]
+        steps = [(0, 0, multiply), (2, 2, total), (1, 2.9, spread), (0, 3, cross), (3, 4, gather)]
         if g == 0:
             steps += [(3, 6, pivot), (4, 5, pivot_two)]
         if c == 0:

time: 590 us -> 549 us (0.931)
  waiting for transfers between devices: 268 us -> 199 us
  Pallas kernels: 156 us -> 198 us
  local copies, waits for them, and re-layouts: 64.2 us -> 33.3 us
  starting transfers between devices: 66.8 us -> 91.8 us
  matrix products: 7.27 us -> 0 us
    ppermute x6, waiting for transfers between devices: 69.5 us -> 15.3 us  [cross(): v['y', n] = lax.ppermute(crossing, 'layer', YPAIR)]
    ppermute x4, waiting for transfers between devices: 57.8 us -> 4.9 us  [stack(): v['other', m] = lax.ppermute(own, 'row', SWAP)]
    pallas_call x46 -> x53, Pallas kernels: 53.8 us -> 88.9 us  [step(): pl.pallas_call(body, grid_spec=pltpu.PrefetchScalarGridSpec(num_scalar_pr...]
    ppermute x4, waiting for transfers between devices: 69.1 us -> 92.9 us  [slices(): v['a', m] = lax.ppermute(to_a, 'col', [(1, 0), (2, 3), (0, 2), (3, 1)])]
    ppermute x6, waiting for transfers between devices: 9.38 us -> 30.8 us  [total(): v['ty', n] = lax.ppermute(tq, 'layer', YPAIR)]
    unnamed x256 -> x190, local copies, waits for them, and re-layouts: 51.4 us -> 33.1 us
    ppermute x4, starting transfers between devices: 11 us -> 25.5 us  [slices(): v['a', m] = lax.ppermute(to_a, 'col', [(1, 0), (2, 3), (0, 2), (3, 1)])]
    all_gather x2, waiting for transfers between devices: 13.3 us -> 0.02 us  [share(): lax.all_gather(own, 'col', axis_index_groups=[[0, 1], [2, 3]], axis=0, ti...]
  transfers between devices with their start and end apart: 64 -> 64, of which waited for: 25 -> 21; matrix products, arithmetic and copies ran while one was open for 3% -> 0% of each run, Pallas kernels for 16% -> 33%
where the time goes in v3:
time: 549 us; the launch traced here: 539 us
  waiting for transfers between devices  199 us (36%)
  Pallas kernels  198 us (36%)
  starting transfers between devices  91.8 us (17%)
  local copies, waits for them, and re-layouts  33.3 us (6%)
  between operations  16 us (3%)
    ppermute x4, waiting for transfers between devices, slices(): v['a', m] = lax.ppermute(to_a, 'col', [(1, 0), (2, 3), (0, 2), (3, 1)])  92.9 us
    pallas_call x53, Pallas kernels, step(): pl.pallas_call(body, grid_spec=pltpu.PrefetchScalarGridSpec(num_scalar_pr...  88.9 us
    pallas_call x6, Pallas kernels, products(): pl.pallas_call(functools.partial(product_kernel, swapped=swapped, g=g, c=...  58.9 us
    pallas_call x6, Pallas kernels, final(): pl.pallas_call(functools.partial(final_kernel, g=g, c=c, nt=nt, rt=rt, ct...  37.3 us
    unnamed x190, local copies, waits for them, and re-layouts  33.1 us
    ppermute x6, waiting for transfers between devices, total(): v['ty', n] = lax.ppermute(tq, 'layer', YPAIR)  30.8 us
    ppermute x4, starting transfers between devices, slices(): v['a', m] = lax.ppermute(to_a, 'col', [(1, 0), (2, 3), (0, 2), (3, 1)])  25.5 us
    ppermute x3, waiting for transfers between devices, panel(): v['p1', g] = (pq, lax.ppermute(pq, 'col', [(0, 2)]))  16.5 us
  transfers between devices with their start and end apart: 64, of which 21 were waited for; matrix products, arithmetic and copies ran while one was open for 0% of the time, Pallas kernels for 33%

profile of v3, /device:TPU:0, one launch (start us, length us, event | category | flops | bytes accessed | tf_op | source)
XLA Modules:
  0.0 539.4 jit_solution(9823173388114463407)
XLA Ops:
  12.8 4.9 lower.2
  17.8 4.1 collective-permute-start
  31.1 5.5 %lower.3 = bf16[2,2048,512]{2,1,0:T(8,128)(2,1)S(1)} custom-call(s32[3]{0:T(128)S(1)} %pad_add_fusion.place, bf16[1,2,3072,512]{3,2,1,0:T(8,128)(2,1)S(1)} %bitcast.29, bf16[1,2,512,512]{3,2,1,0:T(8,128)(2,1)S(1)} %copy-done.34), custom_call_target="tpu_custom_call" | custom-call | flops 1 | bytes 1 | tf_op jit(solution)/shard_map/lower/pallas_call | solution.py:72
  45.1 3.9 collective-permute-done.first
  52.3 10.4 %collective-permute-start.2 = (bf16[2,256,768]{2,1,0:T(8,128)(2,1)S(1)}, bf16[2,256,768]{2,1,0:T(8,128)(2,1)S(1)}, u32[]{:S(2)}, u32[]{:S(2)}) collective-permute-start(bf16[2,256,768]{2,1,0:T(8,128)(2,1)S(1)} %copy-done.84), channel_id=1, source_target_pairs={{1,0},{2,3},{0,2},{3,1},{5,4},{6,7},{4,6},{7,5},{9,8},{10,11},{8,1... | collective-permute-start | bytes 2359304 | tf_op jit(solution)/shard_map/ppermute | solution.py:393
  63.5 33.6 %collective-permute-done.2.first = bf16[2,256,768]{2,1,0:T(8,128)(2,1)S(1)} collective-permute-done((bf16[2,256,768]{2,1,0:T(8,128)(2,1)S(1)}, bf16[2,256,768]{2,1,0:T(8,128)(2,1)S(1)}, u32[]{:S(2)}, u32[]{:S(2)}) %collective-permute-start.2) | collective-permute-done | bytes 786464 | tf_op jit(solution)/shard_map/ppermute | solution.py:393
  102.4 2.9 collective-permute-start.5
  107.0 22.5 %collective-permute-done.5.first = bf16[2,256,768]{2,1,0:T(8,128)(2,1)} collective-permute-done((bf16[2,256,768]{2,1,0:T(8,128)(2,1)}, bf16[2,256,768]{2,1,0:T(8,128)(2,1)}, u32[]{:S(2)}, u32[]{:S(2)}) %collective-permute-start.5) | collective-permute-done | bytes 786464 | tf_op jit(solution)/shard_map/ppermute | solution.py:393
  132.7 4.9 collective-permute-done.7.st_ref
  137.6 3.8 upper.5.up1
  141.5 9.2 %products.6 = (f32[2,2,256,768]{3,2,1,0:T(8,128)S(1)}, bf16[2,2,256,768]{3,2,1,0:T(8,128)(2,1)S(1)}) custom-call(s32[3]{0:T(128)S(1)} %pad_add_fusion.place, s32[4608]{0:T(1024)S(1)} %reshape.31.tiles, bf16[2,2,1024,512]{3,2,1,0:T(8,128)(2,1)S(1)} %bitcast.22, bf16[2,2,1024,512]{3,2,1,0:T(8,128)(2,1)S(1)} %bitcast.23, ...), custom_call_target="tpu_custom_call" | custom-call | flops 1 | bytes 1 | tf_op jit(solution)/shard_map/products/pallas_call | solution.py:234
  150.8 8.0 %collective-permute-start.8 = (bf16[2,256,768]{2,1,0:T(8,128)(2,1)S(1)}, bf16[2,256,768]{2,1,0:T(8,128)(2,1)S(1)}, u32[]{:S(2)}, u32[]{:S(2)}) collective-permute-start(bf16[2,256,768]{2,1,0:T(8,128)(2,1)S(1)} %copy-done.81), channel_id=1, source_target_pairs={{1,0},{2,3},{0,2},{3,1},{5,4},{6,7},{4,6},{7,5},{9,8},{10,11},{8,1... | collective-permute-start | bytes 2359304 | tf_op jit(solution)/shard_map/ppermute | solution.py:393
  161.1 32.9 %collective-permute-done.8.first = bf16[2,256,768]{2,1,0:T(8,128)(2,1)S(1)} collective-permute-done((bf16[2,256,768]{2,1,0:T(8,128)(2,1)S(1)}, bf16[2,256,768]{2,1,0:T(8,128)(2,1)S(1)}, u32[]{:S(2)}, u32[]{:S(2)}) %collective-permute-start.8) | collective-permute-done | bytes 786464 | tf_op jit(solution)/shard_map/ppermute | solution.py:393
  200.2 15.3 %collective-permute-done.12.came = bf16[2,256,768]{2,1,0:T(8,128)(2,1)S(1)} collective-permute-done((bf16[2,256,768]{2,1,0:T(8,128)(2,1)S(1)}, bf16[2,256,768]{2,1,0:T(8,128)(2,1)S(1)}, u32[]{:S(2)}, u32[]{:S(2)}) %collective-permute-start.12) | collective-permute-done | bytes 786464 | tf_op jit(solution)/shard_map/ppermute | solution.py:460
  216.3 3.1 collective-permute-start.13
  220.1 16.5 %collective-permute-done.13.arrived = bf16[256,768]{1,0:T(8,128)(2,1)S(1)} collective-permute-done((bf16[256,768]{1,0:T(8,128)(2,1)S(1)}, bf16[256,768]{1,0:T(8,128)(2,1)S(1)}, u32[]{:S(2)}, u32[]{:S(2)}) %collective-permute-start.13) | collective-permute-done | bytes 393248 | tf_op jit(solution)/shard_map/ppermute | solution.py:468
  240.9 4.1 upper.7.up1
  245.0 9.2 %products.7 = (f32[2,2,256,768]{3,2,1,0:T(8,128)S(1)}, bf16[2,2,256,768]{3,2,1,0:T(8,128)(2,1)S(1)}) custom-call(s32[3]{0:T(128)S(1)} %pad_add_fusion.place, s32[4608]{0:T(1024)S(1)} %copy-done.66, bf16[2,2,1024,512]{3,2,1,0:T(8,128)(2,1)S(1)} %bitcast.24, bf16[2,2,1024,512]{3,2,1,0:T(8,128)(2,1)S(1)} %bitcast.25, bf16[2,2,512,768]{3,2,1,0:T(8,128)(2,1)S(1)} %upper.6.up0, ...), custom_call_target="tpu_custom_call" | custom-call | flops 1 | bytes 1 | tf_op jit(solution)/shard_map/products/pallas_call | solution.py:234
  260.4 5.4 %collective-permute-done.17.two.ty.refs_2_ = bf16[256,768]{1,0:T(8,128)(2,1)S(1)} collective-permute-done((bf16[256,768]{1,0:T(8,128)(2,1)S(1)}, bf16[256,768]{1,0:T(8,128)(2,1)S(1)}, u32[]{:S(2)}, u32[]{:S(2)}) %collective-permute-start.17) | collective-permute-done | bytes 393248 | tf_op jit(solution)/shard_map/ppermute | solution.py:475
  268.1 4.6 collective-permute-start.18
  272.7 5.9 %collective-permute-done.18.came = bf16[256,512]{1,0:T(8,128)(2,1)S(1)} collective-permute-done((bf16[256,512]{1,0:T(8,128)(2,1)S(1)}, bf16[256,512]{1,0:T(8,128)(2,1)S(1)}, u32[]{:S(2)}, u32[]{:S(2)}) %collective-permute-start.18) | collective-permute-done | bytes 262176 | tf_op jit(solution)/shard_map/ppermute | solution.py:492
  283.4 3.4 copy-done
  289.4 10.1 %products.8 = (f32[2,2,256,768]{3,2,1,0:T(8,128)S(1)}, bf16[2,2,256,768]{3,2,1,0:T(8,128)(2,1)}) custom-call(s32[3]{0:T(128)S(1)} %pad_add_fusion.place, s32[4608]{0:T(1024)S(1)} %copy-done.67, bf16[2,2,2048,512]{3,2,1,0:T(8,128)(2,1)S(1)} %bitcast.12, bf16[2,2,2048,512]{3,2,1,0:T(8,128)(2,1)S(1)} %bitcast.13, bf16[2,2,512,768]{3,2,1,0:T(8,128)(2,1)S(1)} %upper.4.up0, ...), custom_call_target="tpu_custom_call" | custom-call | flops 1 | bytes 1 | tf_op jit(solution)/shard_map/products/pallas_call | solution.py:234
  307.5 7.1 %collective-permute-start.22 = (bf16[256,512]{1,0:T(8,128)(2,1)S(1)}, bf16[256,512]{1,0:T(8,128)(2,1)S(1)}, u32[]{:S(2)}, u32[]{:S(2)}) collective-permute-start(bf16[256,512]{1,0:T(8,128)(2,1)S(1)} %copy-done.64), channel_id=1, source_target_pairs={{0,1},{2,3},{4,5},{6,7},{8,9},{10,11},{12,13},{14,15},{16,17},{18,... | collective-permute-start | bytes 786440 | tf_op jit(solution)/shard_map/ppermute | solution.py:503
  314.6 6.2 %collective-permute-done.22.came = bf16[256,512]{1,0:T(8,128)(2,1)S(1)} collective-permute-done((bf16[256,512]{1,0:T(8,128)(2,1)S(1)}, bf16[256,512]{1,0:T(8,128)(2,1)S(1)}, u32[]{:S(2)}, u32[]{:S(2)}) %collective-permute-start.22) | collective-permute-done | bytes 262176 | tf_op jit(solution)/shard_map/ppermute | solution.py:503
  324.8 10.1 %products.9 = (f32[2,2,256,768]{3,2,1,0:T(8,128)S(1)}, bf16[2,2,256,768]{3,2,1,0:T(8,128)(2,1)}) custom-call(s32[3]{0:T(128)S(1)} %pad_add_fusion.place, s32[4608]{0:T(1024)S(1)} %copy-done.68, bf16[2,2,2048,512]{3,2,1,0:T(8,128)(2,1)S(1)} %bitcast.14, bf16[2,2,2048,512]{3,2,1,0:T(8,128)(2,1)S(1)} %bitcast.15, bf16[2,2,512,768]{3,2,1,0:T(8,128)(2,1)S(1)} %upper.4.up0, ...), custom_call_target="tpu_custom_call" | custom-call | flops 1 | bytes 1 | tf_op jit(solution)/shard_map/products/pallas_call | solution.py:234
  336.7 2.7 spread.8
  353.8 6.2 %final.6 = (f32[3072,1536]{1,0:T(8,128)}, bf16[3072,512]{1,0:T(8,128)(2,1)}) custom-call(s32[3]{0:T(128)S(1)} %pad_add_fusion.place, s32[576]{0:T(1024)S(1)} %reshape.30.tiles, f32[3072,1536]{1,0:T(8,128)} %refs_0_.11, bf16[256,768]{1,0:T(8,128)(2,1)S(1)} %total.6.tq.one.refs_1_, bf16[256,768]{1,0:T(8,128)(2,1)S(1)} %copy-done.36, ...), custom_call_target="tpu_custom_call" | custom-call | flops 1 | bytes 1 | tf_op jit(solution)/shard_map/final/pallas_call | solution.py:319
  360.7 3.4 copy-done.1
  364.0 10.1 %products.10 = (f32[2,2,256,768]{3,2,1,0:T(8,128)S(1)}, bf16[2,2,256,768]{3,2,1,0:T(8,128)(2,1)}) custom-call(s32[3]{0:T(128)S(1)} %pad_add_fusion.place, s32[4608]{0:T(1024)S(1)} %copy-done.69, bf16[2,2,2048,512]{3,2,1,0:T(8,128)(2,1)S(1)} %bitcast.16, bf16[2,2,2048,512]{3,2,1,0:T(8,128)(2,1)S(1)} %bitcast.17, bf16[2,2,512,768]{3,2,1,0:T(8,128)(2,1)S(1)} %copy-done.4, ...), custom_call_target="tpu_custom_call" | custom-call | flops 1 | bytes 1 | tf_op jit(solution)/shard_map/products/pallas_call | solution.py:234
  379.0 3.0 spread.9
  394.9 10.1 %products.11 = (f32[2,2,256,768]{3,2,1,0:T(8,128)S(1)}, bf16[2,2,256,768]{3,2,1,0:T(8,128)(2,1)}) custom-call(s32[3]{0:T(128)S(1)} %pad_add_fusion.place, s32[4608]{0:T(1024)S(1)} %copy-done.70, bf16[2,2,2048,512]{3,2,1,0:T(8,128)(2,1)S(1)} %bitcast.20, bf16[2,2,2048,512]{3,2,1,0:T(8,128)(2,1)S(1)} %bitcast.21, bf16[2,2,512,768]{3,2,1,0:T(8,128)(2,1)S(1)} %copy-done.5, ...), custom_call_target="tpu_custom_call" | custom-call | flops 1 | bytes 1 | tf_op jit(solution)/shard_map/products/pallas_call | solution.py:234
  406.7 2.6 total.9.tq.one.refs_1_
  418.8 2.7 collective-permute-start.39
  422.2 22.3 %collective-permute-done.41.two.refs_2_ = bf16[256,768]{1,0:T(8,128)(2,1)S(1)} collective-permute-done((bf16[256,768]{1,0:T(8,128)(2,1)S(1)}, bf16[256,768]{1,0:T(8,128)(2,1)S(1)}, u32[]{:S(2)}, u32[]{:S(2)}) %collective-permute-start.41) | collective-permute-done | bytes 393248 | tf_op jit(solution)/shard_map/ppermute | solution.py:475
  444.5 4.0 collective-permute-start.42
  449.1 4.8 collective-permute-done.42.came
  456.7 6.7 %final.7.refs_8_ = f32[3072,1536]{1,0:T(8,128)} custom-call(s32[3]{0:T(128)S(1)} %pad_add_fusion.place, s32[576]{0:T(1024)S(1)} %copy-done.77, f32[3072,1536]{1,0:T(8,128)} %refs_0_.11, bf16[256,768]{1,0:T(8,128)(2,1)} %total.7.one.tq.refs_1_, bf16[256,768]{1,0:T(8,128)(2,1)} %collective-permute-done.35.two.ty.refs_2_, ...), custom_call_target="tpu_custom_call", output_to_operand_aliasing={{}: (10, {})} | custom-call | flops 1 | bytes 1 | tf_op jit(solution)/shard_map/final/pallas_call | solution.py:319
  466.1 4.9 collective-permute-start.47
  475.4 5.9 %collective-permute-done.47.came = bf16[256,512]{1,0:T(8,128)(2,1)S(1)} collective-permute-done((bf16[256,512]{1,0:T(8,128)(2,1)S(1)}, bf16[256,512]{1,0:T(8,128)(2,1)S(1)}, u32[]{:S(2)}, u32[]{:S(2)}) %collective-permute-start.47) | collective-permute-done | bytes 262176 | tf_op jit(solution)/shard_map/ppermute | solution.py:492
  483.2 3.7 collective-permute-done.49.came
  490.7 3.2 collective-permute-done.53.two.refs_6_
  496.9 6.6 %final.8 = (f32[3072,1536]{1,0:T(8,128)}, bf16[3072,512]{1,0:T(8,128)(2,1)}) custom-call(s32[3]{0:T(128)S(1)} %pad_add_fusion.place, s32[576]{0:T(1024)S(1)} %copy-done.78, f32[3072,1536]{1,0:T(8,128)} %refs_0_.11, bf16[256,768]{1,0:T(8,128)(2,1)S(1)} %copy-done.25, bf16[256,768]{1,0:T(8,128)(2,1)S(1)} %copy-done.54, ...), custom_call_target="tpu_custom_call", output_to_operand_aliasing={{0}: (10, {}), {1}: (11, {})} | custom-call | flops 1 | bytes 1 | tf_op jit(solution)/shard_map/final/pallas_call | solution.py:319
  503.5 3.1 collective-permute-done.56.two.refs_2_
  507.2 4.5 collective-permute-done.57.two.refs_6_
  514.3 6.1 %final.9 = (f32[3072,1536]{1,0:T(8,128)}, bf16[3072,512]{1,0:T(8,128)(2,1)}) custom-call(s32[3]{0:T(128)S(1)} %pad_add_fusion.place, s32[576]{0:T(1024)S(1)} %copy-done.78, f32[3072,1536]{1,0:T(8,128)} %refs_0_.11, bf16[256,768]{1,0:T(8,128)(2,1)} %total.9.tq.one.refs_1_, ...), custom_call_target="tpu_custom_call", output_to_operand_aliasing={{0}: (10, {}), {1}: (11, {})} | custom-call | flops 1 | bytes 1 | tf_op jit(solution)/shard_map/final/pallas_call | solution.py:319
  520.4 5.7 %final.10.refs_8_ = f32[3072,1536]{1,0:T(8,128)} custom-call(s32[3]{0:T(128)S(1)} %pad_add_fusion.place, s32[576]{0:T(1024)S(1)} %copy-done.78, f32[3072,1536]{1,0:T(8,128)} %refs_0_.11, bf16[256,768]{1,0:T(8,128)(2,1)S(1)} %total.10.one.refs_1_, bf16[256,768]{1,0:T(8,128)(2,1)S(1)} %collective-permute-done.51.two.refs_2_, ...), custom_call_target="tpu_custom_call", output_to_operand_aliasing={{}: (10, {})} | custom-call | flops 1 | bytes 1 | tf_op jit(solution)/shard_map/final/pallas_call | solution.py:319
  526.1 5.9 %final.11 = f32[3072,1536]{1,0:T(8,128)} custom-call(s32[3]{0:T(128)S(1)} %pad_add_fusion.place, s32[576]{0:T(1024)S(1)} %copy-done.78, f32[3072,1536]{1,0:T(8,128)} %refs_0_.11, bf16[256,768]{1,0:T(8,128)(2,1)S(1)} %total.11.one.refs_1_, bf16[256,768]{1,0:T(8,128)(2,1)S(1)} %collective-permute-done.56.two.refs_2_, ...), custom_call_target="tpu_custom_call", output_to_operand_aliasing={{}: (10, {})} | custom-call | flops 1 | bytes 1 | tf_op jit(solution)/shard_map/final/pallas_call | solution.py:319
  (349 shorter events, 147.5 us)
Async XLA Ops:
  7.2 94.2 %all-gather.5.cloned.1.call-start = ((), (), s32[]{:S(2)}) async-start(), calls=%async_computation | async-start | bytes 6291456 | tf_op jit(solution)/shard_map/all_gather | solution.py:411
  17.7 265.7 %all-gather.7.cloned.1.call-start = ((), (), s32[]{:S(2)}) async-start(), calls=%async_computation.1 | async-start | bytes 12582912 | tf_op jit(solution)/shard_map/all_gather | solution.py:411
  17.8 31.2 %collective-permute-start = (bf16[2,256,768]{2,1,0:T(8,128)(2,1)}, bf16[2,256,768]{2,1,0:T(8,128)(2,1)}, u32[]{:S(2)}, u32[]{:S(2)}) collective-permute-start(bf16[2,256,768]{2,1,0:T(8,128)(2,1)} %copy-done.85), channel_id=1, source_target_pairs={{1,0},{2,3},{0,2},{3,1},{5,4},{6,7},{4,6},{7,5},{9,8},{10,11},{8,1... | collective-permute-start | bytes 2359304 | tf_op jit(solution)/shard_map/ppermute | solution.py:393
  21.9 27.1 %collective-permute-start.1 = (bf16[2,256,768]{2,1,0:T(8,128)(2,1)S(1)}, bf16[2,256,768]{2,1,0:T(8,128)(2,1)}, u32[]{:S(2)}, u32[]{:S(2)}) collective-permute-start(bf16[2,256,768]{2,1,0:T(8,128)(2,1)S(1)} %get-tuple-element.113.kept), channel_id=1, source_target_pairs={{1,2},{2,1},{5,6},{6,5},{9,10},{10,9},{13,14},{14,13},{17,18},{18,... | collective-permute-start | bytes 2359304 | tf_op jit(solution)/shard_map/ppermute | solution.py:394
  51.0 47.9 %collective-permute-start.4 = (bf16[2,2,256,768]{3,2,1,0:T(8,128)(2,1)S(1)}, bf16[2,2,256,768]{3,2,1,0:T(8,128)(2,1)S(1)}, u32[]{:S(2)}, u32[]{:S(2)}) collective-permute-start(bf16[2,2,256,768]{3,2,1,0:T(8,128)(2,1)S(1)} %stack.20.so_ref), channel_id=1, source_target_pairs={{0,4},{4,0},{1,5},{5,1},{2,6},{6,2},{3,7},{7,3},{8,12},{12,8},{9,1... | collective-permute-start | bytes 4718600 | tf_op jit(solution)/shard_map/ppermute | solution.py:423
  52.3 44.8 %collective-permute-start.2 = (bf16[2,256,768]{2,1,0:T(8,128)(2,1)S(1)}, bf16[2,256,768]{2,1,0:T(8,128)(2,1)S(1)}, u32[]{:S(2)}, u32[]{:S(2)}) collective-permute-start(bf16[2,256,768]{2,1,0:T(8,128)(2,1)S(1)} %copy-done.84), channel_id=1, source_target_pairs={{1,0},{2,3},{0,2},{3,1},{5,4},{6,7},{4,6},{7,5},{9,8},{10,11},{8,1... | collective-permute-start | bytes 2359304 | tf_op jit(solution)/shard_map/ppermute | solution.py:393
  62.8 34.3 %collective-permute-start.3 = (bf16[2,256,768]{2,1,0:T(8,128)(2,1)S(1)}, bf16[2,256,768]{2,1,0:T(8,128)(2,1)S(1)}, u32[]{:S(2)}, u32[]{:S(2)}) collective-permute-start(bf16[2,256,768]{2,1,0:T(8,128)(2,1)S(1)} %get-tuple-element.115.kept), channel_id=1, source_target_pairs={{1,2},{2,1},{5,6},{6,5},{9,10},{10,9},{13,14},{14,13},{17,18},{18,... | collective-permute-start | bytes 2359304 | tf_op jit(solution)/shard_map/ppermute | solution.py:394
  101.3 36.3 %collective-permute-start.7 = (bf16[2,2,256,768]{3,2,1,0:T(8,128)(2,1)}, bf16[2,2,256,768]{3,2,1,0:T(8,128)(2,1)}, u32[]{:S(2)}, u32[]{:S(2)}) collective-permute-start(bf16[2,2,256,768]{3,2,1,0:T(8,128)(2,1)} %copy-done.26), channel_id=1, source_target_pairs={{0,4},{4,0},{1,5},{5,1},{2,6},{6,2},{3,7},{7,3},{8,12},{12,8},{9,1... | collective-permute-start | bytes 4718600 | tf_op jit(solution)/shard_map/ppermute | solution.py:423
  102.4 27.1 %collective-permute-start.5 = (bf16[2,256,768]{2,1,0:T(8,128)(2,1)}, bf16[2,256,768]{2,1,0:T(8,128)(2,1)}, u32[]{:S(2)}, u32[]{:S(2)}) collective-permute-start(bf16[2,256,768]{2,1,0:T(8,128)(2,1)} %copy-done.82), channel_id=1, source_target_pairs={{1,0},{2,3},{0,2},{3,1},{5,4},{6,7},{4,6},{7,5},{9,8},{10,11},{8,1... | collective-permute-start | bytes 2359304 | tf_op jit(solution)/shard_map/ppermute | solution.py:393
  105.3 24.2 %collective-permute-start.6 = (bf16[2,256,768]{2,1,0:T(8,128)(2,1)}, bf16[2,256,768]{2,1,0:T(8,128)(2,1)}, u32[]{:S(2)}, u32[]{:S(2)}) collective-permute-start(bf16[2,256,768]{2,1,0:T(8,128)(2,1)} %copy-done.73), channel_id=1, source_target_pairs={{1,2},{2,1},{5,6},{6,5},{9,10},{10,9},{13,14},{14,13},{17,18},{18,... | collective-permute-start | bytes 2359304 | tf_op jit(solution)/shard_map/ppermute | solution.py:394
  150.8 43.2 %collective-permute-start.8 = (bf16[2,256,768]{2,1,0:T(8,128)(2,1)S(1)}, bf16[2,256,768]{2,1,0:T(8,128)(2,1)S(1)}, u32[]{:S(2)}, u32[]{:S(2)}) collective-permute-start(bf16[2,256,768]{2,1,0:T(8,128)(2,1)S(1)} %copy-done.81), channel_id=1, source_target_pairs={{1,0},{2,3},{0,2},{3,1},{5,4},{6,7},{4,6},{7,5},{9,8},{10,11},{8,1... | collective-permute-start | bytes 2359304 | tf_op jit(solution)/shard_map/ppermute | solution.py:393
  158.8 35.2 %collective-permute-start.10 = (bf16[2,256,768]{2,1,0:T(8,128)(2,1)S(1)}, bf16[2,256,768]{2,1,0:T(8,128)(2,1)S(1)}, u32[]{:S(2)}, u32[]{:S(2)}) collective-permute-start(bf16[2,256,768]{2,1,0:T(8,128)(2,1)S(1)} %copy-done.72), channel_id=1, source_target_pairs={{1,2},{2,1},{5,6},{6,5},{9,10},{10,9},{13,14},{14,13},{17,18},{18,... | collective-permute-start | bytes 2359304 | tf_op jit(solution)/shard_map/ppermute | solution.py:394
  159.5 38.4 %collective-permute-start.11 = (bf16[2,2,256,768]{3,2,1,0:T(8,128)(2,1)S(1)}, bf16[2,2,256,768]{3,2,1,0:T(8,128)(2,1)S(1)}, u32[]{:S(2)}, u32[]{:S(2)}) collective-permute-start(bf16[2,2,256,768]{3,2,1,0:T(8,128)(2,1)S(1)} %stack.22.so_ref), channel_id=1, source_target_pairs={{0,4},{4,0},{1,5},{5,1},{2,6},{6,2},{3,7},{7,3},{8,12},{12,8},{9,1... | collective-permute-start | bytes 4718600 | tf_op jit(solution)/shard_map/ppermute | solution.py:423
  195.8 45.1 %collective-permute-start.15 = (bf16[2,2,256,768]{3,2,1,0:T(8,128)(2,1)}, bf16[2,2,256,768]{3,2,1,0:T(8,128)(2,1)}, u32[]{:S(2)}, u32[]{:S(2)}) collective-permute-start(bf16[2,2,256,768]{3,2,1,0:T(8,128)(2,1)} %stack.23.so_ref), channel_id=1, source_target_pairs={{0,4},{4,0},{1,5},{5,1},{2,6},{6,2},{3,7},{7,3},{8,12},{12,8},{9,1... | collective-permute-start | bytes 4718600 | tf_op jit(solution)/shard_map/ppermute | solution.py:423
  196.4 19.1 %collective-permute-start.12 = (bf16[2,256,768]{2,1,0:T(8,128)(2,1)S(1)}, bf16[2,256,768]{2,1,0:T(8,128)(2,1)S(1)}, u32[]{:S(2)}, u32[]{:S(2)}) collective-permute-start(bf16[2,256,768]{2,1,0:T(8,128)(2,1)S(1)} %cross.6), channel_id=1, source_target_pairs={{0,16},{16,0},{8,24},{24,8},{1,17},{17,1},{9,25},{25,9},{2,18},{18... | collective-permute-start | bytes 2359304 | tf_op jit(solution)/shard_map/ppermute | solution.py:460
  216.3 20.3 %collective-permute-start.13 = (bf16[256,768]{1,0:T(8,128)(2,1)S(1)}, bf16[256,768]{1,0:T(8,128)(2,1)S(1)}, u32[]{:S(2)}, u32[]{:S(2)}) collective-permute-start(bf16[256,768]{1,0:T(8,128)(2,1)S(1)} %get-tuple-element.142), channel_id=1, source_target_pairs={{0,1},{3,2},{1,3},{2,0},{4,5},{7,6},{5,7},{6,4},{8,9},{11,10},{9,1... | collective-permute-start | bytes 1179656 | tf_op jit(solution)/shard_map/ppermute | solution.py:468
  219.4 17.2 %collective-permute-start.14 = (bf16[256,768]{1,0:T(8,128)(2,1)S(1)}, bf16[256,768]{1,0:T(8,128)(2,1)S(1)}, u32[]{:S(2)}, u32[]{:S(2)}) collective-permute-start(bf16[256,768]{1,0:T(8,128)(2,1)S(1)} %get-tuple-element.143.kept), channel_id=1, source_target_pairs={{1,2},{2,1},{5,6},{6,5},{9,10},{10,9},{13,14},{14,13},{17,18},{18,... | collective-permute-start | bytes 1179656 | tf_op jit(solution)/shard_map/ppermute | solution.py:469
  266.4 13.4 %collective-permute-start.19 = (bf16[2,256,768]{2,1,0:T(8,128)(2,1)S(1)}, bf16[2,256,768]{2,1,0:T(8,128)(2,1)S(1)}, u32[]{:S(2)}, u32[]{:S(2)}) collective-permute-start(bf16[2,256,768]{2,1,0:T(8,128)(2,1)S(1)} %pair.9), channel_id=1, source_target_pairs={{0,8},{8,0},{16,24},{24,16},{1,9},{9,1},{17,25},{25,17},{2,10},{10... | collective-permute-start | bytes 2359304 | tf_op jit(solution)/shard_map/ppermute | solution.py:483
  266.5 33.0 %collective-permute-start.20 = (bf16[2,256,768]{2,1,0:T(8,128)(2,1)}, bf16[2,256,768]{2,1,0:T(8,128)(2,1)}, u32[]{:S(2)}, u32[]{:S(2)}) collective-permute-start(bf16[2,256,768]{2,1,0:T(8,128)(2,1)} %cross.7), channel_id=1, source_target_pairs={{0,16},{16,0},{8,24},{24,8},{1,17},{17,1},{9,25},{25,9},{2,18},{18... | collective-permute-start | bytes 2359304 | tf_op jit(solution)/shard_map/ppermute | solution.py:460
  305.0 31.7 %collective-permute-start.26 = (bf16[2,256,768]{2,1,0:T(8,128)(2,1)S(1)}, bf16[2,256,768]{2,1,0:T(8,128)(2,1)S(1)}, u32[]{:S(2)}, u32[]{:S(2)}) collective-permute-start(bf16[2,256,768]{2,1,0:T(8,128)(2,1)S(1)} %cross.8), channel_id=1, source_target_pairs={{0,16},{16,0},{8,24},{24,8},{1,17},{17,1},{9,25},{25,9},{2,18},{18... | collective-permute-start | bytes 2359304 | tf_op jit(solution)/shard_map/ppermute | solution.py:460
  305.6 18.0 %collective-permute-start.23 = (bf16[256,768]{1,0:T(8,128)(2,1)S(1)}, bf16[256,768]{1,0:T(8,128)(2,1)S(1)}, u32[]{:S(2)}, u32[]{:S(2)}) collective-permute-start(bf16[256,768]{1,0:T(8,128)(2,1)S(1)} %copy-done.58), channel_id=1, source_target_pairs={{0,4},{4,0},{1,5},{5,1},{2,6},{6,2},{3,7},{7,3},{8,12},{12,8},{9,1... | collective-permute-start | bytes 1179656 | tf_op jit(solution)/shard_map/ppermute | solution.py:524
  306.8 28.1 %collective-permute-start.24 = (bf16[256,768]{1,0:T(8,128)(2,1)S(1)}, bf16[256,768]{1,0:T(8,128)(2,1)S(1)}, u32[]{:S(2)}, u32[]{:S(2)}) collective-permute-start(bf16[256,768]{1,0:T(8,128)(2,1)S(1)} %get-tuple-element.163), channel_id=1, source_target_pairs={{0,1},{3,2},{1,3},{2,0},{4,5},{7,6},{5,7},{6,4},{8,9},{11,10},{9,1... | collective-permute-start | bytes 1179656 | tf_op jit(solution)/shard_map/ppermute | solution.py:468
  306.8 28.1 %collective-permute-start.25 = (bf16[256,768]{1,0:T(8,128)(2,1)S(1)}, bf16[256,768]{1,0:T(8,128)(2,1)S(1)}, u32[]{:S(2)}, u32[]{:S(2)}) collective-permute-start(bf16[256,768]{1,0:T(8,128)(2,1)S(1)} %get-tuple-element.157.kept), channel_id=1, source_target_pairs={{1,2},{2,1},{5,6},{6,5},{9,10},{10,9},{13,14},{14,13},{17,18},{18,... | collective-permute-start | bytes 1179656 | tf_op jit(solution)/shard_map/ppermute | solution.py:469
  307.5 13.3 %collective-permute-start.22 = (bf16[256,512]{1,0:T(8,128)(2,1)S(1)}, bf16[256,512]{1,0:T(8,128)(2,1)S(1)}, u32[]{:S(2)}, u32[]{:S(2)}) collective-permute-start(bf16[256,512]{1,0:T(8,128)(2,1)S(1)} %copy-done.64), channel_id=1, source_target_pairs={{0,1},{2,3},{4,5},{6,7},{8,9},{10,11},{12,13},{14,15},{16,17},{18,... | collective-permute-start | bytes 786440 | tf_op jit(solution)/shard_map/ppermute | solution.py:503
  322.1 20.4 %collective-permute-start.29 = (bf16[256,512]{1,0:T(8,128)(2,1)}, bf16[256,512]{1,0:T(8,128)(2,1)}, u32[]{:S(2)}, u32[]{:S(2)}) collective-permute-start(bf16[256,512]{1,0:T(8,128)(2,1)} %choose.7.one.refs_5_), channel_id=1, source_target_pairs={{0,16},{16,0},{8,24},{24,8},{1,17},{17,1},{9,25},{25,9},{2,18},{18... | collective-permute-start | bytes 786440 | tf_op jit(solution)/shard_map/ppermute | solution.py:509
  342.0 37.0 %collective-permute-start.32 = (bf16[2,256,768]{2,1,0:T(8,128)(2,1)}, bf16[2,256,768]{2,1,0:T(8,128)(2,1)}, u32[]{:S(2)}, u32[]{:S(2)}) collective-permute-start(bf16[2,256,768]{2,1,0:T(8,128)(2,1)} %cross.9), channel_id=1, source_target_pairs={{0,16},{16,0},{8,24},{24,8},{1,17},{17,1},{9,25},{25,9},{2,18},{18... | collective-permute-start | bytes 2359304 | tf_op jit(solution)/shard_map/ppermute | solution.py:460
  344.2 30.0 %collective-permute-start.27 = (bf16[256,768]{1,0:T(8,128)(2,1)}, bf16[256,768]{1,0:T(8,128)(2,1)}, u32[]{:S(2)}, u32[]{:S(2)}) collective-permute-start(bf16[256,768]{1,0:T(8,128)(2,1)} %get-tuple-element.167), channel_id=1, source_target_pairs={{0,1},{3,2},{1,3},{2,0},{4,5},{7,6},{5,7},{6,4},{8,9},{11,10},{9,1... | collective-permute-start | bytes 1179656 | tf_op jit(solution)/shard_map/ppermute | solution.py:468
  346.7 27.4 %collective-permute-start.31 = (bf16[256,768]{1,0:T(8,128)(2,1)}, bf16[256,768]{1,0:T(8,128)(2,1)}, u32[]{:S(2)}, u32[]{:S(2)}) collective-permute-start(bf16[256,768]{1,0:T(8,128)(2,1)} %get-tuple-element.168.kept), channel_id=1, source_target_pairs={{1,2},{2,1},{5,6},{6,5},{9,10},{10,9},{13,14},{14,13},{17,18},{18,... | collective-permute-start | bytes 1179656 | tf_op jit(solution)/shard_map/ppermute | solution.py:469
  348.3 36.2 %collective-permute-start.35 = (bf16[256,768]{1,0:T(8,128)(2,1)}, bf16[256,768]{1,0:T(8,128)(2,1)}, u32[]{:S(2)}, u32[]{:S(2)}) collective-permute-start(bf16[256,768]{1,0:T(8,128)(2,1)} %total.7.one.tq.refs_1_), channel_id=1, source_target_pairs={{0,16},{16,0},{8,24},{24,8},{1,17},{17,1},{9,25},{25,9},{2,18},{18... | collective-permute-start | bytes 1179656 | tf_op jit(solution)/shard_map/ppermute | solution.py:475
  386.6 25.1 %collective-permute-start.38 = (bf16[2,256,768]{2,1,0:T(8,128)(2,1)}, bf16[2,256,768]{2,1,0:T(8,128)(2,1)}, u32[]{:S(2)}, u32[]{:S(2)}) collective-permute-start(bf16[2,256,768]{2,1,0:T(8,128)(2,1)} %cross.10), channel_id=1, source_target_pairs={{0,16},{16,0},{8,24},{24,8},{1,17},{17,1},{9,25},{25,9},{2,18},{18... | collective-permute-start | bytes 2359304 | tf_op jit(solution)/shard_map/ppermute | solution.py:460
  387.7 19.1 %collective-permute-start.33 = (bf16[256,768]{1,0:T(8,128)(2,1)}, bf16[256,768]{1,0:T(8,128)(2,1)}, u32[]{:S(2)}, u32[]{:S(2)}) collective-permute-start(bf16[256,768]{1,0:T(8,128)(2,1)} %get-tuple-element.178), channel_id=1, source_target_pairs={{0,1},{3,2},{1,3},{2,0},{4,5},{7,6},{5,7},{6,4},{8,9},{11,10},{9,1... | collective-permute-start | bytes 1179656 | tf_op jit(solution)/shard_map/ppermute | solution.py:468
  389.1 17.7 %collective-permute-start.37 = (bf16[256,768]{1,0:T(8,128)(2,1)}, bf16[256,768]{1,0:T(8,128)(2,1)}, u32[]{:S(2)}, u32[]{:S(2)}) collective-permute-start(bf16[256,768]{1,0:T(8,128)(2,1)} %get-tuple-element.180.kept), channel_id=1, source_target_pairs={{1,2},{2,1},{5,6},{6,5},{9,10},{10,9},{13,14},{14,13},{17,18},{18,... | collective-permute-start | bytes 1179656 | tf_op jit(solution)/shard_map/ppermute | solution.py:469
  416.0 48.1 %collective-permute-start.45 = (bf16[2,256,768]{2,1,0:T(8,128)(2,1)S(1)}, bf16[2,256,768]{2,1,0:T(8,128)(2,1)S(1)}, u32[]{:S(2)}, u32[]{:S(2)}) collective-permute-start(bf16[2,256,768]{2,1,0:T(8,128)(2,1)S(1)} %cross.11), channel_id=1, source_target_pairs={{0,16},{16,0},{8,24},{24,8},{1,17},{17,1},{9,25},{25,9},{2,18},{18... | collective-permute-start | bytes 2359304 | tf_op jit(solution)/shard_map/ppermute | solution.py:460
  417.0 27.5 %collective-permute-start.41 = (bf16[256,768]{1,0:T(8,128)(2,1)S(1)}, bf16[256,768]{1,0:T(8,128)(2,1)S(1)}, u32[]{:S(2)}, u32[]{:S(2)}) collective-permute-start(bf16[256,768]{1,0:T(8,128)(2,1)S(1)} %copy-done.24), channel_id=1, source_target_pairs={{0,16},{16,0},{8,24},{24,8},{1,17},{17,1},{9,25},{25,9},{2,18},{18... | collective-permute-start | bytes 1179656 | tf_op jit(solution)/shard_map/ppermute | solution.py:475
  418.1 37.4 %collective-permute-start.43 = (bf16[256,768]{1,0:T(8,128)(2,1)S(1)}, bf16[256,768]{1,0:T(8,128)(2,1)S(1)}, u32[]{:S(2)}, u32[]{:S(2)}) collective-permute-start(bf16[256,768]{1,0:T(8,128)(2,1)S(1)} %pivot.3.own), channel_id=1, source_target_pairs={{0,4},{4,0},{1,5},{5,1},{2,6},{6,2},{3,7},{7,3},{8,12},{12,8},{9,1... | collective-permute-start | bytes 1179656 | tf_op jit(solution)/shard_map/ppermute | solution.py:524
  418.8 44.6 %collective-permute-start.39 = (bf16[256,768]{1,0:T(8,128)(2,1)S(1)}, bf16[256,768]{1,0:T(8,128)(2,1)S(1)}, u32[]{:S(2)}, u32[]{:S(2)}) collective-permute-start(bf16[256,768]{1,0:T(8,128)(2,1)S(1)} %get-tuple-element.190), channel_id=1, source_target_pairs={{0,1},{3,2},{1,3},{2,0},{4,5},{7,6},{5,7},{6,4},{8,9},{11,10},{9,1... | collective-permute-start | bytes 1179656 | tf_op jit(solution)/shard_map/ppermute | solution.py:468
  421.5 42.0 %collective-permute-start.44 = (bf16[256,768]{1,0:T(8,128)(2,1)S(1)}, bf16[256,768]{1,0:T(8,128)(2,1)S(1)}, u32[]{:S(2)}, u32[]{:S(2)}) collective-permute-start(bf16[256,768]{1,0:T(8,128)(2,1)S(1)} %get-tuple-element.191.kept), channel_id=1, source_target_pairs={{1,2},{2,1},{5,6},{6,5},{9,10},{10,9},{13,14},{14,13},{17,18},{18,... | collective-permute-start | bytes 1179656 | tf_op jit(solution)/shard_map/ppermute | solution.py:469
  453.9 19.0 %collective-permute-start.46 = (bf16[256,768]{1,0:T(8,128)(2,1)}, bf16[256,768]{1,0:T(8,128)(2,1)}, u32[]{:S(2)}, u32[]{:S(2)}) collective-permute-start(bf16[256,768]{1,0:T(8,128)(2,1)} %total.9.tq.one.refs_1_), channel_id=1, source_target_pairs={{0,16},{16,0},{8,24},{24,8},{1,17},{17,1},{9,25},{25,9},{2,18},{18... | collective-permute-start | bytes 1179656 | tf_op jit(solution)/shard_map/ppermute | solution.py:475
  466.0 22.2 %collective-permute-start.48 = (bf16[256,768]{1,0:T(8,128)(2,1)S(1)}, bf16[256,768]{1,0:T(8,128)(2,1)S(1)}, u32[]{:S(2)}, u32[]{:S(2)}) collective-permute-start(bf16[256,768]{1,0:T(8,128)(2,1)S(1)} %get-tuple-element.202), channel_id=1, source_target_pairs={{0,1},{3,2},{1,3},{2,0},{4,5},{7,6},{5,7},{6,4},{8,9},{11,10},{9,1... | collective-permute-start | bytes 1179656 | tf_op jit(solution)/shard_map/ppermute | solution.py:468
  466.1 15.2 %collective-permute-start.47 = (bf16[256,512]{1,0:T(8,128)(2,1)S(1)}, bf16[256,512]{1,0:T(8,128)(2,1)S(1)}, u32[]{:S(2)}, u32[]{:S(2)}) collective-permute-start(bf16[256,512]{1,0:T(8,128)(2,1)S(1)} %panel.5.own), channel_id=1, source_target_pairs={{0,2},{4,6},{8,10},{12,14},{16,18},{20,22},{24,26},{28,30}} | collective-permute-start | bytes 786440 | tf_op jit(solution)/shard_map/ppermute | solution.py:492
  471.0 15.9 %collective-permute-start.49 = (bf16[256,512]{1,0:T(8,128)(2,1)S(1)}, bf16[256,512]{1,0:T(8,128)(2,1)S(1)}, u32[]{:S(2)}, u32[]{:S(2)}) collective-permute-start(bf16[256,512]{1,0:T(8,128)(2,1)S(1)} %choose.8.own), channel_id=1, source_target_pairs={{0,1},{2,3},{4,5},{6,7},{8,9},{10,11},{12,13},{14,15},{16,17},{18,... | collective-permute-start | bytes 786440 | tf_op jit(solution)/shard_map/ppermute | solution.py:503
  472.3 15.9 %collective-permute-start.50 = (bf16[256,768]{1,0:T(8,128)(2,1)S(1)}, bf16[256,768]{1,0:T(8,128)(2,1)S(1)}, u32[]{:S(2)}, u32[]{:S(2)}) collective-permute-start(bf16[256,768]{1,0:T(8,128)(2,1)S(1)} %get-tuple-element.199.kept), channel_id=1, source_target_pairs={{1,2},{2,1},{5,6},{6,5},{9,10},{10,9},{13,14},{14,13},{17,18},{18,... | collective-permute-start | bytes 1179656 | tf_op jit(solution)/shard_map/ppermute | solution.py:469
  473.0 15.9 %collective-permute-start.51 = (bf16[256,768]{1,0:T(8,128)(2,1)S(1)}, bf16[256,768]{1,0:T(8,128)(2,1)S(1)}, u32[]{:S(2)}, u32[]{:S(2)}) collective-permute-start(bf16[256,768]{1,0:T(8,128)(2,1)S(1)} %total.10.one.refs_1_), channel_id=1, source_target_pairs={{0,16},{16,0},{8,24},{24,8},{1,17},{17,1},{9,25},{25,9},{2,18},{18... | collective-permute-start | bytes 1179656 | tf_op jit(solution)/shard_map/ppermute | solution.py:475
  494.6 12.0 %collective-permute-start.56 = (bf16[256,768]{1,0:T(8,128)(2,1)S(1)}, bf16[256,768]{1,0:T(8,128)(2,1)S(1)}, u32[]{:S(2)}, u32[]{:S(2)}) collective-permute-start(bf16[256,768]{1,0:T(8,128)(2,1)S(1)} %total.11.one.refs_1_), channel_id=1, source_target_pairs={{0,16},{16,0},{8,24},{24,8},{1,17},{17,1},{9,25},{25,9},{2,18},{18... | collective-permute-start | bytes 1179656 | tf_op jit(solution)/shard_map/ppermute | solution.py:475
  495.3 18.4 %collective-permute-start.58 = (bf16[2,256,768]{2,1,0:T(8,128)(2,1)S(1)}, bf16[2,256,768]{2,1,0:T(8,128)(2,1)S(1)}, u32[]{:S(2)}, u32[]{:S(2)}) collective-permute-start(bf16[2,256,768]{2,1,0:T(8,128)(2,1)S(1)} %pair.13), channel_id=1, source_target_pairs={{0,8},{8,0},{16,24},{24,16},{1,9},{9,1},{17,25},{25,17},{2,10},{10... | collective-permute-start | bytes 2359304 | tf_op jit(solution)/shard_map/ppermute | solution.py:483
  495.5 16.3 %collective-permute-start.57 = (bf16[256,512]{1,0:T(8,128)(2,1)S(1)}, bf16[256,512]{1,0:T(8,128)(2,1)S(1)}, u32[]{:S(2)}, u32[]{:S(2)}) collective-permute-start(bf16[256,512]{1,0:T(8,128)(2,1)S(1)} %choose.11.one.refs_5_), channel_id=1, source_target_pairs={{0,16},{16,0},{8,24},{24,8},{1,17},{17,1},{9,25},{25,9},{2,18},{18... | collective-permute-start | bytes 786440 | tf_op jit(solution)/shard_map/ppermute | solution.py:509
  496.8 23.6 %collective-permute-start.60 = (bf16[2,256,768]{2,1,0:T(8,128)(2,1)S(1)}, bf16[2,256,768]{2,1,0:T(8,128)(2,1)S(1)}, u32[]{:S(2)}, u32[]{:S(2)}) collective-permute-start(bf16[2,256,768]{2,1,0:T(8,128)(2,1)S(1)} %pair.14), channel_id=1, source_target_pairs={{0,8},{8,0},{16,24},{24,16},{1,9},{9,1},{17,25},{25,17},{2,10},{10... | collective-permute-start | bytes 2359304 | tf_op jit(solution)/shard_map/ppermute | solution.py:483
  507.2 19.0 %collective-permute-start.61 = (bf16[2,256,768]{2,1,0:T(8,128)(2,1)S(1)}, bf16[2,256,768]{2,1,0:T(8,128)(2,1)S(1)}, u32[]{:S(2)}, u32[]{:S(2)}) collective-permute-start(bf16[2,256,768]{2,1,0:T(8,128)(2,1)S(1)} %pair.16), channel_id=1, source_target_pairs={{0,8},{8,0},{16,24},{24,16},{1,9},{9,1},{17,25},{25,17},{2,10},{10... | collective-permute-start | bytes 2359304 | tf_op jit(solution)/shard_map/ppermute | solution.py:483
  (111 other events, 1201.3 us)
Sparse Core Ops, SparseCore 0:
  17.8 82.9 all-gather.4
  102.9 135.1 all-gather.6
